TPU v7x, 32 devices: a whole 2x2x4 slice. The times are simulated.
32 devices in a mesh: ctx: 16 (over z, y, x), dp: 2 (over core).
Axes of the slice: x: 2, y: 2, z: 4, core: 2. Of those that a mesh axis runs over, the one named last changes fastest.
Arguments:
- normed_input: bfloat16 [2, 2048, 4096], P('dp', 'ctx'), may hold values from -6 to 6
- projection_output_gradient: bfloat16 [2, 2048, 4096], P('dp', 'ctx'), may hold values from -1 to 1
- query: bfloat16 [2, 2048, 2048], P('dp', 'ctx'), may hold values from -5 to 5
- key: bfloat16 [2, 2048, 2048], P('dp', 'ctx'), may hold values from -5 to 5
- value: bfloat16 [2, 2048, 2048], P('dp', 'ctx'), may hold values from -5 to 5
- frozen_output_gradient: bfloat16 [2, 2048, 2048], P('dp', 'ctx'), may hold values from -1 to 1
- query_down_weight: bfloat16 [4096, 8], replicated, may hold values from -0.09375 to 0.09375
- query_up_weight: bfloat16 [8, 2048], replicated, may hold values from -2 to 2
- key_down_weight: bfloat16 [4096, 8], replicated, may hold values from -0.09375 to 0.09375
- key_up_weight: bfloat16 [8, 2048], replicated, may hold values from -2 to 2
- value_down_weight: bfloat16 [4096, 8], replicated, may hold values from -0.09375 to 0.09375
- value_up_weight: bfloat16 [8, 2048], replicated, may hold values from -2 to 2
- output_down_weight: bfloat16 [2048, 8], replicated, may hold values from -2 to 2
- output_up_weight: bfloat16 [8, 4096], replicated, may hold values from -2 to 2
Outputs:
- grad_a_query: float32 [4096, 8], replicated
- grad_b_query: float32 [8, 2048], replicated
- grad_a_key: float32 [4096, 8], replicated
- grad_b_key: float32 [8, 2048], replicated
- grad_a_value: float32 [4096, 8], replicated
- grad_b_value: float32 [8, 2048], replicated
- grad_a_out: float32 [2048, 8], replicated
- grad_b_out: float32 [8, 4096], replicated
All inputs are finite; a program needn't handle non-finite values.
Results may differ from a plain program's by a relative error of at most 0.012.
Values may be sent and summed in bfloat16 or wider, within the bound.
No kernel may reach another device: no remote copies, remote signals or barrier semaphores. Data moves between devices by JAX's collectives and lax.ppermute only.
A program may use at most 128 MiB of HBM per device.

v0:
```python
import jax
import jax.numpy as jnp
from jax import lax
from jax.sharding import PartitionSpec as P

SHIFT_HEADS = 16
HEAD_WIDTH = 128
ADAPTER_RANK = 8
GROUP = 2048


masked_score = -1e30


def passed_along(value, axis, steps):
    count = lax.axis_size(axis)
    pairs = [(source, (source + steps) % count) for source in range(count)]
    return lax.ppermute(value, axis, pairs)


def head_terms(queries, grads, keys, values, key_low, value_low, key_up, value_up, allowed):
    scale = HEAD_WIDTH ** (-0.5)
    scores = jnp.dot(queries, keys.T, preferred_element_type=jnp.float32) * scale
    scores = jnp.where(allowed > 0, scores, masked_score)
    summit = jnp.max(scores, axis=-1, keepdims=True)
    weights = jnp.exp(scores - summit)
    weights = weights / jnp.sum(weights, axis=-1, keepdims=True)
    rounded = weights.astype(jnp.bfloat16)
    output = jnp.dot(rounded, values, preferred_element_type=jnp.float32)
    delta = jnp.sum(grads.astype(jnp.float32) * output, axis=-1, keepdims=True)
    dweights = jnp.dot(grads, values.T, preferred_element_type=jnp.float32)
    dscores = (scale * weights * (dweights - delta)).astype(jnp.bfloat16)
    query_gradient = jnp.dot(dscores, keys, preferred_element_type=jnp.float32).astype(jnp.bfloat16)
    query_proj = jnp.dot(queries, key_up.T, preferred_element_type=jnp.float32).astype(jnp.bfloat16)
    grad_proj = jnp.dot(grads, value_up.T, preferred_element_type=jnp.float32).astype(jnp.bfloat16)
    key_terms = jnp.dot(dscores.T, query_proj, preferred_element_type=jnp.float32)
    value_terms = jnp.dot(rounded.T, grad_proj, preferred_element_type=jnp.float32)
    key_mix = jnp.dot(dscores, key_low, preferred_element_type=jnp.float32).astype(jnp.bfloat16)
    value_mix = jnp.dot(rounded, value_low, preferred_element_type=jnp.float32).astype(jnp.bfloat16)
    key_up_grad = jnp.dot(key_mix.T, queries, preferred_element_type=jnp.float32)
    value_up_grad = jnp.dot(value_mix.T, grads, preferred_element_type=jnp.float32)
    return (
        query_gradient,
        output.astype(jnp.bfloat16),
        key_up_grad,
        value_up_grad,
        key_terms,
        value_terms,
    )


def heads_last(stacked):
    return jnp.transpose(stacked, (1, 0, 2)).reshape(
        stacked.shape[1], stacked.shape[0] * stacked.shape[2]
    )


def attend_half(
    query_cols, grad_cols, key_blocks, value_blocks, key_low, value_low, key_up, value_up, allowed
):
    count = key_blocks.shape[0] * key_blocks.shape[1]
    key_flat = key_blocks.reshape(count, key_blocks.shape[2])
    value_flat = value_blocks.reshape(count, value_blocks.shape[2])
    low_keys = key_low.reshape(count, key_low.shape[2])
    low_values = value_low.reshape(count, value_low.shape[2])
    heads_here = query_cols.shape[1] // HEAD_WIDTH

    def per_head(head):
        start = head * HEAD_WIDTH

        def column(array):
            return lax.dynamic_slice_in_dim(array, start, HEAD_WIDTH, 1)

        return head_terms(
            column(query_cols),
            column(grad_cols),
            column(key_flat),
            column(value_flat),
            low_keys,
            low_values,
            column(key_up),
            column(value_up),
            allowed,
        )

    query_gradient, output, key_up_grad, value_up_grad, key_terms, value_terms = lax.map(
        per_head, jnp.arange(heads_here, dtype=jnp.int32)
    )
    return (
        heads_last(query_gradient),
        heads_last(output),
        heads_last(key_up_grad),
        heads_last(value_up_grad),
        jnp.sum(key_terms, axis=0),
        jnp.sum(value_terms, axis=0),
    )


def block_mask(distance, place, tok_rows):
    rows = jnp.arange(tok_rows)[:, None]
    columns = jnp.arange(tok_rows)[None, :]
    causal = columns <= rows
    usable = (distance >= 0) & (distance <= place)
    earlier = distance > 0
    allowed = usable[None, :, None] & (earlier[None, :, None] | causal[:, None, :])
    return allowed.reshape(tok_rows, distance.shape[0] * tok_rows).astype(jnp.int32)


def per_device(
    normed_input,
    projection_output_gradient,
    query,
    key,
    value,
    frozen_output_gradient,
    query_down_weight,
    query_up_weight,
    key_down_weight,
    key_up_weight,
    value_down_weight,
    value_up_weight,
    output_down_weight,
    output_up_weight,
):
    token_count = normed_input[0]
    incoming_gradient = projection_output_gradient[0]
    queries = query[0]
    keys = key[0]
    values = value[0]
    base = frozen_output_gradient[0]
    tok_rows = token_count.shape[0]
    group_devs = GROUP // tok_rows
    half_columns = SHIFT_HEADS // 2 * HEAD_WIDTH
    my_index = lax.axis_index("ctx")
    place_plain = my_index % group_devs
    place_moved = (my_index + group_devs // 2) % group_devs
    reduced_query = jnp.dot(
        token_count, query_down_weight, preferred_element_type=jnp.float32
    ).astype(jnp.bfloat16)
    reduced_key = jnp.dot(token_count, key_down_weight, preferred_element_type=jnp.float32).astype(
        jnp.bfloat16
    )
    reduced_value = jnp.dot(
        token_count, value_down_weight, preferred_element_type=jnp.float32
    ).astype(jnp.bfloat16)
    reduced_output = jnp.dot(
        incoming_gradient, output_up_weight.T, preferred_element_type=jnp.float32
    ).astype(jnp.bfloat16)
    grads = (
        base.astype(jnp.float32)
        + jnp.dot(reduced_output, output_down_weight.T, preferred_element_type=jnp.float32)
    ).astype(jnp.bfloat16)
    plain_query = queries[:, :half_columns]
    moved_query = queries[:, half_columns:]
    plain_grads = grads[:, :half_columns]
    moved_grads = grads[:, half_columns:]
    plain_keys = keys[:, :half_columns]
    moved_keys = keys[:, half_columns:]
    plain_values = values[:, :half_columns]
    moved_values = values[:, half_columns:]
    unshifted_key_rows = key_up_weight[:, :half_columns]
    shifted_key_rows = key_up_weight[:, half_columns:]
    unshifted_value_rows = value_up_weight[:, :half_columns]
    shifted_value_rows = value_up_weight[:, half_columns:]
    distances = jnp.arange(group_devs, dtype=jnp.int32)
    received = [(plain_keys, plain_values, moved_keys, moved_values, reduced_key, reduced_value)]
    for distance in range(1, group_devs):
        received.append(
            passed_along(
                (plain_keys, plain_values, moved_keys, moved_values, reduced_key, reduced_value),
                "ctx",
                distance,
            )
        )
    stacked = [jnp.stack([entry[member] for entry in received]) for member in range(6)]
    plain = attend_half(
        plain_query,
        plain_grads,
        stacked[0],
        stacked[1],
        stacked[4],
        stacked[5],
        unshifted_key_rows,
        unshifted_value_rows,
        block_mask(distances, place_plain, tok_rows),
    )
    moved = attend_half(
        moved_query,
        moved_grads,
        stacked[2],
        stacked[3],
        stacked[4],
        stacked[5],
        shifted_key_rows,
        shifted_value_rows,
        block_mask(distances, place_moved, tok_rows),
    )
    owed = jnp.concatenate([plain[4] + moved[4], plain[5] + moved[5]], axis=1)
    owed = owed.reshape(group_devs, tok_rows, 2 * ADAPTER_RANK)
    owner_terms = owed[0]
    for distance in range(1, group_devs):
        owner_terms = owner_terms + passed_along(owed[distance], "ctx", -distance)
    moved_dquery = moved[0]
    moved_output = moved[1]
    query_gradient = jnp.concatenate([plain[0], moved_dquery], axis=1)
    attention_probs = jnp.concatenate([plain[1], moved_output], axis=1)
    key_terms = owner_terms[:, :ADAPTER_RANK].astype(jnp.bfloat16)
    value_terms = owner_terms[:, ADAPTER_RANK:].astype(jnp.bfloat16)
    reduced_query_gradient = jnp.dot(
        query_gradient, query_up_weight.T, preferred_element_type=jnp.float32
    ).astype(jnp.bfloat16)
    output_reduced = jnp.dot(
        attention_probs, output_down_weight, preferred_element_type=jnp.float32
    ).astype(jnp.bfloat16)
    part_a_query = jnp.dot(
        token_count.T, reduced_query_gradient, preferred_element_type=jnp.float32
    )
    part_b_query = jnp.dot(reduced_query.T, query_gradient, preferred_element_type=jnp.float32)
    part_a_key = jnp.dot(token_count.T, key_terms, preferred_element_type=jnp.float32)
    part_b_key = jnp.concatenate([plain[2], moved[2]], axis=1)
    part_a_value = jnp.dot(token_count.T, value_terms, preferred_element_type=jnp.float32)
    part_b_value = jnp.concatenate([plain[3], moved[3]], axis=1)
    part_a_out = jnp.dot(attention_probs.T, reduced_output, preferred_element_type=jnp.float32)
    part_b_out = jnp.dot(output_reduced.T, incoming_gradient, preferred_element_type=jnp.float32)
    totals = lax.psum(
        (
            part_a_query,
            part_b_query,
            part_a_key,
            part_b_key,
            part_a_value,
            part_b_value,
            part_a_out,
            part_b_out,
        ),
        ("ctx", "dp"),
    )
    return (totals[0], totals[1], totals[2], totals[3], totals[4], totals[5], totals[6], totals[7])


def solution(mesh):
    placed = (
        P("dp", "ctx", None),
        P("dp", "ctx", None),
        P("dp", "ctx", None),
        P("dp", "ctx", None),
        P("dp", "ctx", None),
        P("dp", "ctx", None),
        P(),
        P(),
        P(),
        P(),
        P(),
        P(),
        P(),
        P(),
    )
    return jax.shard_map(
        per_device,
        mesh=mesh,
        in_specs=placed,
        out_specs=(P(), P(), P(), P(), P(), P(), P(), P()),
        check_vma=False,
    )
```

profile of v0, /device:TPU:0, one launch (start us, length us, event | category | flops | bytes accessed | tf_op | source)
XLA Modules:
  0.0 931.0 jit_solution(10857089335979722576)
XLA Ops:
  29.3 14.7 %collective-permute-done.30 = bf16[128,8]{0,1:T(8,128)(2,1)S(1)} collective-permute-done((bf16[128,8]{0,1:T(8,128)(2,1)S(1)}, bf16[128,8]{0,1:T(8,128)(2,1)S(1)}, u32[]{:S(2)}, u32[]{:S(2)}) %collective-permute-start.30) | collective-permute-done | bytes 2080 | tf_op jit(solution)/shard_map/ppermute | solution.py:18
  44.0 6.3 collective-permute-done.31
  50.3 6.3 collective-permute-done.32
  56.6 5.4 collective-permute-done.33
  62.0 6.3 collective-permute-done.34
  68.3 5.4 collective-permute-done.35
  73.7 5.4 collective-permute-done.36
  79.0 4.5 collective-permute-done.37
  83.5 5.4 collective-permute-done.38
  89.5 3.8 collective-permute-done.39
  94.6 3.2 collective-permute-done.40
  97.9 5.1 collective-permute-start.41
  108.8 3.8 collective-permute-start.43
  113.9 5.0 collective-permute-start.44
  120.2 7.4 collective-permute-done.45
  127.6 6.3 collective-permute-done.46
  133.9 6.3 collective-permute-done.47
  140.2 5.4 collective-permute-done.48
  145.6 6.3 collective-permute-done.49
  151.8 5.4 collective-permute-done.50
  157.2 5.4 collective-permute-done.51
  162.6 4.5 collective-permute-done.52
  167.1 5.4 collective-permute-done.53
  173.1 4.0 collective-permute-done.54
  178.2 3.6 collective-permute-done.55
  181.9 5.1 collective-permute-start.56
  192.7 3.9 collective-permute-start.58
  196.6 10.0 %collective-permute-done.58 = bf16[128,8]{0,1:T(8,128)(2,1)S(1)} collective-permute-done((bf16[128,8]{0,1:T(8,128)(2,1)S(1)}, bf16[128,8]{0,1:T(8,128)(2,1)S(1)}, u32[]{:S(2)}, u32[]{:S(2)}) %collective-permute-start.58) | collective-permute-done | bytes 2080 | tf_op jit(solution)/shard_map/ppermute | solution.py:18
  206.6 3.6 collective-permute-done.59
  212.1 8.2 collective-permute-start.6
  226.6 11.5 %collective-permute-done.4 = bf16[128,1024]{1,0:T(8,128)(2,1)S(1)} collective-permute-done((bf16[128,1024]{1,0:T(8,128)(2,1)}, bf16[128,1024]{1,0:T(8,128)(2,1)S(1)}, u32[]{:S(2)}, u32[]{:S(2)}) %collective-permute-start.4) | collective-permute-done | bytes 262176 | tf_op jit(solution)/shard_map/ppermute | solution.py:18
  238.8 8.9 collective-permute-start.10
  249.1 12.6 %collective-permute-done.7 = bf16[128,1024]{1,0:T(8,128)(2,1)S(1)} collective-permute-done((bf16[128,1024]{1,0:T(8,128)(2,1)}, bf16[128,1024]{1,0:T(8,128)(2,1)S(1)}, u32[]{:S(2)}, u32[]{:S(2)}) %collective-permute-start.7) | collective-permute-done | bytes 262176 | tf_op jit(solution)/shard_map/ppermute | solution.py:18
  262.4 8.5 collective-permute-start.13
  271.7 3.8 collective-permute-start.14
  280.3 13.3 %collective-permute-start.17 = (bf16[128,1024]{1,0:T(8,128)(2,1)}, bf16[128,1024]{1,0:T(8,128)(2,1)S(1)}, u32[]{:S(2)}, u32[]{:S(2)}) collective-permute-start(bf16[128,1024]{1,0:T(8,128)(2,1)} %get-tuple-element.500), channel_id=1, source_target_pairs={{0,6},{2,8},{4,10},{6,12},{8,14},{10,16},{12,18},{14,20},{16,22},{... | collective-permute-start | bytes 786440 | tf_op jit(solution)/shard_map/ppermute | solution.py:18
  306.0 3.7 collective-permute-start.23
  309.8 12.2 %collective-permute-done.19 = bf16[128,1024]{1,0:T(8,128)(2,1)S(1)} collective-permute-done((bf16[128,1024]{1,0:T(8,128)(2,1)}, bf16[128,1024]{1,0:T(8,128)(2,1)S(1)}, u32[]{:S(2)}, u32[]{:S(2)}) %collective-permute-start.19) | collective-permute-done | bytes 262176 | tf_op jit(solution)/shard_map/ppermute | solution.py:18
  322.0 10.8 %collective-permute-done.20 = bf16[128,1024]{1,0:T(8,128)(2,1)S(1)} collective-permute-done((bf16[128,1024]{1,0:T(8,128)(2,1)}, bf16[128,1024]{1,0:T(8,128)(2,1)S(1)}, u32[]{:S(2)}, u32[]{:S(2)}) %collective-permute-start.20) | collective-permute-done | bytes 262176 | tf_op jit(solution)/shard_map/ppermute | solution.py:18
  332.8 7.0 collective-permute-start.26
  340.3 11.3 %collective-permute-start.28 = (bf16[128,1024]{1,0:T(8,128)(2,1)S(1)}, bf16[128,1024]{1,0:T(8,128)(2,1)S(1)}, u32[]{:S(2)}, u32[]{:S(2)}) collective-permute-start(bf16[128,1024]{1,0:T(8,128)(2,1)S(1)} %copy-done.11), channel_id=1, source_target_pairs={{0,28},{2,30},{4,0},{6,2},{8,4},{10,6},{12,8},{14,10},{16,12},{18,... | collective-permute-start | bytes 786440 | tf_op jit(solution)/shard_map/ppermute | solution.py:18
  351.6 5.5 collective-permute-start.29
  368.1 94.7 %while.42 = (s32[]{:T(128)}, bf16[8,128,128]{1,2,0:T(8,128)(2,1)S(1)}, bf16[8,128,128]{1,2,0:T(8,128)(2,1)}, f32[8,8,128]{2,1,0:T(8,128)S(1)}, f32[8,8,128]{2,1,...) while((s32[]{:T(128)}, ...), condition=%wide.region_4.5_spmd.clone, body=%wide.region_0.4_spmd.clone.sunk | while | flops 291065472 | bytes 13966631 | solution.py:86
  462.9 4.4 collective-permute-start.80
  475.7 3.8 collective-permute-start.83
  482.9 11.0 %collective-permute-start.85 = (bf16[128,1024]{1,0:T(8,128)(2,1)}, bf16[128,1024]{1,0:T(8,128)(2,1)S(1)}, u32[]{:S(2)}, u32[]{:S(2)}) collective-permute-start(bf16[128,1024]{1,0:T(8,128)(2,1)} %get-tuple-element.501), channel_id=1, source_target_pairs={{0,22},{2,24},{4,26},{6,28},{8,30},{10,0},{12,2},{14,4},{16,6},{18... | collective-permute-start | bytes 786440 | tf_op jit(solution)/shard_map/ppermute | solution.py:18
  494.7 5.7 collective-permute-start.86
  501.1 5.8 collective-permute-start.87
  507.7 9.6 %collective-permute-start.88 = (bf16[128,1024]{1,0:T(8,128)(2,1)}, bf16[128,1024]{1,0:T(8,128)(2,1)S(1)}, u32[]{:S(2)}, u32[]{:S(2)}) collective-permute-start(bf16[128,1024]{1,0:T(8,128)(2,1)} %get-tuple-element.501), channel_id=1, source_target_pairs={{0,28},{2,30},{4,0},{6,2},{8,4},{10,6},{12,8},{14,10},{16,12},{18,... | collective-permute-start | bytes 786440 | tf_op jit(solution)/shard_map/ppermute | solution.py:18
  518.0 18.1 %collective-permute-start.89 = (bf16[128,1024]{1,0:T(8,128)(2,1)}, bf16[128,1024]{1,0:T(8,128)(2,1)S(1)}, u32[]{:S(2)}, u32[]{:S(2)}) collective-permute-start(bf16[128,1024]{1,0:T(8,128)(2,1)} %get-tuple-element.501), channel_id=1, source_target_pairs={{0,30},{2,0},{4,2},{6,4},{8,6},{10,8},{12,10},{14,12},{16,14},{18,... | collective-permute-start | bytes 786440 | tf_op jit(solution)/shard_map/ppermute | solution.py:18
  541.8 4.8 collective-permute-done.89
  550.0 5.3 collective-permute-start.65
  555.4 8.7 collective-permute-start.66
  567.2 7.1 collective-permute-done.64
  574.3 17.6 %collective-permute-start.70 = (bf16[128,1024]{1,0:T(8,128)(2,1)S(1)}, bf16[128,1024]{1,0:T(8,128)(2,1)S(1)}, u32[]{:S(2)}, u32[]{:S(2)}) collective-permute-start(bf16[128,1024]{1,0:T(8,128)(2,1)S(1)} %copy-done.10), channel_id=1, source_target_pairs={{0,22},{2,24},{4,26},{6,28},{8,30},{10,0},{12,2},{14,4},{16,6},{18... | collective-permute-start | bytes 786440 | tf_op jit(solution)/shard_map/ppermute | solution.py:18
  597.5 15.9 %collective-permute-start.73 = (bf16[128,1024]{1,0:T(8,128)(2,1)S(1)}, bf16[128,1024]{1,0:T(8,128)(2,1)S(1)}, u32[]{:S(2)}, u32[]{:S(2)}) collective-permute-start(bf16[128,1024]{1,0:T(8,128)(2,1)S(1)} %copy-done.10), channel_id=1, source_target_pairs={{0,28},{2,30},{4,0},{6,2},{8,4},{10,6},{12,8},{14,10},{16,12},{18,... | collective-permute-start | bytes 786440 | tf_op jit(solution)/shard_map/ppermute | solution.py:18
  613.4 3.2 collective-permute-start.74
  617.3 3.2 collective-permute-done.74
  624.0 111.9 %while.43 = (s32[]{:T(128)}, bf16[8,128,128]{1,2,0:T(8,128)(2,1)S(1)}, bf16[8,128,128]{1,2,0:T(8,128)(2,1)}, f32[8,8,128]{2,1,0:T(8,128)S(1)}, f32[8,8,128]{2,1,...) while((s32[]{:T(128)}, ...), condition=%wide.region_9.10_spmd.clone, body=%wide.region_5.9_spmd.clone.sunk | while | flops 291065472 | bytes 13967139 | solution.py:86
  742.7 6.1 collective-permute-start.90
  751.5 6.7 collective-permute-start.95
  765.3 5.6 collective-permute-start.102
  772.8 4.5 collective-permute-done.103
  780.1 131.9 %all-reduce.3.cloned.1.call-done = (f32[4096,8]{0,1:T(8,128)}, f32[8,2048]{1,0:T(8,128)}, f32[4096,8]{0,1:T(8,128)}, f32[8,2048]{1,0:T(8,128)}, f32[4096,8]{0,1:...) async-done(((f32[4096,8]{0,1:T(8,128)}, f32[8,2048]{1,0:T(8,128)}, f32[4096,8]{0,1:T(8,128)}, f32[8,2048]{1,0:T(8,128)}, f32[4096,8]{0,1:T(8,128)}, ...) | async-done | bytes 786448 | tf_op jit(solution)/shard_map/psum | solution.py:225
  (595 shorter events, 345.7 us)
Async XLA Ops:
  7.2 904.8 %all-reduce.3.cloned.1.call-start = ((), (), s32[]{:S(2)}) async-start(), calls=%async_computation | async-start | bytes 1572864 | tf_op jit(solution)/shard_map/psum | solution.py:225
  9.3 201.1 %collective-permute-start = (bf16[128,1024]{1,0:T(8,128)(2,1)}, bf16[128,1024]{1,0:T(8,128)(2,1)}, u32[]{:S(2)}, u32[]{:S(2)}) collective-permute-start(bf16[128,1024]{1,0:T(8,128)(2,1)} %get-tuple-element.506), channel_id=1, source_target_pairs={{0,2},{2,4},{4,6},{6,8},{8,10},{10,12},{12,14},{14,16},{16,18},{18... | collective-permute-start | bytes 786440 | tf_op jit(solution)/shard_map/ppermute | solution.py:18
  12.2 199.9 %collective-permute-start.1 = (bf16[128,1024]{1,0:T(8,128)(2,1)}, bf16[128,1024]{1,0:T(8,128)(2,1)}, u32[]{:S(2)}, u32[]{:S(2)}) collective-permute-start(bf16[128,1024]{1,0:T(8,128)(2,1)} %get-tuple-element.506), channel_id=1, source_target_pairs={{0,4},{2,6},{4,8},{6,10},{8,12},{10,14},{12,16},{14,18},{16,20},{1... | collective-permute-start | bytes 786440 | tf_op jit(solution)/shard_map/ppermute | solution.py:18
  13.7 208.3 %collective-permute-start.2 = (bf16[128,1024]{1,0:T(8,128)(2,1)}, bf16[128,1024]{1,0:T(8,128)(2,1)}, u32[]{:S(2)}, u32[]{:S(2)}) collective-permute-start(bf16[128,1024]{1,0:T(8,128)(2,1)} %get-tuple-element.506), channel_id=1, source_target_pairs={{0,6},{2,8},{4,10},{6,12},{8,14},{10,16},{12,18},{14,20},{16,22},{... | collective-permute-start | bytes 786440 | tf_op jit(solution)/shard_map/ppermute | solution.py:18
  16.2 207.5 %collective-permute-start.3 = (bf16[128,1024]{1,0:T(8,128)(2,1)}, bf16[128,1024]{1,0:T(8,128)(2,1)}, u32[]{:S(2)}, u32[]{:S(2)}) collective-permute-start(bf16[128,1024]{1,0:T(8,128)(2,1)} %get-tuple-element.506), channel_id=1, source_target_pairs={{0,8},{2,10},{4,12},{6,14},{8,16},{10,18},{12,20},{14,22},{16,24},... | collective-permute-start | bytes 786440 | tf_op jit(solution)/shard_map/ppermute | solution.py:18
  19.0 25.0 %collective-permute-start.30 = (bf16[128,8]{0,1:T(8,128)(2,1)S(1)}, bf16[128,8]{0,1:T(8,128)(2,1)S(1)}, u32[]{:S(2)}, u32[]{:S(2)}) collective-permute-start(bf16[128,8]{0,1:T(8,128)(2,1)S(1)} %get-tuple-element.532), channel_id=1, source_target_pairs={{0,2},{2,4},{4,6},{6,8},{8,10},{10,12},{12,14},{14,16},{16,18},{18... | collective-permute-start | bytes 6152 | tf_op jit(solution)/shard_map/ppermute | solution.py:18
  192.7 13.9 %collective-permute-start.58 = (bf16[128,8]{0,1:T(8,128)(2,1)S(1)}, bf16[128,8]{0,1:T(8,128)(2,1)S(1)}, u32[]{:S(2)}, u32[]{:S(2)}) collective-permute-start(bf16[128,8]{0,1:T(8,128)(2,1)S(1)} %get-tuple-element.534), channel_id=1, source_target_pairs={{0,28},{2,30},{4,0},{6,2},{8,4},{10,6},{12,8},{14,10},{16,12},{18,... | collective-permute-start | bytes 6152 | tf_op jit(solution)/shard_map/ppermute | solution.py:18
  210.2 27.9 %collective-permute-start.4 = (bf16[128,1024]{1,0:T(8,128)(2,1)}, bf16[128,1024]{1,0:T(8,128)(2,1)S(1)}, u32[]{:S(2)}, u32[]{:S(2)}) collective-permute-start(bf16[128,1024]{1,0:T(8,128)(2,1)} %get-tuple-element.506), channel_id=1, source_target_pairs={{0,10},{2,12},{4,14},{6,16},{8,18},{10,20},{12,22},{14,24},{16,26}... | collective-permute-start | bytes 786440 | tf_op jit(solution)/shard_map/ppermute | solution.py:18
  210.4 28.5 %collective-permute-start.5 = (bf16[128,1024]{1,0:T(8,128)(2,1)}, bf16[128,1024]{1,0:T(8,128)(2,1)S(1)}, u32[]{:S(2)}, u32[]{:S(2)}) collective-permute-start(bf16[128,1024]{1,0:T(8,128)(2,1)} %get-tuple-element.506), channel_id=1, source_target_pairs={{0,12},{2,14},{4,16},{6,18},{8,20},{10,22},{12,24},{14,26},{16,28}... | collective-permute-start | bytes 786440 | tf_op jit(solution)/shard_map/ppermute | solution.py:18
  212.1 36.3 %collective-permute-start.6 = (bf16[128,1024]{1,0:T(8,128)(2,1)}, bf16[128,1024]{1,0:T(8,128)(2,1)S(1)}, u32[]{:S(2)}, u32[]{:S(2)}) collective-permute-start(bf16[128,1024]{1,0:T(8,128)(2,1)} %get-tuple-element.506), channel_id=1, source_target_pairs={{0,14},{2,16},{4,18},{6,20},{8,22},{10,24},{12,26},{14,28},{16,30}... | collective-permute-start | bytes 786440 | tf_op jit(solution)/shard_map/ppermute | solution.py:18
  222.0 39.7 %collective-permute-start.7 = (bf16[128,1024]{1,0:T(8,128)(2,1)}, bf16[128,1024]{1,0:T(8,128)(2,1)S(1)}, u32[]{:S(2)}, u32[]{:S(2)}) collective-permute-start(bf16[128,1024]{1,0:T(8,128)(2,1)} %get-tuple-element.506), channel_id=1, source_target_pairs={{0,16},{2,18},{4,20},{6,22},{8,24},{10,26},{12,28},{14,30},{16,0},... | collective-permute-start | bytes 786440 | tf_op jit(solution)/shard_map/ppermute | solution.py:18
  223.7 38.7 %collective-permute-start.8 = (bf16[128,1024]{1,0:T(8,128)(2,1)}, bf16[128,1024]{1,0:T(8,128)(2,1)S(1)}, u32[]{:S(2)}, u32[]{:S(2)}) collective-permute-start(bf16[128,1024]{1,0:T(8,128)(2,1)} %get-tuple-element.506), channel_id=1, source_target_pairs={{0,18},{2,20},{4,22},{6,24},{8,26},{10,28},{12,30},{14,0},{16,2},{... | collective-permute-start | bytes 786440 | tf_op jit(solution)/shard_map/ppermute | solution.py:18
  238.1 33.6 %collective-permute-start.9 = (bf16[128,1024]{1,0:T(8,128)(2,1)}, bf16[128,1024]{1,0:T(8,128)(2,1)S(1)}, u32[]{:S(2)}, u32[]{:S(2)}) collective-permute-start(bf16[128,1024]{1,0:T(8,128)(2,1)} %get-tuple-element.506), channel_id=1, source_target_pairs={{0,20},{2,22},{4,24},{6,26},{8,28},{10,30},{12,0},{14,2},{16,4},{1... | collective-permute-start | bytes 786440 | tf_op jit(solution)/shard_map/ppermute | solution.py:18
  238.8 37.4 %collective-permute-start.10 = (bf16[128,1024]{1,0:T(8,128)(2,1)}, bf16[128,1024]{1,0:T(8,128)(2,1)S(1)}, u32[]{:S(2)}, u32[]{:S(2)}) collective-permute-start(bf16[128,1024]{1,0:T(8,128)(2,1)} %get-tuple-element.506), channel_id=1, source_target_pairs={{0,22},{2,24},{4,26},{6,28},{8,30},{10,0},{12,2},{14,4},{16,6},{18... | collective-permute-start | bytes 786440 | tf_op jit(solution)/shard_map/ppermute | solution.py:18
  248.4 29.1 %collective-permute-start.11 = (bf16[128,1024]{1,0:T(8,128)(2,1)}, bf16[128,1024]{1,0:T(8,128)(2,1)S(1)}, u32[]{:S(2)}, u32[]{:S(2)}) collective-permute-start(bf16[128,1024]{1,0:T(8,128)(2,1)} %get-tuple-element.506), channel_id=1, source_target_pairs={{0,24},{2,26},{4,28},{6,30},{8,0},{10,2},{12,4},{14,6},{16,8},{18,... | collective-permute-start | bytes 786440 | tf_op jit(solution)/shard_map/ppermute | solution.py:18
  261.7 18.6 %collective-permute-start.12 = (bf16[128,1024]{1,0:T(8,128)(2,1)}, bf16[128,1024]{1,0:T(8,128)(2,1)S(1)}, u32[]{:S(2)}, u32[]{:S(2)}) collective-permute-start(bf16[128,1024]{1,0:T(8,128)(2,1)} %get-tuple-element.506), channel_id=1, source_target_pairs={{0,26},{2,28},{4,30},{6,0},{8,2},{10,4},{12,6},{14,8},{16,10},{18,... | collective-permute-start | bytes 786440 | tf_op jit(solution)/shard_map/ppermute | solution.py:18
  262.4 31.9 %collective-permute-start.13 = (bf16[128,1024]{1,0:T(8,128)(2,1)}, bf16[128,1024]{1,0:T(8,128)(2,1)S(1)}, u32[]{:S(2)}, u32[]{:S(2)}) collective-permute-start(bf16[128,1024]{1,0:T(8,128)(2,1)} %get-tuple-element.506), channel_id=1, source_target_pairs={{0,28},{2,30},{4,0},{6,2},{8,4},{10,6},{12,8},{14,10},{16,12},{18,... | collective-permute-start | bytes 786440 | tf_op jit(solution)/shard_map/ppermute | solution.py:18
  271.7 25.8 %collective-permute-start.14 = (bf16[128,1024]{1,0:T(8,128)(2,1)}, bf16[128,1024]{1,0:T(8,128)(2,1)S(1)}, u32[]{:S(2)}, u32[]{:S(2)}) collective-permute-start(bf16[128,1024]{1,0:T(8,128)(2,1)} %get-tuple-element.506), channel_id=1, source_target_pairs={{0,30},{2,0},{4,2},{6,4},{8,6},{10,8},{12,10},{14,12},{16,14},{18,... | collective-permute-start | bytes 786440 | tf_op jit(solution)/shard_map/ppermute | solution.py:18
  276.2 24.4 %collective-permute-start.15 = (bf16[128,1024]{1,0:T(8,128)(2,1)}, bf16[128,1024]{1,0:T(8,128)(2,1)S(1)}, u32[]{:S(2)}, u32[]{:S(2)}) collective-permute-start(bf16[128,1024]{1,0:T(8,128)(2,1)} %get-tuple-element.500), channel_id=1, source_target_pairs={{0,2},{2,4},{4,6},{6,8},{8,10},{10,12},{12,14},{14,16},{16,18},{18... | collective-permute-start | bytes 786440 | tf_op jit(solution)/shard_map/ppermute | solution.py:18
  277.5 25.0 %collective-permute-start.16 = (bf16[128,1024]{1,0:T(8,128)(2,1)}, bf16[128,1024]{1,0:T(8,128)(2,1)S(1)}, u32[]{:S(2)}, u32[]{:S(2)}) collective-permute-start(bf16[128,1024]{1,0:T(8,128)(2,1)} %get-tuple-element.500), channel_id=1, source_target_pairs={{0,4},{2,6},{4,8},{6,10},{8,12},{10,14},{12,16},{14,18},{16,20},{1... | collective-permute-start | bytes 786440 | tf_op jit(solution)/shard_map/ppermute | solution.py:18
  280.3 25.2 %collective-permute-start.17 = (bf16[128,1024]{1,0:T(8,128)(2,1)}, bf16[128,1024]{1,0:T(8,128)(2,1)S(1)}, u32[]{:S(2)}, u32[]{:S(2)}) collective-permute-start(bf16[128,1024]{1,0:T(8,128)(2,1)} %get-tuple-element.500), channel_id=1, source_target_pairs={{0,6},{2,8},{4,10},{6,12},{8,14},{10,16},{12,18},{14,20},{16,22},{... | collective-permute-start | bytes 786440 | tf_op jit(solution)/shard_map/ppermute | solution.py:18
  297.5 24.5 %collective-permute-start.19 = (bf16[128,1024]{1,0:T(8,128)(2,1)}, bf16[128,1024]{1,0:T(8,128)(2,1)S(1)}, u32[]{:S(2)}, u32[]{:S(2)}) collective-permute-start(bf16[128,1024]{1,0:T(8,128)(2,1)} %get-tuple-element.500), channel_id=1, source_target_pairs={{0,10},{2,12},{4,14},{6,16},{8,18},{10,20},{12,22},{14,24},{16,26}... | collective-permute-start | bytes 786440 | tf_op jit(solution)/shard_map/ppermute | solution.py:18
  300.7 32.1 %collective-permute-start.20 = (bf16[128,1024]{1,0:T(8,128)(2,1)}, bf16[128,1024]{1,0:T(8,128)(2,1)S(1)}, u32[]{:S(2)}, u32[]{:S(2)}) collective-permute-start(bf16[128,1024]{1,0:T(8,128)(2,1)} %get-tuple-element.500), channel_id=1, source_target_pairs={{0,12},{2,14},{4,16},{6,18},{8,20},{10,22},{12,24},{14,26},{16,28}... | collective-permute-start | bytes 786440 | tf_op jit(solution)/shard_map/ppermute | solution.py:18
  302.5 30.3 %collective-permute-start.21 = (bf16[128,1024]{1,0:T(8,128)(2,1)S(1)}, bf16[128,1024]{1,0:T(8,128)(2,1)S(1)}, u32[]{:S(2)}, u32[]{:S(2)}) collective-permute-start(bf16[128,1024]{1,0:T(8,128)(2,1)S(1)} %copy-done.11), channel_id=1, source_target_pairs={{0,14},{2,16},{4,18},{6,20},{8,22},{10,24},{12,26},{14,28},{16,30}... | collective-permute-start | bytes 786440 | tf_op jit(solution)/shard_map/ppermute | solution.py:18
  305.4 34.4 %collective-permute-start.22 = (bf16[128,1024]{1,0:T(8,128)(2,1)S(1)}, bf16[128,1024]{1,0:T(8,128)(2,1)S(1)}, u32[]{:S(2)}, u32[]{:S(2)}) collective-permute-start(bf16[128,1024]{1,0:T(8,128)(2,1)S(1)} %copy-done.11), channel_id=1, source_target_pairs={{0,16},{2,18},{4,20},{6,22},{8,24},{10,26},{12,28},{14,30},{16,0},... | collective-permute-start | bytes 786440 | tf_op jit(solution)/shard_map/ppermute | solution.py:18
  306.0 34.3 %collective-permute-start.23 = (bf16[128,1024]{1,0:T(8,128)(2,1)S(1)}, bf16[128,1024]{1,0:T(8,128)(2,1)S(1)}, u32[]{:S(2)}, u32[]{:S(2)}) collective-permute-start(bf16[128,1024]{1,0:T(8,128)(2,1)S(1)} %copy-done.11), channel_id=1, source_target_pairs={{0,18},{2,20},{4,22},{6,24},{8,26},{10,28},{12,30},{14,0},{16,2},{... | collective-permute-start | bytes 786440 | tf_op jit(solution)/shard_map/ppermute | solution.py:18
  322.0 29.6 %collective-permute-start.24 = (bf16[128,1024]{1,0:T(8,128)(2,1)S(1)}, bf16[128,1024]{1,0:T(8,128)(2,1)S(1)}, u32[]{:S(2)}, u32[]{:S(2)}) collective-permute-start(bf16[128,1024]{1,0:T(8,128)(2,1)S(1)} %copy-done.11), channel_id=1, source_target_pairs={{0,20},{2,22},{4,24},{6,26},{8,28},{10,30},{12,0},{14,2},{16,4},{1... | collective-permute-start | bytes 786440 | tf_op jit(solution)/shard_map/ppermute | solution.py:18
  332.8 24.4 %collective-permute-start.25 = (bf16[128,1024]{1,0:T(8,128)(2,1)S(1)}, bf16[128,1024]{1,0:T(8,128)(2,1)S(1)}, u32[]{:S(2)}, u32[]{:S(2)}) collective-permute-start(bf16[128,1024]{1,0:T(8,128)(2,1)S(1)} %copy-done.11), channel_id=1, source_target_pairs={{0,22},{2,24},{4,26},{6,28},{8,30},{10,0},{12,2},{14,4},{16,6},{18... | collective-permute-start | bytes 786440 | tf_op jit(solution)/shard_map/ppermute | solution.py:18
  332.8 25.0 %collective-permute-start.26 = (bf16[128,1024]{1,0:T(8,128)(2,1)S(1)}, bf16[128,1024]{1,0:T(8,128)(2,1)S(1)}, u32[]{:S(2)}, u32[]{:S(2)}) collective-permute-start(bf16[128,1024]{1,0:T(8,128)(2,1)S(1)} %copy-done.11), channel_id=1, source_target_pairs={{0,24},{2,26},{4,28},{6,30},{8,0},{10,2},{12,4},{14,6},{16,8},{18,... | collective-permute-start | bytes 786440 | tf_op jit(solution)/shard_map/ppermute | solution.py:18
  339.8 20.1 %collective-permute-start.27 = (bf16[128,1024]{1,0:T(8,128)(2,1)S(1)}, bf16[128,1024]{1,0:T(8,128)(2,1)S(1)}, u32[]{:S(2)}, u32[]{:S(2)}) collective-permute-start(bf16[128,1024]{1,0:T(8,128)(2,1)S(1)} %copy-done.11), channel_id=1, source_target_pairs={{0,26},{2,28},{4,30},{6,0},{8,2},{10,4},{12,6},{14,8},{16,10},{18,... | collective-permute-start | bytes 786440 | tf_op jit(solution)/shard_map/ppermute | solution.py:18
  340.3 22.0 %collective-permute-start.28 = (bf16[128,1024]{1,0:T(8,128)(2,1)S(1)}, bf16[128,1024]{1,0:T(8,128)(2,1)S(1)}, u32[]{:S(2)}, u32[]{:S(2)}) collective-permute-start(bf16[128,1024]{1,0:T(8,128)(2,1)S(1)} %copy-done.11), channel_id=1, source_target_pairs={{0,28},{2,30},{4,0},{6,2},{8,4},{10,6},{12,8},{14,10},{16,12},{18,... | collective-permute-start | bytes 786440 | tf_op jit(solution)/shard_map/ppermute | solution.py:18
  351.6 11.8 %collective-permute-start.29 = (bf16[128,1024]{1,0:T(8,128)(2,1)S(1)}, bf16[128,1024]{1,0:T(8,128)(2,1)S(1)}, u32[]{:S(2)}, u32[]{:S(2)}) collective-permute-start(bf16[128,1024]{1,0:T(8,128)(2,1)S(1)} %copy-done.11), channel_id=1, source_target_pairs={{0,30},{2,0},{4,2},{6,4},{8,6},{10,8},{12,10},{14,12},{16,14},{18,... | collective-permute-start | bytes 786440 | tf_op jit(solution)/shard_map/ppermute | solution.py:18
  357.2 105.7 %collective-permute-start.75 = (bf16[128,1024]{1,0:T(8,128)(2,1)}, bf16[128,1024]{1,0:T(8,128)(2,1)}, u32[]{:S(2)}, u32[]{:S(2)}) collective-permute-start(bf16[128,1024]{1,0:T(8,128)(2,1)} %get-tuple-element.501), channel_id=1, source_target_pairs={{0,2},{2,4},{4,6},{6,8},{8,10},{10,12},{12,14},{14,16},{16,18},{18... | collective-permute-start | bytes 786440 | tf_op jit(solution)/shard_map/ppermute | solution.py:18
  357.8 111.2 %collective-permute-start.76 = (bf16[128,1024]{1,0:T(8,128)(2,1)}, bf16[128,1024]{1,0:T(8,128)(2,1)}, u32[]{:S(2)}, u32[]{:S(2)}) collective-permute-start(bf16[128,1024]{1,0:T(8,128)(2,1)} %get-tuple-element.501), channel_id=1, source_target_pairs={{0,4},{2,6},{4,8},{6,10},{8,12},{10,14},{12,16},{14,18},{16,20},{1... | collective-permute-start | bytes 786440 | tf_op jit(solution)/shard_map/ppermute | solution.py:18
  359.9 113.2 %collective-permute-start.77 = (bf16[128,1024]{1,0:T(8,128)(2,1)}, bf16[128,1024]{1,0:T(8,128)(2,1)}, u32[]{:S(2)}, u32[]{:S(2)}) collective-permute-start(bf16[128,1024]{1,0:T(8,128)(2,1)} %get-tuple-element.501), channel_id=1, source_target_pairs={{0,6},{2,8},{4,10},{6,12},{8,14},{10,16},{12,18},{14,20},{16,22},{... | collective-permute-start | bytes 786440 | tf_op jit(solution)/shard_map/ppermute | solution.py:18
  362.4 113.4 %collective-permute-start.78 = (bf16[128,1024]{1,0:T(8,128)(2,1)}, bf16[128,1024]{1,0:T(8,128)(2,1)}, u32[]{:S(2)}, u32[]{:S(2)}) collective-permute-start(bf16[128,1024]{1,0:T(8,128)(2,1)} %get-tuple-element.501), channel_id=1, source_target_pairs={{0,8},{2,10},{4,12},{6,14},{8,16},{10,18},{12,20},{14,22},{16,24},... | collective-permute-start | bytes 786440 | tf_op jit(solution)/shard_map/ppermute | solution.py:18
  363.4 117.9 %collective-permute-start.79 = (bf16[128,1024]{1,0:T(8,128)(2,1)}, bf16[128,1024]{1,0:T(8,128)(2,1)}, u32[]{:S(2)}, u32[]{:S(2)}) collective-permute-start(bf16[128,1024]{1,0:T(8,128)(2,1)} %get-tuple-element.501), channel_id=1, source_target_pairs={{0,10},{2,12},{4,14},{6,16},{8,18},{10,20},{12,22},{14,24},{16,26}... | collective-permute-start | bytes 786440 | tf_op jit(solution)/shard_map/ppermute | solution.py:18
  462.9 20.1 %collective-permute-start.80 = (bf16[128,1024]{1,0:T(8,128)(2,1)}, bf16[128,1024]{1,0:T(8,128)(2,1)S(1)}, u32[]{:S(2)}, u32[]{:S(2)}) collective-permute-start(bf16[128,1024]{1,0:T(8,128)(2,1)} %get-tuple-element.501), channel_id=1, source_target_pairs={{0,12},{2,14},{4,16},{6,18},{8,20},{10,22},{12,24},{14,26},{16,28}... | collective-permute-start | bytes 786440 | tf_op jit(solution)/shard_map/ppermute | solution.py:18
  469.0 25.7 %collective-permute-start.81 = (bf16[128,1024]{1,0:T(8,128)(2,1)}, bf16[128,1024]{1,0:T(8,128)(2,1)S(1)}, u32[]{:S(2)}, u32[]{:S(2)}) collective-permute-start(bf16[128,1024]{1,0:T(8,128)(2,1)} %get-tuple-element.501), channel_id=1, source_target_pairs={{0,14},{2,16},{4,18},{6,20},{8,22},{10,24},{12,26},{14,28},{16,30}... | collective-permute-start | bytes 786440 | tf_op jit(solution)/shard_map/ppermute | solution.py:18
  473.1 28.0 %collective-permute-start.82 = (bf16[128,1024]{1,0:T(8,128)(2,1)}, bf16[128,1024]{1,0:T(8,128)(2,1)S(1)}, u32[]{:S(2)}, u32[]{:S(2)}) collective-permute-start(bf16[128,1024]{1,0:T(8,128)(2,1)} %get-tuple-element.501), channel_id=1, source_target_pairs={{0,16},{2,18},{4,20},{6,22},{8,24},{10,26},{12,28},{14,30},{16,0},... | collective-permute-start | bytes 786440 | tf_op jit(solution)/shard_map/ppermute | solution.py:18
  475.7 31.9 %collective-permute-start.83 = (bf16[128,1024]{1,0:T(8,128)(2,1)}, bf16[128,1024]{1,0:T(8,128)(2,1)S(1)}, u32[]{:S(2)}, u32[]{:S(2)}) collective-permute-start(bf16[128,1024]{1,0:T(8,128)(2,1)} %get-tuple-element.501), channel_id=1, source_target_pairs={{0,18},{2,20},{4,22},{6,24},{8,26},{10,28},{12,30},{14,0},{16,2},{... | collective-permute-start | bytes 786440 | tf_op jit(solution)/shard_map/ppermute | solution.py:18
  481.2 36.8 %collective-permute-start.84 = (bf16[128,1024]{1,0:T(8,128)(2,1)}, bf16[128,1024]{1,0:T(8,128)(2,1)S(1)}, u32[]{:S(2)}, u32[]{:S(2)}) collective-permute-start(bf16[128,1024]{1,0:T(8,128)(2,1)} %get-tuple-element.501), channel_id=1, source_target_pairs={{0,20},{2,22},{4,24},{6,26},{8,28},{10,30},{12,0},{14,2},{16,4},{1... | collective-permute-start | bytes 786440 | tf_op jit(solution)/shard_map/ppermute | solution.py:18
  482.9 53.9 %collective-permute-start.85 = (bf16[128,1024]{1,0:T(8,128)(2,1)}, bf16[128,1024]{1,0:T(8,128)(2,1)S(1)}, u32[]{:S(2)}, u32[]{:S(2)}) collective-permute-start(bf16[128,1024]{1,0:T(8,128)(2,1)} %get-tuple-element.501), channel_id=1, source_target_pairs={{0,22},{2,24},{4,26},{6,28},{8,30},{10,0},{12,2},{14,4},{16,6},{18... | collective-permute-start | bytes 786440 | tf_op jit(solution)/shard_map/ppermute | solution.py:18
  494.7 43.5 %collective-permute-start.86 = (bf16[128,1024]{1,0:T(8,128)(2,1)}, bf16[128,1024]{1,0:T(8,128)(2,1)S(1)}, u32[]{:S(2)}, u32[]{:S(2)}) collective-permute-start(bf16[128,1024]{1,0:T(8,128)(2,1)} %get-tuple-element.501), channel_id=1, source_target_pairs={{0,24},{2,26},{4,28},{6,30},{8,0},{10,2},{12,4},{14,6},{16,8},{18,... | collective-permute-start | bytes 786440 | tf_op jit(solution)/shard_map/ppermute | solution.py:18
  501.1 39.2 %collective-permute-start.87 = (bf16[128,1024]{1,0:T(8,128)(2,1)}, bf16[128,1024]{1,0:T(8,128)(2,1)S(1)}, u32[]{:S(2)}, u32[]{:S(2)}) collective-permute-start(bf16[128,1024]{1,0:T(8,128)(2,1)} %get-tuple-element.501), channel_id=1, source_target_pairs={{0,26},{2,28},{4,30},{6,0},{8,2},{10,4},{12,6},{14,8},{16,10},{18,... | collective-permute-start | bytes 786440 | tf_op jit(solution)/shard_map/ppermute | solution.py:18
  507.7 33.4 %collective-permute-start.88 = (bf16[128,1024]{1,0:T(8,128)(2,1)}, bf16[128,1024]{1,0:T(8,128)(2,1)S(1)}, u32[]{:S(2)}, u32[]{:S(2)}) collective-permute-start(bf16[128,1024]{1,0:T(8,128)(2,1)} %get-tuple-element.501), channel_id=1, source_target_pairs={{0,28},{2,30},{4,0},{6,2},{8,4},{10,6},{12,8},{14,10},{16,12},{18,... | collective-permute-start | bytes 786440 | tf_op jit(solution)/shard_map/ppermute | solution.py:18
  518.0 28.6 %collective-permute-start.89 = (bf16[128,1024]{1,0:T(8,128)(2,1)}, bf16[128,1024]{1,0:T(8,128)(2,1)S(1)}, u32[]{:S(2)}, u32[]{:S(2)}) collective-permute-start(bf16[128,1024]{1,0:T(8,128)(2,1)} %get-tuple-element.501), channel_id=1, source_target_pairs={{0,30},{2,0},{4,2},{6,4},{8,6},{10,8},{12,10},{14,12},{16,14},{18,... | collective-permute-start | bytes 786440 | tf_op jit(solution)/shard_map/ppermute | solution.py:18
  536.8 13.2 %collective-permute-start.60 = (bf16[128,1024]{1,0:T(8,128)(2,1)S(1)}, bf16[128,1024]{1,0:T(8,128)(2,1)S(1)}, u32[]{:S(2)}, u32[]{:S(2)}) collective-permute-start(bf16[128,1024]{1,0:T(8,128)(2,1)S(1)} %copy-done.10), channel_id=1, source_target_pairs={{0,2},{2,4},{4,6},{6,8},{8,10},{10,12},{12,14},{14,16},{16,18},{18... | collective-permute-start | bytes 786440 | tf_op jit(solution)/shard_map/ppermute | solution.py:18
  538.1 17.2 %collective-permute-start.61 = (bf16[128,1024]{1,0:T(8,128)(2,1)S(1)}, bf16[128,1024]{1,0:T(8,128)(2,1)S(1)}, u32[]{:S(2)}, u32[]{:S(2)}) collective-permute-start(bf16[128,1024]{1,0:T(8,128)(2,1)S(1)} %copy-done.10), channel_id=1, source_target_pairs={{0,4},{2,6},{4,8},{6,10},{8,12},{10,14},{12,16},{14,18},{16,20},{1... | collective-permute-start | bytes 786440 | tf_op jit(solution)/shard_map/ppermute | solution.py:18
  540.3 23.7 %collective-permute-start.62 = (bf16[128,1024]{1,0:T(8,128)(2,1)S(1)}, bf16[128,1024]{1,0:T(8,128)(2,1)S(1)}, u32[]{:S(2)}, u32[]{:S(2)}) collective-permute-start(bf16[128,1024]{1,0:T(8,128)(2,1)S(1)} %copy-done.10), channel_id=1, source_target_pairs={{0,6},{2,8},{4,10},{6,12},{8,14},{10,16},{12,18},{14,20},{16,22},{... | collective-permute-start | bytes 786440 | tf_op jit(solution)/shard_map/ppermute | solution.py:18
  541.1 23.1 %collective-permute-start.63 = (bf16[128,1024]{1,0:T(8,128)(2,1)S(1)}, bf16[128,1024]{1,0:T(8,128)(2,1)S(1)}, u32[]{:S(2)}, u32[]{:S(2)}) collective-permute-start(bf16[128,1024]{1,0:T(8,128)(2,1)S(1)} %copy-done.10), channel_id=1, source_target_pairs={{0,8},{2,10},{4,12},{6,14},{8,16},{10,18},{12,20},{14,22},{16,24},... | collective-permute-start | bytes 786440 | tf_op jit(solution)/shard_map/ppermute | solution.py:18
  546.6 27.7 %collective-permute-start.64 = (bf16[128,1024]{1,0:T(8,128)(2,1)S(1)}, bf16[128,1024]{1,0:T(8,128)(2,1)S(1)}, u32[]{:S(2)}, u32[]{:S(2)}) collective-permute-start(bf16[128,1024]{1,0:T(8,128)(2,1)S(1)} %copy-done.10), channel_id=1, source_target_pairs={{0,10},{2,12},{4,14},{6,16},{8,18},{10,20},{12,22},{14,24},{16,26}... | collective-permute-start | bytes 786440 | tf_op jit(solution)/shard_map/ppermute | solution.py:18
  550.0 24.3 %collective-permute-start.65 = (bf16[128,1024]{1,0:T(8,128)(2,1)S(1)}, bf16[128,1024]{1,0:T(8,128)(2,1)S(1)}, u32[]{:S(2)}, u32[]{:S(2)}) collective-permute-start(bf16[128,1024]{1,0:T(8,128)(2,1)S(1)} %copy-done.10), channel_id=1, source_target_pairs={{0,12},{2,14},{4,16},{6,18},{8,20},{10,22},{12,24},{14,26},{16,28}... | collective-permute-start | bytes 786440 | tf_op jit(solution)/shard_map/ppermute | solution.py:18
  555.4 36.6 %collective-permute-start.66 = (bf16[128,1024]{1,0:T(8,128)(2,1)S(1)}, bf16[128,1024]{1,0:T(8,128)(2,1)S(1)}, u32[]{:S(2)}, u32[]{:S(2)}) collective-permute-start(bf16[128,1024]{1,0:T(8,128)(2,1)S(1)} %copy-done.10), channel_id=1, source_target_pairs={{0,14},{2,16},{4,18},{6,20},{8,22},{10,24},{12,26},{14,28},{16,30}... | collective-permute-start | bytes 786440 | tf_op jit(solution)/shard_map/ppermute | solution.py:18
  564.1 30.8 %collective-permute-start.67 = (bf16[128,1024]{1,0:T(8,128)(2,1)S(1)}, bf16[128,1024]{1,0:T(8,128)(2,1)S(1)}, u32[]{:S(2)}, u32[]{:S(2)}) collective-permute-start(bf16[128,1024]{1,0:T(8,128)(2,1)S(1)} %copy-done.10), channel_id=1, source_target_pairs={{0,16},{2,18},{4,20},{6,22},{8,24},{10,26},{12,28},{14,30},{16,0},... | collective-permute-start | bytes 786440 | tf_op jit(solution)/shard_map/ppermute | solution.py:18
  564.2 33.3 %collective-permute-start.68 = (bf16[128,1024]{1,0:T(8,128)(2,1)S(1)}, bf16[128,1024]{1,0:T(8,128)(2,1)S(1)}, u32[]{:S(2)}, u32[]{:S(2)}) collective-permute-start(bf16[128,1024]{1,0:T(8,128)(2,1)S(1)} %copy-done.10), channel_id=1, source_target_pairs={{0,18},{2,20},{4,22},{6,24},{8,26},{10,28},{12,30},{14,0},{16,2},{... | collective-permute-start | bytes 786440 | tf_op jit(solution)/shard_map/ppermute | solution.py:18
  574.3 39.1 %collective-permute-start.69 = (bf16[128,1024]{1,0:T(8,128)(2,1)S(1)}, bf16[128,1024]{1,0:T(8,128)(2,1)S(1)}, u32[]{:S(2)}, u32[]{:S(2)}) collective-permute-start(bf16[128,1024]{1,0:T(8,128)(2,1)S(1)} %copy-done.10), channel_id=1, source_target_pairs={{0,20},{2,22},{4,24},{6,26},{8,28},{10,30},{12,0},{14,2},{16,4},{1... | collective-permute-start | bytes 786440 | tf_op jit(solution)/shard_map/ppermute | solution.py:18
  574.3 42.3 %collective-permute-start.70 = (bf16[128,1024]{1,0:T(8,128)(2,1)S(1)}, bf16[128,1024]{1,0:T(8,128)(2,1)S(1)}, u32[]{:S(2)}, u32[]{:S(2)}) collective-permute-start(bf16[128,1024]{1,0:T(8,128)(2,1)S(1)} %copy-done.10), channel_id=1, source_target_pairs={{0,22},{2,24},{4,26},{6,28},{8,30},{10,0},{12,2},{14,4},{16,6},{18... | collective-permute-start | bytes 786440 | tf_op jit(solution)/shard_map/ppermute | solution.py:18
  591.9 24.7 %collective-permute-start.71 = (bf16[128,1024]{1,0:T(8,128)(2,1)S(1)}, bf16[128,1024]{1,0:T(8,128)(2,1)S(1)}, u32[]{:S(2)}, u32[]{:S(2)}) collective-permute-start(bf16[128,1024]{1,0:T(8,128)(2,1)S(1)} %copy-done.10), channel_id=1, source_target_pairs={{0,24},{2,26},{4,28},{6,30},{8,0},{10,2},{12,4},{14,6},{16,8},{18,... | collective-permute-start | bytes 786440 | tf_op jit(solution)/shard_map/ppermute | solution.py:18
  594.8 21.9 %collective-permute-start.72 = (bf16[128,1024]{1,0:T(8,128)(2,1)S(1)}, bf16[128,1024]{1,0:T(8,128)(2,1)S(1)}, u32[]{:S(2)}, u32[]{:S(2)}) collective-permute-start(bf16[128,1024]{1,0:T(8,128)(2,1)S(1)} %copy-done.10), channel_id=1, source_target_pairs={{0,26},{2,28},{4,30},{6,0},{8,2},{10,4},{12,6},{14,8},{16,10},{18,... | collective-permute-start | bytes 786440 | tf_op jit(solution)/shard_map/ppermute | solution.py:18
  597.5 19.8 %collective-permute-start.73 = (bf16[128,1024]{1,0:T(8,128)(2,1)S(1)}, bf16[128,1024]{1,0:T(8,128)(2,1)S(1)}, u32[]{:S(2)}, u32[]{:S(2)}) collective-permute-start(bf16[128,1024]{1,0:T(8,128)(2,1)S(1)} %copy-done.10), channel_id=1, source_target_pairs={{0,28},{2,30},{4,0},{6,2},{8,4},{10,6},{12,8},{14,10},{16,12},{18,... | collective-permute-start | bytes 786440 | tf_op jit(solution)/shard_map/ppermute | solution.py:18
  748.9 13.3 %collective-permute-start.94 = (f32[128,16]{0,1:T(8,128)S(1)}, f32[128,16]{0,1:T(8,128)S(1)}, u32[]{:S(2)}, u32[]{:S(2)}) collective-permute-start(f32[128,16]{0,1:T(8,128)S(1)} %get-tuple-element.516), channel_id=1, source_target_pairs={{0,22},{2,24},{4,26},{6,28},{8,30},{10,0},{12,2},{14,4},{16,6},{18... | collective-permute-start | bytes 24584 | tf_op jit(solution)/shard_map/ppermute | solution.py:18
  751.5 13.3 %collective-permute-start.95 = (f32[128,16]{0,1:T(8,128)S(1)}, f32[128,16]{0,1:T(8,128)S(1)}, u32[]{:S(2)}, u32[]{:S(2)}) collective-permute-start(f32[128,16]{0,1:T(8,128)S(1)} %get-tuple-element.517), channel_id=1, source_target_pairs={{0,20},{2,22},{4,24},{6,26},{8,28},{10,30},{12,0},{14,2},{16,4},{1... | collective-permute-start | bytes 24584 | tf_op jit(solution)/shard_map/ppermute | solution.py:18
  758.2 12.7 %collective-permute-start.97 = (f32[128,16]{0,1:T(8,128)S(1)}, f32[128,16]{0,1:T(8,128)S(1)}, u32[]{:S(2)}, u32[]{:S(2)}) collective-permute-start(f32[128,16]{0,1:T(8,128)S(1)} %get-tuple-element.519), channel_id=1, source_target_pairs={{0,16},{2,18},{4,20},{6,22},{8,24},{10,26},{12,28},{14,30},{16,0},... | collective-permute-start | bytes 24584 | tf_op jit(solution)/shard_map/ppermute | solution.py:18
  (63 other events, 1057.8 us)
Sparse Core Ops, SparseCore 0:
  780.2 131.7 all-reduce.2
where the time goes:
time: 937 us; the launch traced here: 931 us
  waiting for transfers between devices  353 us (38%)
  starting transfers between devices  281 us (30%)
  matrix products  155 us (17%)
  local copies, waits for them, and re-layouts  102 us (11%)
  between operations  14.8 us (2%)
  other arithmetic  13.3 us (1%)
  loops' own time  11.3 us (1%)
    ppermute x105, starting transfers between devices, passed_along(): return lax.ppermute(value, axis, pairs)  281 us
    ppermute x105, waiting for transfers between devices, passed_along(): return lax.ppermute(value, axis, pairs)  221 us
    psum x1, waiting for transfers between devices, per_device(): lax.psum((part_a_query, part_b_query, part_a_key, part_b_key, part_a_valu...  132 us
    unnamed x136, local copies, waits for them, and re-layouts  44.6 us
    dot_general x16, matrix products, head_terms(): jnp.dot(queries, keys.T, preferred_element_type=jnp.float32) * scale  24.3 us
    dot_general x16, matrix products, head_terms(): output = jnp.dot(rounded, values, preferred_element_type=jnp.float32)  22.7 us
    dot_general x16, matrix products, head_terms(): dweights = jnp.dot(grads, values.T, preferred_element_type=jnp.float32)  21.5 us
    dot_general x16, matrix products, head_terms(): jnp.dot(dscores, keys, preferred_element_type=jnp.float32)  21.3 us
  transfers between devices with their start and end apart: 106, of which 43 were waited for; matrix products, arithmetic and copies ran while one was open for 15% of the time, Pallas kernels for 0%

commit v1 on v0

v1 whole, which is shorter than its diff:
```python
import functools
import math

import jax
import jax.numpy as jnp
from jax import lax
from jax.experimental import pallas as pl
from jax.experimental.pallas import tpu as pltpu
from jax.sharding import PartitionSpec as P

SHIFT_HEADS = 16
HEAD_WIDTH = 128
ADAPTER_RANK = 8
GROUP = 2048

HALF_HEADS = SHIFT_HEADS // 2
HALF_COLUMNS = HALF_HEADS * HEAD_WIDTH
SCALE = HEAD_WIDTH ** (-0.5)
LOG2E = math.log2(math.e)
MASKED = -1e30
F32 = jnp.float32
BF16 = jnp.bfloat16
NT = (((1,), (1,)), ((), ()))
BLOCK = 256
VMEM_LIMIT = 56 * 1024 * 1024


def dot(a, b):
    return jnp.dot(a, b, preferred_element_type=F32)


def dot_nt(a, b):
    return lax.dot_general(a, b, NT, preferred_element_type=F32)


def whole():
    return pl.BlockSpec(memory_space=pltpu.VMEM)


def scalars():
    return pl.BlockSpec(memory_space=pltpu.SMEM)


def call(kernel, out_shape, inputs, scratch=(), flops=0, moved=0, exps=0):
    return pl.pallas_call(
        kernel,
        out_shape=out_shape,
        in_specs=[scalars() if i == 0 else whole() for i in range(len(inputs))],
        out_specs=jax.tree.map(lambda _: whole(), out_shape),
        scratch_shapes=list(scratch),
        compiler_params=pltpu.CompilerParams(vmem_limit_bytes=VMEM_LIMIT),
        cost_estimate=pl.CostEstimate(flops=flops, bytes_accessed=moved, transcendentals=exps),
    )(*inputs)


def head_columns(ref, head):
    return ref[:, pl.ds(pl.multiple_of(head * HEAD_WIDTH, HEAD_WIDTH), HEAD_WIDTH)]


def tokens_first(rows):
    pad = jnp.zeros((HEAD_WIDTH - rows.shape[0], rows.shape[1]), F32)
    return jnp.transpose(jnp.concatenate([rows, pad], axis=0))


def pack_kernel(info, x, pog, q, k, v, f, qd, kd, vd, ou, od, out, cross):
    tok = x.shape[0]
    down = jnp.concatenate([qd[...], kd[...], vd[...]], axis=0)
    low = dot_nt(down, x[...])
    low_out = dot_nt(ou[...], pog[...])
    low = jnp.concatenate([low, low_out], axis=0)
    low_b = low.astype(BF16)
    by_token = tokens_first(low_b.astype(F32)).astype(BF16)[:, :32]
    up = jnp.concatenate([jnp.zeros((24, od.shape[1]), BF16), od[...]], axis=0)
    grads = (f[...].astype(F32) + dot(by_token, up)).astype(BF16)
    low_kv = low_b.astype(F32)[8:24].astype(BF16)
    odd = info[0] == 1

    def pick(array, j, first):
        plain = array[:, j * HEAD_WIDTH:(j + 1) * HEAD_WIDTH]
        moved = array[:, HALF_COLUMNS + j * HEAD_WIDTH:HALF_COLUMNS + (j + 1) * HEAD_WIDTH]
        return jnp.where(odd, moved, plain) if first else jnp.where(odd, plain, moved)

    for j in range(HALF_HEADS):
        for i, first in enumerate((True, False)):
            for a, array in enumerate((q, k, v, grads)):
                piece = pick(array, j, first)
                out[j, (4 * i + a) * tok:(4 * i + a + 1) * tok, :] = piece
                if first and a in (1, 2):
                    cross[j, (a - 1) * tok:a * tok, :] = piece
        out[j, 8 * tok:8 * tok + 32, :] = low_b
        cross[j, 2 * tok:2 * tok + 16, :] = low_kv


def attend(head, base, prev, r1, r2, qu, ku, vu, od, kext, vext, sums, emit_terms, emit_head):
    peers = r1.shape[0]
    tok = HEAD_WIDTH
    length = peers * tok
    lead = length if prev else 0
    low = []
    for p in range(peers):
        rows = r1[p, 8 * tok:8 * tok + 32, :]
        low.append(rows)
        t = tokens_first(rows.astype(F32)).astype(BF16)
        at = lead + p * tok
        kext[at:at + tok, :tok] = r1[p, (base + 1) * tok:(base + 2) * tok, :]
        vext[at:at + tok, :tok] = r1[p, (base + 2) * tok:(base + 3) * tok, :]
        kext[at:at + tok, tok:] = t
        vext[at:at + tok, tok:] = t
        if prev:
            at = p * tok
            kext[at:at + tok, :tok] = r2[p, :tok, :]
            vext[at:at + tok, :tok] = r2[p, tok:2 * tok, :]
            rows = r2[p, 2 * tok:2 * tok + 16, :].astype(F32)
            t = tokens_first(jnp.concatenate([jnp.zeros((8, tok), F32), rows], axis=0)).astype(BF16)
            kext[at:at + tok, tok:] = t
            vext[at:at + tok, tok:] = t
    low = jnp.concatenate(low, axis=1).astype(F32)
    low_q = low[0:8].astype(BF16)
    low_o = low[24:32].astype(BF16)
    up_q = head_columns(qu, head)
    up_k = head_columns(ku, head)
    up_v = head_columns(vu, head)
    down = head_columns(od, head)
    total = lead + length
    sums[...] = jnp.zeros_like(sums)
    bq = jnp.zeros((8, HEAD_WIDTH), F32)
    bk, bv, ao = bq, bq, bq
    factor = SCALE * LOG2E
    rows_of = lax.broadcasted_iota(jnp.int32, (BLOCK, BLOCK), 0)
    columns_of = lax.broadcasted_iota(jnp.int32, (BLOCK, BLOCK), 1)
    causal = columns_of <= rows_of
    per = BLOCK // tok
    for b in range(length // BLOCK):
        def block(a):
            return jnp.concatenate(
                [r1[p, (base + a) * tok:(base + a + 1) * tok, :] for p in range(b * per, (b + 1) * per)], axis=0)
        qb, gb = block(0), block(3)
        past = lead + b * BLOCK
        reach = past + BLOCK
        scores = dot_nt(qb, kext[:reach, :tok])
        diagonal = jnp.where(causal, scores[:, past:], MASKED)
        scores = jnp.concatenate([scores[:, :past], diagonal], axis=1) if past else diagonal
        summit = jnp.max(scores, axis=1, keepdims=True)
        e = jnp.exp2((scores - summit) * factor)
        inv = 1.0 / jnp.sum(e, axis=1, keepdims=True)
        p = e.astype(BF16)
        mixed = dot(p, vext[:reach, :])
        output = mixed[:, :tok] * inv
        delta = jnp.sum(gb.astype(F32) * output, axis=1, keepdims=True)
        dweights = dot_nt(gb, vext[:reach, :tok])
        ds = (e * (dweights - delta)).astype(BF16)
        dmixed = dot(ds, kext[:reach, :])
        row_scale = inv * SCALE
        dq = (dmixed[:, :tok] * row_scale).astype(BF16)
        qs = (qb.astype(F32) * row_scale).astype(BF16)
        gs = (gb.astype(F32) * inv).astype(BF16)
        ob = output.astype(BF16)
        sums[0:8, :reach] += dot(dot_nt(up_k, qs).astype(BF16), ds)
        sums[8:16, :reach] += dot(dot_nt(up_v, gs).astype(BF16), p)
        bk += dot(jnp.transpose(dmixed[:, tok:])[8:16].astype(BF16), qs)
        bv += dot(jnp.transpose(mixed[:, tok:])[16:24].astype(BF16), gs)
        bq += dot(low_q[:, b * BLOCK:(b + 1) * BLOCK], dq)
        ao += dot(low_o[:, b * BLOCK:(b + 1) * BLOCK], ob)
        low_dq = dot_nt(up_q, dq)
        out_red = dot_nt(down, ob)
        for i in range(per):
            emit_terms(b * per + i, 0, low_dq[:, i * tok:(i + 1) * tok])
            emit_terms(b * per + i, 8, out_red[:, i * tok:(i + 1) * tok])
    for p in range(peers):
        at = lead + p * tok
        emit_terms(p, 16, sums[:, at:at + tok])
        if prev:
            emit_terms(p, 32, sums[:, p * tok:(p + 1) * tok])
    emit_head(jnp.concatenate([bq, bk, bv, ao], axis=0))


def first_kernel(info, r1, qu, ku, vu, od, terms, head, kext, vext, sums):
    def emit_terms(p, row, value):
        terms[p, row:row + value.shape[0], :] = value

    def emit_head(value):
        head[...] = value

    attend(info[1], 0, False, r1, None, qu, ku, vu, od, kext, vext, sums, emit_terms, emit_head)


def second_kernel(info, r1, r2, qu, ku, vu, od, first_terms, terms, head, kext, vext, sums):
    def emit_terms(p, row, value):
        if row < 32:
            value = value + first_terms[p, row:row + value.shape[0], :]
        terms[p, row:row + value.shape[0], :] = value

    def emit_head(value):
        head[...] = value

    attend(info[2], 4, True, r1, r2, qu, ku, vu, od, kext, vext, sums, emit_terms, emit_head)


def product_kernel(direct, info, terms, back, x, pog, head_f, head_s, *outs):
    own = jnp.sum(terms[:, :32, :], axis=0)
    mixed = own[16:32] + back[...]
    left = jnp.concatenate([own[0:8], mixed], axis=0).astype(BF16)
    right = own[8:16].astype(BF16)
    wide = x.shape[1] // HEAD_WIDTH
    odd = info[0] == 1
    f, s = head_f[...], head_s[...]
    head = jnp.concatenate([jnp.where(odd, s, f), jnp.where(odd, f, s)], axis=0).astype(BF16)
    slot = info[3]
    step = 4
    for c in range(0, wide, step):
        columns = slice(c * HEAD_WIDTH, (c + step) * HEAD_WIDTH)
        a = jnp.concatenate([dot(left, x[:, columns]), dot(right, pog[:, columns])], axis=0).astype(BF16)
        for i in range(step):
            outs[0][c + i, :32, :] = a[:, i * HEAD_WIDTH:(i + 1) * HEAD_WIDTH]
    if direct:
        share = 64 // (wide // HALF_HEADS)
        outs[0][:, 32:, :] = jnp.zeros((wide, share, HEAD_WIDTH), BF16)
        for i in range(wide // HALF_HEADS):
            outs[0][slot * (wide // HALF_HEADS) + i, 32:, :] = head[i * share:(i + 1) * share]
    else:
        outs[1][...] = jnp.zeros(outs[1].shape, BF16)
        outs[1][slot] = head


def share_kernel(info, parts, out):
    summed = jnp.sum(parts[...].astype(F32), axis=0).astype(BF16)
    out[...] = jnp.broadcast_to(summed[None], out.shape)


def finish_kernel(info, main, *refs):
    if len(refs) == 9:
        heads, outs = refs[0], refs[1:]
    else:
        heads, outs = None, refs
    wide = outs[0].shape[1] // HEAD_WIDTH
    per = wide // HALF_HEADS
    for c in range(wide):
        rows = main[c].astype(F32)
        for i, o in enumerate((0, 2, 4, 7)):
            outs[o][:, c * HEAD_WIDTH:(c + 1) * HEAD_WIDTH] = rows[8 * i:8 * i + 8]
    for j in range(HALF_HEADS):
        if heads is None:
            rows = jnp.concatenate([main[j * per + i, 32:, :] for i in range(per)], axis=0).astype(F32)
        else:
            rows = heads[j].astype(F32)
        for half in range(2):
            at = (j + half * HALF_HEADS) * HEAD_WIDTH
            for i, o in enumerate((1, 3, 5, 6)):
                outs[o][:, at:at + HEAD_WIDTH] = rows[32 * half + 8 * i:32 * half + 8 * i + 8]


def per_device(
    devices,
    normed_input,
    projection_output_gradient,
    query,
    key,
    value,
    frozen_output_gradient,
    query_down_weight,
    query_up_weight,
    key_down_weight,
    key_up_weight,
    value_down_weight,
    value_up_weight,
    output_down_weight,
    output_up_weight,
):
    x = normed_input[0]
    pog = projection_output_gradient[0]
    tok, width = x.shape
    peers = GROUP // 2 // tok
    count = lax.axis_size("ctx")
    groups = [list(range(s, s + peers)) for s in range(0, count, peers)]
    my_index = lax.axis_index("ctx")
    odd = (my_index // peers) % 2
    slot = my_index % peers
    info = jnp.stack([odd, slot + HALF_HEADS * odd, slot + HALF_HEADS * (1 - odd), slot]).astype(jnp.int32)
    down_t = output_down_weight.T
    ahead = [(s, (s + peers) % count) for s in range(count)]
    behind = [(t, s) for s, t in ahead]

    def swap(array):
        return lax.all_to_all(array, "ctx", 0, 0, axis_index_groups=groups)

    payload, cross = call(
        pack_kernel,
        (
            jax.ShapeDtypeStruct((peers, 8 * tok + 32, HEAD_WIDTH), BF16),
            jax.ShapeDtypeStruct((peers, 2 * tok + 16, HEAD_WIDTH), BF16),
        ),
        (info, x, pog, query[0], key[0], value[0], frozen_output_gradient[0], query_down_weight.T,
         key_down_weight.T, value_down_weight.T, output_up_weight, down_t),
        flops=2 * 40 * tok * width,
        moved=7 << 20,
    )
    cross = lax.ppermute(cross, "ctx", ahead)
    r1 = swap(payload)
    r2 = swap(cross)
    length = peers * tok
    ups = (query_up_weight, key_up_weight, value_up_weight, down_t)

    def scratch(keys):
        return (
            pltpu.VMEM((keys, 2 * HEAD_WIDTH), BF16),
            pltpu.VMEM((keys, 2 * HEAD_WIDTH), BF16),
            pltpu.VMEM((16, keys), F32),
        )

    pairs = length * length
    first_terms, head_f = call(
        first_kernel,
        (
            jax.ShapeDtypeStruct((peers, 32, HEAD_WIDTH), F32),
            jax.ShapeDtypeStruct((32, HEAD_WIDTH), F32),
        ),
        (info, r1) + ups,
        scratch(length),
        flops=pairs * 6 * 256,
        moved=3 << 20,
        exps=pairs // 2,
    )
    terms, head_s = call(
        second_kernel,
        (
            jax.ShapeDtypeStruct((peers, 48, HEAD_WIDTH), F32),
            jax.ShapeDtypeStruct((32, HEAD_WIDTH), F32),
        ),
        (info, r1, r2) + ups + (first_terms,),
        scratch(2 * length),
        flops=3 * pairs * 6 * 256,
        moved=3 << 20,
        exps=3 * pairs // 2,
    )
    terms = swap(terms)
    back = lax.ppermute(jnp.sum(terms[:, 32:, :], axis=0), "ctx", behind)
    wide = width // HEAD_WIDTH
    share = HALF_HEADS * 64 // devices
    direct = devices == wide and share % 16 == 0
    if direct:
        shapes = (jax.ShapeDtypeStruct((wide, 32 + share, HEAD_WIDTH), BF16),)
    else:
        shapes = (
            jax.ShapeDtypeStruct((wide, 32, HEAD_WIDTH), BF16),
            jax.ShapeDtypeStruct((HALF_HEADS, 64, HEAD_WIDTH), BF16),
        )
    parts = call(
        functools.partial(product_kernel, direct),
        shapes,
        (info, terms, back, x, pog, head_f, head_s),
        flops=2 * 32 * tok * width,
        moved=3 << 20,
    )
    rows = [wide * 32 // devices, share]
    if direct:
        parts = parts[0]
    else:
        parts = jnp.concatenate(
            [part.reshape(devices, n, HEAD_WIDTH) for part, n in zip(parts, rows)], axis=1)
    parts = lax.all_to_all(parts, ("ctx", "dp"), 0, 0)
    shared = call(
        share_kernel,
        jax.ShapeDtypeStruct(parts.shape, BF16),
        (info, parts),
        moved=1 << 20,
    )
    gathered = lax.all_to_all(shared, ("ctx", "dp"), 0, 0)
    if direct:
        gathered = (gathered,)
    else:
        gathered = (
            gathered[:, :rows[0]].reshape(wide, 32, HEAD_WIDTH),
            gathered[:, rows[0]:].reshape(HALF_HEADS, 64, HEAD_WIDTH),
        )
    narrow = SHIFT_HEADS * HEAD_WIDTH
    columns = (width, narrow, width, narrow, width, narrow, narrow, width)
    outs = call(
        finish_kernel,
        tuple(jax.ShapeDtypeStruct((ADAPTER_RANK, n), F32) for n in columns),
        (info,) + gathered,
        moved=2 << 20,
    )
    return tuple(out.T if i in (0, 2, 4, 6) else out for i, out in enumerate(outs))


def solution(mesh):
    placed = (P("dp", "ctx", None),) * 6 + (P(),) * 8
    return jax.shard_map(
        functools.partial(per_device, mesh.size),
        mesh=mesh,
        in_specs=placed,
        out_specs=(P(),) * 8,
        check_vma=False,
    )
```

time: 937 us -> 134 us (0.14)
  waiting for transfers between devices: 353 us -> 40.9 us
  starting transfers between devices: 281 us -> 17.6 us
  matrix products: 155 us -> 0 us
  local copies, waits for them, and re-layouts: 102 us -> 1.42 us
  blocking collectives: 0 us -> 42.9 us
  Pallas kernels: 0 us -> 28.9 us
  between operations: 14.8 us -> 0.7 us
  other arithmetic: 13.3 us -> 0.68 us
  loops' own time: 11.3 us -> 0 us
    ppermute x105 -> x2, starting transfers between devices: 281 us -> 2.73 us  [the longest x1 2.66 us: per_device(): cross = lax.ppermute(cross, 'ctx', ahead)]
    ppermute x105 -> x2, waiting for transfers between devices: 221 us -> 37.3 us  [the longest x1 32.7 us: per_device(): cross = lax.ppermute(cross, 'ctx', ahead)]
    dot_general x138 -> x0, matrix products: 155 us -> none  [the longest x16 24.3 us: head_terms(): jnp.dot(queries, keys.T, preferred_element_type=jnp.float32) * scale]
    psum x1 -> x0, waiting for transfers between devices: 132 us -> none  [per_device(): lax.psum((part_a_query, part_b_query, part_a_key, part_b_key, part_a_valu...]
    unnamed x136 -> x10, local copies, waits for them, and re-layouts: 44.6 us -> 1.42 us
    all_to_all x0 -> x3, blocking collectives: none -> 42.9 us  [the longest x1 16.5 us: per_device(): parts = lax.all_to_all(parts, ('ctx', 'dp'), 0, 0)]
    pallas_call x0 -> x6, Pallas kernels: none -> 28.9 us  [call(): pl.pallas_call(kernel, out_shape=out_shape, in_specs=[scalars() if i == 0...]
    dynamic_slice x48 -> x0, local copies, waits for them, and re-layouts: 28.9 us -> none  [the longest x16 14.8 us: attend_half(): lax.map(per_head, jnp.arange(heads_here, dtype=jnp.int32))]
  transfers between devices with their start and end apart: 106 -> 4, of which waited for: 43 -> 4; matrix products, arithmetic and copies ran while one was open for 15% -> 0% of each run, Pallas kernels for 0% -> 5%
where the time goes in v1:
time: 134 us; the launch traced here: 133 us
  blocking collectives  42.9 us (32%)
  waiting for transfers between devices  40.9 us (31%)
  Pallas kernels  28.9 us (22%)
  starting transfers between devices  17.6 us (13%)
  local copies, waits for them, and re-layouts  1.42 us (1%)
    ppermute x1, waiting for transfers between devices, per_device(): cross = lax.ppermute(cross, 'ctx', ahead)  32.7 us
    pallas_call x6, Pallas kernels, call(): pl.pallas_call(kernel, out_shape=out_shape, in_specs=[scalars() if i == 0...  28.9 us
    all_to_all x1, blocking collectives, per_device(): parts = lax.all_to_all(parts, ('ctx', 'dp'), 0, 0)  16.5 us
    all_to_all x1, blocking collectives, per_device(): gathered = lax.all_to_all(shared, ('ctx', 'dp'), 0, 0)  16.5 us
    all_to_all x2, starting transfers between devices, swap(): return lax.all_to_all(array, 'ctx', 0, 0, axis_index_groups=groups)  14.8 us
    all_to_all x1, blocking collectives, swap(): return lax.all_to_all(array, 'ctx', 0, 0, axis_index_groups=groups)  9.92 us
    ppermute x1, waiting for transfers between devices, per_device(): back = lax.ppermute(jnp.sum(terms[:, 32:, :], axis=0), 'ctx', behind)  4.54 us
    all_to_all x2, waiting for transfers between devices, swap(): return lax.all_to_all(array, 'ctx', 0, 0, axis_index_groups=groups)  3.59 us
  transfers between devices with their start and end apart: 4, of which 4 were waited for; matrix products, arithmetic and copies ran while one was open for 0% of the time, Pallas kernels for 5%

profile of v1, /device:TPU:0, one launch (start us, length us, event | category | flops | bytes accessed | tf_op | source)
XLA Modules:
  0.0 133.0 jit_solution(2436890195279927467)
XLA Ops:
  0.7 0.7 pad_add_fusion.info
  1.3 5.3 %shard_map.197 = (bf16[8,1056,128]{2,1,0:T(8,128)(2,1)}, bf16[8,272,128]{2,1,0:T(8,128)(2,1)}) custom-call(s32[4]{0:T(128)} %pad_add_fusion.info, bf16[128,4096]{1,0:T(8,128)(2,1)} %bitcast.18, bf16[128,4096]{1,0:T(8,128)(2,1)} %bitcast.20, bf16[128,2048]{1,0:T(8,128)(2,1)} %bitcast.22, bf16[128,2048]{1,0:T(8,128)(2,1)} %bitcast.23, ...), custom_call_target="tpu_custom_call" | custom-call | flops 41943040 | bytes 7340032 | tf_op jit(solution)/shard_map/pallas_call | solution.py:45
  6.7 0.0 copy-start.4
  6.7 6.3 %all-to-all-start = ((bf16[8,1056,128]{2,1,0:T(8,128)(2,1)}), bf16[8,1056,128]{2,1,0:T(8,128)(2,1)S(1)}, u32[]{:S(2)}, u32[]{:S(2)}) async-start(bf16[8,1056,128]{2,1,0:T(8,128)(2,1)} %get-tuple-element.22), calls=%async_computation | async-start | bytes 4325376 | tf_op jit(solution)/shard_map/all_to_all | solution.py:284
  13.0 0.0 copy-done.4
  13.0 2.7 %collective-permute-start = (bf16[8,272,128]{2,1,0:T(8,128)(2,1)S(1)}, bf16[8,272,128]{2,1,0:T(8,128)(2,1)}, u32[]{:S(2)}, u32[]{:S(2)}) collective-permute-start(bf16[8,272,128]{2,1,0:T(8,128)(2,1)S(1)} %copy-done.4), channel_id=1, source_target_pairs={{0,16},{2,18},{4,20},{6,22},{8,24},{10,26},{12,28},{14,30},{16,0},... | collective-permute-start | bytes 1671176 | tf_op jit(solution)/shard_map/ppermute | solution.py:297
  15.6 32.7 %collective-permute-done = bf16[8,272,128]{2,1,0:T(8,128)(2,1)} collective-permute-done((bf16[8,272,128]{2,1,0:T(8,128)(2,1)S(1)}, bf16[8,272,128]{2,1,0:T(8,128)(2,1)}, u32[]{:S(2)}, u32[]{:S(2)}) %collective-permute-start) | collective-permute-done | bytes 557088 | tf_op jit(solution)/shard_map/ppermute | solution.py:297
  48.4 2.1 %all-to-all-done.r1 = bf16[8,1056,128]{2,1,0:T(8,128)(2,1)S(1)} async-done(((bf16[8,1056,128]{2,1,0:T(8,128)(2,1)}), bf16[8,1056,128]{2,1,0:T(8,128)(2,1)S(1)}, u32[]{:S(2)}, u32[]{:S(2)}) %all-to-all-start) | async-done | bytes 2162720 | tf_op jit(solution)/shard_map/all_to_all | solution.py:284
  50.4 0.0 copy-start
  50.4 8.5 %all-to-all-start.1 = ((bf16[8,272,128]{2,1,0:T(8,128)(2,1)}), bf16[8,272,128]{2,1,0:T(8,128)(2,1)S(1)}, u32[]{:S(2)}, u32[]{:S(2)}) async-start(bf16[8,272,128]{2,1,0:T(8,128)(2,1)} %collective-permute-done), calls=%async_computation.1 | async-start | bytes 1114112 | tf_op jit(solution)/shard_map/all_to_all | solution.py:284
  59.0 0.0 copy-done
  59.0 6.7 %shard_map.198 = (f32[8,32,128]{2,1,0:T(8,128)}, f32[32,128]{1,0:T(8,128)}) custom-call(s32[4]{0:T(128)} %pad_add_fusion.info, bf16[8,1056,128]{2,1,0:T(8,128)(2,1)} %copy-done, bf16[8,2048]{1,0:T(8,128)(2,1)} %qu.3, bf16[8,2048]{1,0:T(8,128)(2,1)} %ku.3, bf16[8,2048]{1,0:T(8,128)(2,1)} %vu.3, bf16[8,2048]{1,0:T(8,128)(2,1)} %bitcast.30), custom_call_target="tpu_custom_call" | custom-call | flops 1610612736 | bytes 3145728 | tf_op jit(solution)/shard_map/pallas_call | solution.py:45
  65.7 1.5 %all-to-all-done.1.r2 = bf16[8,272,128]{2,1,0:T(8,128)(2,1)S(1)} async-done(((bf16[8,272,128]{2,1,0:T(8,128)(2,1)}), bf16[8,272,128]{2,1,0:T(8,128)(2,1)S(1)}, u32[]{:S(2)}, u32[]{:S(2)}) %all-to-all-start.1) | async-done | bytes 557088 | tf_op jit(solution)/shard_map/all_to_all | solution.py:284
  67.2 0.0 copy-start.2
  67.2 0.8 copy-done.2
  68.0 10.4 %shard_map.199 = (f32[8,48,128]{2,1,0:T(8,128)}, f32[32,128]{1,0:T(8,128)}) custom-call(s32[4]{0:T(128)} %pad_add_fusion.info, bf16[8,1056,128]{2,1,0:T(8,128)(2,1)} %copy-done, bf16[8,272,128]{2,1,0:T(8,128)(2,1)} %copy-done.2, bf16[8,2048]{1,0:T(8,128)(2,1)} %qu.3, bf16[8,2048]{1,0:T(8,128)(2,1)} %ku.3, bf16[8,2048]{1,0:T(8,128)(2,1)} %vu.3, ...), custom_call_target="tpu_custom_call" | custom-call | flops 4831838208 | bytes 3145728 | tf_op jit(solution)/shard_map/pallas_call | solution.py:45
  78.4 9.9 %all_to_all.25.terms = f32[8,48,128]{2,1,0:T(8,128)S(1)} all-to-all(f32[8,48,128]{2,1,0:T(8,128)} %get-tuple-element.25), channel_id=1, replica_groups={{0,2,4,6,8,10,12,14},{16,18,20,22,24,26,28,30},{1,3,5,7,9,11,13,15},{17..., dimensions={0} | all-to-all | bytes 393216 | tf_op jit(solution)/shard_map/all_to_all | solution.py:284
  88.3 0.0 copy-start.1
  88.4 0.1 collective-permute-start.1
  88.4 4.5 %collective-permute-done.1.back = f32[16,128]{1,0:T(8,128)S(1)} collective-permute-done((f32[16,128]{1,0:T(8,128)S(1)}, f32[16,128]{1,0:T(8,128)S(1)}, u32[]{:S(2)}, u32[]{:S(2)}) %collective-permute-start.1) | collective-permute-done | bytes 8224 | tf_op jit(solution)/shard_map/ppermute | solution.py:336
  93.0 0.0 copy-start.3
  93.0 0.0 copy-done.1
  93.0 0.6 copy-done.3
  93.6 2.8 %shard_map.200 = bf16[32,48,128]{2,1,0:T(8,128)(2,1)} custom-call(s32[4]{0:T(128)} %pad_add_fusion.info, f32[8,48,128]{2,1,0:T(8,128)} %copy-done.1, f32[16,128]{1,0:T(8,128)} %copy-done.3, bf16[128,4096]{1,0:T(8,128)(2,1)} %bitcast.19, bf16[128,4096]{1,0:T(8,128)(2,1)} %bitcast.21, f32[32,128]{1,0:T(8,128)} %get-tuple-element.26.head_f, ...), custom_call_target="tpu_custom_call" | custom-call | flops 33554432 | bytes 3145728 | tf_op jit(solution)/shard_map/pallas_call | solution.py:45
  96.3 16.5 %all_to_all.26.parts = bf16[32,48,128]{2,1,0:T(8,128)(2,1)} all-to-all(bf16[32,48,128]{2,1,0:T(8,128)(2,1)} %shard_map.200), channel_id=1, replica_groups=mesh['ctx'=16,'dp'=2] {'ctx','dp'}, dimensions={0} | all-to-all | bytes 786432 | tf_op jit(solution)/shard_map/all_to_all | solution.py:360
  112.8 1.8 %shard_map.201 = bf16[32,48,128]{2,1,0:T(8,128)(2,1)} custom-call(s32[4]{0:T(128)} %pad_add_fusion.info, bf16[32,48,128]{2,1,0:T(8,128)(2,1)} %all_to_all.26.parts), custom_call_target="tpu_custom_call" | custom-call | bytes 1048576 | tf_op jit(solution)/shard_map/pallas_call | solution.py:45
  114.6 16.5 %all_to_all.27.main = bf16[32,48,128]{2,1,0:T(8,128)(2,1)} all-to-all(bf16[32,48,128]{2,1,0:T(8,128)(2,1)} %shard_map.201), channel_id=1, replica_groups=mesh['ctx'=16,'dp'=2] {'ctx','dp'}, dimensions={0} | all-to-all | bytes 786432 | tf_op jit(solution)/shard_map/all_to_all | solution.py:367
  131.1 1.9 %shard_map.202 = (f32[8,4096]{1,0:T(8,128)}, f32[8,2048]{1,0:T(8,128)}, f32[8,4096]{1,0:T(8,128)}, f32[8,2048]{1,0:T(8,128)}, f32[8,4096]{1,0:T(8,128)}, /*index...) custom-call(s32[4]{0:T(128)} %pad_add_fusion.info, bf16[32,48,128]{2,1,0:T(8,128)(2,1)} %all_to_all.27.main), custom_call_target="tpu_custom_call" | custom-call | bytes 2097152 | tf_op jit(solution)/shard_map/pallas_call | solution.py:45
  (1 shorter events, 0.0 us)
Async XLA Ops:
  6.7 6.3 %copy-start.4 = (bf16[8,272,128]{2,1,0:T(8,128)(2,1)S(1)}, bf16[8,272,128]{2,1,0:T(8,128)(2,1)}, u32[]{:S(2)}) copy-start(bf16[8,272,128]{2,1,0:T(8,128)(2,1)} %get-tuple-element.23) | copy-start | bytes 1671172
  6.7 43.8 %all-to-all-start = ((bf16[8,1056,128]{2,1,0:T(8,128)(2,1)}), bf16[8,1056,128]{2,1,0:T(8,128)(2,1)S(1)}, u32[]{:S(2)}, u32[]{:S(2)}) async-start(bf16[8,1056,128]{2,1,0:T(8,128)(2,1)} %get-tuple-element.22), calls=%async_computation | async-start | bytes 4325376 | tf_op jit(solution)/shard_map/all_to_all | solution.py:284
  13.0 35.4 %collective-permute-start = (bf16[8,272,128]{2,1,0:T(8,128)(2,1)S(1)}, bf16[8,272,128]{2,1,0:T(8,128)(2,1)}, u32[]{:S(2)}, u32[]{:S(2)}) collective-permute-start(bf16[8,272,128]{2,1,0:T(8,128)(2,1)S(1)} %copy-done.4), channel_id=1, source_target_pairs={{0,16},{2,18},{4,20},{6,22},{8,24},{10,26},{12,28},{14,30},{16,0},... | collective-permute-start | bytes 1671176 | tf_op jit(solution)/shard_map/ppermute | solution.py:297
  50.4 8.5 %copy-start = (bf16[8,1056,128]{2,1,0:T(8,128)(2,1)}, bf16[8,1056,128]{2,1,0:T(8,128)(2,1)S(1)}, u32[]{:S(2)}) copy-start(bf16[8,1056,128]{2,1,0:T(8,128)(2,1)S(1)} %all-to-all-done.r1) | copy-start | bytes 6488068
  50.4 16.7 %all-to-all-start.1 = ((bf16[8,272,128]{2,1,0:T(8,128)(2,1)}), bf16[8,272,128]{2,1,0:T(8,128)(2,1)S(1)}, u32[]{:S(2)}, u32[]{:S(2)}) async-start(bf16[8,272,128]{2,1,0:T(8,128)(2,1)} %collective-permute-done), calls=%async_computation.1 | async-start | bytes 1114112 | tf_op jit(solution)/shard_map/all_to_all | solution.py:284
  67.2 0.8 copy-start.2
  88.3 4.6 %copy-start.1 = (f32[8,48,128]{2,1,0:T(8,128)}, f32[8,48,128]{2,1,0:T(8,128)S(1)}, u32[]{:S(2)}) copy-start(f32[8,48,128]{2,1,0:T(8,128)S(1)} %all_to_all.25.terms) | copy-start | bytes 589828
  88.4 4.6 %collective-permute-start.1 = (f32[16,128]{1,0:T(8,128)S(1)}, f32[16,128]{1,0:T(8,128)S(1)}, u32[]{:S(2)}, u32[]{:S(2)}) collective-permute-start(f32[16,128]{1,0:T(8,128)S(1)} %slice_reduce_fusion), channel_id=1, source_target_pairs={{16,0},{18,2},{20,4},{22,6},{24,8},{26,10},{28,12},{30,14},{0,16},... | collective-permute-start | bytes 24584 | tf_op jit(solution)/shard_map/ppermute | solution.py:336
  93.0 0.6 copy-start.3

commit v2 on v1

--- a/solution.py
+++ b/solution.py
@@ -62,61 +62,88 @@
     return jnp.transpose(jnp.concatenate([rows, pad], axis=0))
 
 
-def pack_kernel(info, x, pog, q, k, v, f, qd, kd, vd, ou, od, out, cross):
+def pack_first_kernel(info, x, pog, q, k, v, f, qd, kd, vd, ou, od, out, grads_low):
     tok = x.shape[0]
     down = jnp.concatenate([qd[...], kd[...], vd[...]], axis=0)
     low = dot_nt(down, x[...])
     low_out = dot_nt(ou[...], pog[...])
-    low = jnp.concatenate([low, low_out], axis=0)
+    low = jnp.concatenate([low[0:8], low_out, low[8:24]], axis=0)
     low_b = low.astype(BF16)
-    by_token = tokens_first(low_b.astype(F32)).astype(BF16)[:, :32]
-    up = jnp.concatenate([jnp.zeros((24, od.shape[1]), BF16), od[...]], axis=0)
-    grads = (f[...].astype(F32) + dot(by_token, up)).astype(BF16)
-    low_kv = low_b.astype(F32)[8:24].astype(BF16)
-    odd = info[0] == 1
-
-    def pick(array, j, first):
-        plain = array[:, j * HEAD_WIDTH:(j + 1) * HEAD_WIDTH]
-        moved = array[:, HALF_COLUMNS + j * HEAD_WIDTH:HALF_COLUMNS + (j + 1) * HEAD_WIDTH]
-        return jnp.where(odd, moved, plain) if first else jnp.where(odd, plain, moved)
-
+    by_token = tokens_first(low_b.astype(F32)).astype(BF16)
+    grads_low[...] = by_token
+    pack_heads(by_token, q, k, v, f, od, out, 2 * tok + 32)
     for j in range(HALF_HEADS):
-        for i, first in enumerate((True, False)):
-            for a, array in enumerate((q, k, v, grads)):
-                piece = pick(array, j, first)
-                out[j, (4 * i + a) * tok:(4 * i + a + 1) * tok, :] = piece
-                if first and a in (1, 2):
-                    cross[j, (a - 1) * tok:a * tok, :] = piece
-        out[j, 8 * tok:8 * tok + 32, :] = low_b
-        cross[j, 2 * tok:2 * tok + 16, :] = low_kv
-
-
-def attend(head, base, prev, r1, r2, qu, ku, vu, od, kext, vext, sums, emit_terms, emit_head):
+        out[j, 2 * tok:2 * tok + 32, :] = low_b
+
+
+def pack_second_kernel(info, by_token, q, k, v, f, od, out):
+    pack_heads(by_token[...], q, k, v, f, od, out, 2 * q.shape[0])
+
+
+def pack_heads(by_token, q, k, v, f, od, out, keys_at):
+    tok = q.shape[0]
+    width = od.shape[1]
+    up = jnp.concatenate([jnp.zeros((8, width), BF16), od[...], jnp.zeros((16, width), BF16)], axis=0)
+    grads = (f[...].astype(F32) + dot(by_token[:, :32], up)).astype(BF16)
+    for j in range(HALF_HEADS):
+        columns = slice(j * HEAD_WIDTH, (j + 1) * HEAD_WIDTH)
+        out[j, :tok, :] = q[:, columns]
+        out[j, tok:2 * tok, :] = grads[:, columns]
+        out[j, keys_at:keys_at + tok, :] = k[:, columns]
+        out[j, keys_at + tok:keys_at + 2 * tok, :] = v[:, columns]
+
+
+def call_on_half(kernel, second, out_shape, info, inputs, halved, moved):
+    def spec(i, array):
+        if i in halved:
+            block = (array.shape[0], HALF_COLUMNS)
+            if second:
+                return pl.BlockSpec(block, lambda _, s: (0, 1 - s[0]))
+            return pl.BlockSpec(block, lambda _, s: (0, s[0]))
+        return pl.BlockSpec(array.shape, lambda _, s: (0, 0))
+
+    return pl.pallas_call(
+        kernel,
+        out_shape=out_shape,
+        grid_spec=pltpu.PrefetchScalarGridSpec(
+            num_scalar_prefetch=1,
+            grid=(1,),
+            in_specs=[spec(i, array) for i, array in enumerate(inputs)],
+            out_specs=jax.tree.map(
+                lambda o: pl.BlockSpec(o.shape, lambda _, s, n=len(o.shape): (0,) * n), out_shape),
+        ),
+        compiler_params=pltpu.CompilerParams(vmem_limit_bytes=VMEM_LIMIT),
+        cost_estimate=pl.CostEstimate(flops=1 << 28, bytes_accessed=moved, transcendentals=0),
+    )(info, *inputs)
+
+
+def attend(head, r1, keys_at, low_rows, cross, qu, ku, vu, od, kext, vext, sums, emit_terms, emit_head):
+    prev = cross is not None
     peers = r1.shape[0]
     tok = HEAD_WIDTH
     length = peers * tok
     lead = length if prev else 0
     low = []
     for p in range(peers):
-        rows = r1[p, 8 * tok:8 * tok + 32, :]
+        rows = low_rows(p)
         low.append(rows)
         t = tokens_first(rows.astype(F32)).astype(BF16)
         at = lead + p * tok
-        kext[at:at + tok, :tok] = r1[p, (base + 1) * tok:(base + 2) * tok, :]
-        vext[at:at + tok, :tok] = r1[p, (base + 2) * tok:(base + 3) * tok, :]
+        kext[at:at + tok, :tok] = r1[p, keys_at:keys_at + tok, :]
+        vext[at:at + tok, :tok] = r1[p, keys_at + tok:keys_at + 2 * tok, :]
         kext[at:at + tok, tok:] = t
         vext[at:at + tok, tok:] = t
         if prev:
             at = p * tok
-            kext[at:at + tok, :tok] = r2[p, :tok, :]
-            vext[at:at + tok, :tok] = r2[p, tok:2 * tok, :]
-            rows = r2[p, 2 * tok:2 * tok + 16, :].astype(F32)
-            t = tokens_first(jnp.concatenate([jnp.zeros((8, tok), F32), rows], axis=0)).astype(BF16)
+            kext[at:at + tok, :tok] = cross[p, 16:16 + tok, :]
+            vext[at:at + tok, :tok] = cross[p, 16 + tok:16 + 2 * tok, :]
+            rows = cross[p, :16, :].astype(F32)
+            t = tokens_first(jnp.concatenate([jnp.zeros((16, tok), F32), rows], axis=0)).astype(BF16)
             kext[at:at + tok, tok:] = t
             vext[at:at + tok, tok:] = t
     low = jnp.concatenate(low, axis=1).astype(F32)
     low_q = low[0:8].astype(BF16)
-    low_o = low[24:32].astype(BF16)
+    low_o = low[8:16].astype(BF16)
     up_q = head_columns(qu, head)
     up_k = head_columns(ku, head)
     up_v = head_columns(vu, head)
@@ -133,8 +160,8 @@
     for b in range(length // BLOCK):
         def block(a):
             return jnp.concatenate(
-                [r1[p, (base + a) * tok:(base + a + 1) * tok, :] for p in range(b * per, (b + 1) * per)], axis=0)
-        qb, gb = block(0), block(3)
+                [r1[p, a * tok:(a + 1) * tok, :] for p in range(b * per, (b + 1) * per)], axis=0)
+        qb, gb = block(0), block(1)
         past = lead + b * BLOCK
         reach = past + BLOCK
         scores = dot_nt(qb, kext[:reach, :tok])
@@ -157,8 +184,8 @@
         ob = output.astype(BF16)
         sums[0:8, :reach] += dot(dot_nt(up_k, qs).astype(BF16), ds)
         sums[8:16, :reach] += dot(dot_nt(up_v, gs).astype(BF16), p)
-        bk += dot(jnp.transpose(dmixed[:, tok:])[8:16].astype(BF16), qs)
-        bv += dot(jnp.transpose(mixed[:, tok:])[16:24].astype(BF16), gs)
+        bk += dot(jnp.transpose(dmixed[:, tok:])[16:24].astype(BF16), qs)
+        bv += dot(jnp.transpose(mixed[:, tok:])[24:32].astype(BF16), gs)
         bq += dot(low_q[:, b * BLOCK:(b + 1) * BLOCK], dq)
         ao += dot(low_o[:, b * BLOCK:(b + 1) * BLOCK], ob)
         low_dq = dot_nt(up_q, dq)
@@ -174,31 +201,53 @@
     emit_head(jnp.concatenate([bq, bk, bv, ao], axis=0))
 
 
-def first_kernel(info, r1, qu, ku, vu, od, terms, head, kext, vext, sums):
+def first_kernel(info, r1, qu, ku, vu, od, terms, head, low, kext, vext, sums):
     def emit_terms(p, row, value):
         terms[p, row:row + value.shape[0], :] = value
 
     def emit_head(value):
         head[...] = value
 
-    attend(info[1], 0, False, r1, None, qu, ku, vu, od, kext, vext, sums, emit_terms, emit_head)
-
-
-def second_kernel(info, r1, r2, qu, ku, vu, od, first_terms, terms, head, kext, vext, sums):
+    def low_rows(p):
+        rows = r1[p, 2 * HEAD_WIDTH:2 * HEAD_WIDTH + 32, :]
+        low[p] = rows
+        return rows
+
+    attend(info[1], r1, 2 * HEAD_WIDTH + 32, low_rows, None, qu, ku, vu, od, kext, vext, sums, emit_terms, emit_head)
+
+
+def second_kernel(near, info, r1, low, cross, qu, ku, vu, od, first_terms, terms, head, kext, vext, sums):
+    peers = r1.shape[0]
+    if near:
+        own = info[0] * peers
+        other = peers - own
+        for p in range(peers):
+            terms[other + p, :16, :] = jnp.zeros((16, HEAD_WIDTH), F32)
+
     def emit_terms(p, row, value):
+        rows = value.shape[0]
         if row < 32:
-            value = value + first_terms[p, row:row + value.shape[0], :]
-        terms[p, row:row + value.shape[0], :] = value
+            value = value + first_terms[p, row:row + rows, :]
+        if not near:
+            terms[p, row:row + rows, :] = value
+        elif row < 32:
+            terms[own + p, row:row + rows, :] = value
+        else:
+            terms[other + p, row - 16:row - 16 + rows, :] = value
 
     def emit_head(value):
         head[...] = value
 
-    attend(info[2], 4, True, r1, r2, qu, ku, vu, od, kext, vext, sums, emit_terms, emit_head)
-
-
-def product_kernel(direct, info, terms, back, x, pog, head_f, head_s, *outs):
+    attend(info[2], r1, 2 * HEAD_WIDTH, lambda p: low[p], cross, qu, ku, vu, od, kext, vext, sums, emit_terms, emit_head)
+
+
+def product_kernel(direct, near, info, terms, *refs):
     own = jnp.sum(terms[:, :32, :], axis=0)
-    mixed = own[16:32] + back[...]
+    mixed = own[16:32]
+    if not near:
+        mixed = mixed + refs[0][...]
+        refs = refs[1:]
+    x, pog, head_f, head_s, *outs = refs
     left = jnp.concatenate([own[0:8], mixed], axis=0).astype(BF16)
     right = own[8:16].astype(BF16)
     wide = x.shape[1] // HEAD_WIDTH
@@ -227,22 +276,31 @@
     out[...] = jnp.broadcast_to(summed[None], out.shape)
 
 
-def finish_kernel(info, main, *refs):
-    if len(refs) == 9:
-        heads, outs = refs[0], refs[1:]
-    else:
-        heads, outs = None, refs
+def finish_kernel(kind, info, *refs):
+    outs = refs[-8:]
+    refs = refs[:-8]
     wide = outs[0].shape[1] // HEAD_WIDTH
     per = wide // HALF_HEADS
+    zero = info[4] == 0
+
+    def chunk(c):
+        if kind == "paired":
+            mine, other = refs[0][c // 2], refs[1][c // 2]
+            return jnp.where(zero, mine, other) if c % 2 == 0 else jnp.where(zero, other, mine)
+        return refs[0][c]
+
+    head = []
     for c in range(wide):
-        rows = main[c].astype(F32)
+        rows = chunk(c).astype(F32)
         for i, o in enumerate((0, 2, 4, 7)):
             outs[o][:, c * HEAD_WIDTH:(c + 1) * HEAD_WIDTH] = rows[8 * i:8 * i + 8]
+        if kind != "parts":
+            head.append(rows[32:])
     for j in range(HALF_HEADS):
-        if heads is None:
-            rows = jnp.concatenate([main[j * per + i, 32:, :] for i in range(per)], axis=0).astype(F32)
+        if kind == "parts":
+            rows = refs[1][j].astype(F32)
         else:
-            rows = heads[j].astype(F32)
+            rows = jnp.concatenate(head[j * per:(j + 1) * per], axis=0)
         for half in range(2):
             at = (j + half * HALF_HEADS) * HEAD_WIDTH
             for i, o in enumerate((1, 3, 5, 6)):
@@ -275,28 +333,42 @@
     my_index = lax.axis_index("ctx")
     odd = (my_index // peers) % 2
     slot = my_index % peers
-    info = jnp.stack([odd, slot + HALF_HEADS * odd, slot + HALF_HEADS * (1 - odd), slot]).astype(jnp.int32)
+    info = jnp.stack(
+        [odd, slot + HALF_HEADS * odd, slot + HALF_HEADS * (1 - odd), slot, lax.axis_index("dp")]).astype(jnp.int32)
     down_t = output_down_weight.T
     ahead = [(s, (s + peers) % count) for s in range(count)]
     behind = [(t, s) for s, t in ahead]
+    near = count == 2 * peers
 
     def swap(array):
         return lax.all_to_all(array, "ctx", 0, 0, axis_index_groups=groups)
 
-    payload, cross = call(
-        pack_kernel,
+    by_head = (query[0], key[0], value[0], frozen_output_gradient[0])
+    payload, by_token = call_on_half(
+        pack_first_kernel,
+        False,
         (
-            jax.ShapeDtypeStruct((peers, 8 * tok + 32, HEAD_WIDTH), BF16),
-            jax.ShapeDtypeStruct((peers, 2 * tok + 16, HEAD_WIDTH), BF16),
+            jax.ShapeDtypeStruct((peers, 4 * tok + 32, HEAD_WIDTH), BF16),
+            jax.ShapeDtypeStruct((tok, HEAD_WIDTH), BF16),
         ),
-        (info, x, pog, query[0], key[0], value[0], frozen_output_gradient[0], query_down_weight.T,
-         key_down_weight.T, value_down_weight.T, output_up_weight, down_t),
-        flops=2 * 40 * tok * width,
-        moved=7 << 20,
-    )
-    cross = lax.ppermute(cross, "ctx", ahead)
+        info,
+        (x, pog) + by_head
+        + (query_down_weight.T, key_down_weight.T, value_down_weight.T, output_up_weight, down_t),
+        (2, 3, 4, 5, 10),
+        5 << 20,
+    )
+    second = call_on_half(
+        pack_second_kernel,
+        True,
+        jax.ShapeDtypeStruct((peers, 4 * tok, HEAD_WIDTH), BF16),
+        info,
+        (by_token,) + by_head + (down_t,),
+        (1, 2, 3, 4, 5),
+        2 << 20,
+    )
     r1 = swap(payload)
-    r2 = swap(cross)
+    cross = lax.ppermute(r1[:, 2 * tok + 16:, :], "ctx", ahead)
+    r2 = swap(second)
     length = peers * tok
     ups = (query_up_weight, key_up_weight, value_up_weight, down_t)
 
@@ -308,11 +380,12 @@
         )
 
     pairs = length * length
-    first_terms, head_f = call(
+    first_terms, head_f, low = call(
         first_kernel,
         (
             jax.ShapeDtypeStruct((peers, 32, HEAD_WIDTH), F32),
             jax.ShapeDtypeStruct((32, HEAD_WIDTH), F32),
+            jax.ShapeDtypeStruct((peers, 32, HEAD_WIDTH), BF16),
         ),
         (info, r1) + ups,
         scratch(length),
@@ -321,19 +394,23 @@
         exps=pairs // 2,
     )
     terms, head_s = call(
-        second_kernel,
+        functools.partial(second_kernel, near),
         (
-            jax.ShapeDtypeStruct((peers, 48, HEAD_WIDTH), F32),
+            jax.ShapeDtypeStruct((count, 32, HEAD_WIDTH) if near else (peers, 48, HEAD_WIDTH), F32),
             jax.ShapeDtypeStruct((32, HEAD_WIDTH), F32),
         ),
-        (info, r1, r2) + ups + (first_terms,),
+        (info, r2, low, cross) + ups + (first_terms,),
         scratch(2 * length),
         flops=3 * pairs * 6 * 256,
         moved=3 << 20,
         exps=3 * pairs // 2,
     )
-    terms = swap(terms)
-    back = lax.ppermute(jnp.sum(terms[:, 32:, :], axis=0), "ctx", behind)
+    if near:
+        back = ()
+        terms = lax.all_to_all(terms, "ctx", 0, 0)
+    else:
+        terms = swap(terms)
+        back = (lax.ppermute(jnp.sum(terms[:, 32:, :], axis=0), "ctx", behind),)
     wide = width // HEAD_WIDTH
     share = HALF_HEADS * 64 // devices
     direct = devices == wide and share % 16 == 0
@@ -345,9 +422,9 @@
             jax.ShapeDtypeStruct((HALF_HEADS, 64, HEAD_WIDTH), BF16),
         )
     parts = call(
-        functools.partial(product_kernel, direct),
+        functools.partial(product_kernel, direct, near),
         shapes,
-        (info, terms, back, x, pog, head_f, head_s),
+        (info, terms) + back + (x, pog, head_f, head_s),
         flops=2 * 32 * tok * width,
         moved=3 << 20,
     )
@@ -358,24 +435,28 @@
         parts = jnp.concatenate(
             [part.reshape(devices, n, HEAD_WIDTH) for part, n in zip(parts, rows)], axis=1)
     parts = lax.all_to_all(parts, ("ctx", "dp"), 0, 0)
+    paired = direct and lax.axis_size("dp") == 2
     shared = call(
         share_kernel,
-        jax.ShapeDtypeStruct(parts.shape, BF16),
+        jax.ShapeDtypeStruct((count if paired else devices,) + parts.shape[1:], BF16),
         (info, parts),
         moved=1 << 20,
     )
-    gathered = lax.all_to_all(shared, ("ctx", "dp"), 0, 0)
-    if direct:
-        gathered = (gathered,)
+    if paired:
+        mine = lax.all_to_all(shared, "ctx", 0, 0)
+        gathered = (mine, lax.ppermute(mine, "dp", [(0, 1), (1, 0)]))
     else:
+        gathered = (lax.all_to_all(shared, ("ctx", "dp"), 0, 0),)
+    if not direct:
         gathered = (
-            gathered[:, :rows[0]].reshape(wide, 32, HEAD_WIDTH),
-            gathered[:, rows[0]:].reshape(HALF_HEADS, 64, HEAD_WIDTH),
+            gathered[0][:, :rows[0]].reshape(wide, 32, HEAD_WIDTH),
+            gathered[0][:, rows[0]:].reshape(HALF_HEADS, 64, HEAD_WIDTH),
         )
+    kind = "paired" if paired else "whole" if direct else "parts"
     narrow = SHIFT_HEADS * HEAD_WIDTH
     columns = (width, narrow, width, narrow, width, narrow, narrow, width)
     outs = call(
-        finish_kernel,
+        functools.partial(finish_kernel, kind),
         tuple(jax.ShapeDtypeStruct((ADAPTER_RANK, n), F32) for n in columns),
         (info,) + gathered,
         moved=2 << 20,

time: 134 us -> 122 us (0.910)
  waiting for transfers between devices: 40.9 us -> 30.4 us
  starting transfers between devices: 17.6 us -> 12.4 us
  blocking collectives: 42.9 us -> 45.1 us
  Pallas kernels: 28.9 us -> 30.6 us
    ppermute x2, waiting for transfers between devices: 37.3 us -> 1.44 us  [the longest x1 1.44 us: per_device(): gathered = (mine, lax.ppermute(mine, 'dp', [(0, 1), (1, 0)]))]
    all_to_all x2, waiting for transfers between devices: 3.59 us -> 28.9 us  [swap(): return lax.all_to_all(array, 'ctx', 0, 0, axis_index_groups=groups)]
    pallas_call x0 -> x2, Pallas kernels: none -> 7.71 us  [call_on_half(): pl.pallas_call(kernel, out_shape=out_shape, grid_spec=pltpu.PrefetchScala...]
    pallas_call x6 -> x5, Pallas kernels: 28.9 us -> 22.9 us  [call(): pl.pallas_call(kernel, out_shape=out_shape, in_specs=[scalars() if i == 0...]
    all_to_all x2, starting transfers between devices: 14.8 us -> 9.74 us  [swap(): return lax.all_to_all(array, 'ctx', 0, 0, axis_index_groups=groups)]
    all_to_all x2, blocking collectives: 26.4 us -> 28.7 us  [the longest x1 16.5 us: per_device(): terms = lax.all_to_all(terms, 'ctx', 0, 0)]
  transfers between devices with their start and end apart: 4 -> 4, of which waited for: 4 -> 3; matrix products, arithmetic and copies ran while one was open for 0% -> 0% of each run, Pallas kernels for 5% -> 8%
where the time goes in v2:
time: 122 us
  blocking collectives  45.1 us (37%)
  Pallas kernels  30.6 us (25%)
  waiting for transfers between devices  30.4 us (25%)
  starting transfers between devices  12.4 us (10%)
  local copies, waits for them, and re-layouts  2.5 us (2%)
    all_to_all x2, waiting for transfers between devices, swap(): return lax.all_to_all(array, 'ctx', 0, 0, axis_index_groups=groups)  28.9 us
    pallas_call x5, Pallas kernels, call(): pl.pallas_call(kernel, out_shape=out_shape, in_specs=[scalars() if i == 0...  22.9 us
    all_to_all x1, blocking collectives, per_device(): terms = lax.all_to_all(terms, 'ctx', 0, 0)  16.5 us
    all_to_all x1, blocking collectives, per_device(): parts = lax.all_to_all(parts, ('ctx', 'dp'), 0, 0)  16.5 us
    all_to_all x1, blocking collectives, per_device(): mine = lax.all_to_all(shared, 'ctx', 0, 0)  12.2 us
    all_to_all x2, starting transfers between devices, swap(): return lax.all_to_all(array, 'ctx', 0, 0, axis_index_groups=groups)  9.74 us
    pallas_call x2, Pallas kernels, call_on_half(): pl.pallas_call(kernel, out_shape=out_shape, grid_spec=pltpu.PrefetchScala...  7.71 us
    ppermute x1, starting transfers between devices, per_device(): cross = lax.ppermute(r1[:, 2 * tok + 16:, :], 'ctx', ahead)  2.64 us
  transfers between devices with their start and end apart: 4, of which 3 were waited for; matrix products, arithmetic and copies ran while one was open for 0% of the time, Pallas kernels for 8%

profile of v2, /device:TPU:0, one launch (start us, length us, event | category | flops | bytes accessed | tf_op | source)
XLA Modules:
  0.0 121.7 jit_solution(17446012581312163409)
XLA Ops:
  0.7 0.6 stack.23.info
  1.3 4.6 %shard_map.197 = (bf16[8,544,128]{2,1,0:T(8,128)(2,1)}, bf16[128,128]{1,0:T(8,128)(2,1)}) custom-call(s32[5]{0:T(128)} %stack.23.info, bf16[128,4096]{1,0:T(8,128)(2,1)} %bitcast.19, bf16[128,4096]{1,0:T(8,128)(2,1)} %bitcast.21, bf16[128,2048]{1,0:T(8,128)(2,1)} %bitcast.23, bf16[128,2048]{1,0:T(8,128)(2,1)} %bitcast.25, bf16[128,2048]{1,0:T(8,128)(2,1)} %bitcast.27, ...), custom_call_target="tpu_custom_call" | custom-call | flops 268435456 | bytes 5242880 | tf_op jit(solution)/shard_map/pallas_call | solution.py:105
  5.8 6.2 %all-to-all-start.1 = ((bf16[8,544,128]{2,1,0:T(8,128)(2,1)}), bf16[8,544,128]{2,1,0:T(8,128)(2,1)S(1)}, u32[]{:S(2)}, u32[]{:S(2)}) async-start(bf16[8,544,128]{2,1,0:T(8,128)(2,1)} %get-tuple-element.24), calls=%async_computation.1 | async-start | bytes 2228224 | tf_op jit(solution)/shard_map/all_to_all | solution.py:344
  12.0 3.1 %shard_map.198 = bf16[8,512,128]{2,1,0:T(8,128)(2,1)} custom-call(s32[5]{0:T(128)} %stack.23.info, bf16[128,128]{1,0:T(8,128)(2,1)} %get-tuple-element.23.by_token, bf16[128,2048]{1,0:T(8,128)(2,1)} %bitcast.24, bf16[128,2048]{1,0:T(8,128)(2,1)} %bitcast.26, bf16[128,2048]{1,0:T(8,128)(2,1)} %bitcast.28, bf16[128,2048]{1,0:T(8,128)(2,1)} %bitcast.30, ...), custom_call_target="tpu_custom_call" | custom-call | flops 268435456 | bytes 2097152 | tf_op jit(solution)/shard_map/pallas_call | solution.py:105
  15.2 12.3 %all-to-all-done.1.r1 = bf16[8,544,128]{2,1,0:T(8,128)(2,1)S(1)} async-done(((bf16[8,544,128]{2,1,0:T(8,128)(2,1)}), bf16[8,544,128]{2,1,0:T(8,128)(2,1)S(1)}, u32[]{:S(2)}, u32[]{:S(2)}) %all-to-all-start.1) | async-done | bytes 1114144 | tf_op jit(solution)/shard_map/all_to_all | solution.py:344
  27.4 0.0 copy-start
  27.4 3.6 %all-to-all-start = ((bf16[8,512,128]{2,1,0:T(8,128)(2,1)}), bf16[8,512,128]{2,1,0:T(8,128)(2,1)S(1)}, u32[]{:S(2)}, u32[]{:S(2)}) async-start(bf16[8,512,128]{2,1,0:T(8,128)(2,1)} %shard_map.198), calls=%async_computation | async-start | bytes 2097152 | tf_op jit(solution)/shard_map/all_to_all | solution.py:344
  31.0 0.0 copy-done
  31.1 2.6 %collective-permute-start = (bf16[8,272,128]{2,1,0:T(8,128)(2,1)S(1)}, bf16[8,272,128]{2,1,0:T(8,128)(2,1)S(1)}, u32[]{:S(2)}, u32[]{:S(2)}) collective-permute-start(bf16[8,272,128]{2,1,0:T(8,128)(2,1)S(1)} %slice.4), channel_id=1, source_target_pairs={{0,16},{2,18},{4,20},{6,22},{8,24},{10,26},{12,28},{14,30},{16,0},... | collective-permute-start | bytes 1671176 | tf_op jit(solution)/shard_map/ppermute | solution.py:370
  33.7 6.3 %shard_map.199 = (f32[8,32,128]{2,1,0:T(8,128)}, f32[32,128]{1,0:T(8,128)}, bf16[8,32,128]{2,1,0:T(8,128)(2,1)}) custom-call(s32[5]{0:T(128)} %stack.23.info, bf16[8,544,128]{2,1,0:T(8,128)(2,1)} %copy-done, bf16[8,2048]{1,0:T(8,128)(2,1)} %qu.3, bf16[8,2048]{1,0:T(8,128)(2,1)} %ku.3, bf16[8,2048]{1,0:T(8,128)(2,1)} %vu.3, bf16[8,2048]{1,0:T(8,128)(2,1)} %bitcast.33), custom_call_target="tpu_custom_call" | custom-call | flops 1610612736 | bytes 3145728 | tf_op jit(solution)/shard_map/pallas_call | solution.py:45
  40.0 16.6 %all-to-all-done.r1 = bf16[8,512,128]{2,1,0:T(8,128)(2,1)S(1)} async-done(((bf16[8,512,128]{2,1,0:T(8,128)(2,1)}), bf16[8,512,128]{2,1,0:T(8,128)(2,1)S(1)}, u32[]{:S(2)}, u32[]{:S(2)}) %all-to-all-start) | async-done | bytes 1048608 | tf_op jit(solution)/shard_map/all_to_all | solution.py:344
  56.7 0.0 copy-start.1
  56.7 0.0 collective-permute-done.cross
  56.7 0.0 copy-start.4
  56.7 1.0 copy-done.1
  57.7 0.2 copy-done.4
  57.9 10.1 %shard_map.200 = (f32[16,32,128]{2,1,0:T(8,128)}, f32[32,128]{1,0:T(8,128)}) custom-call(s32[5]{0:T(128)} %stack.23.info, bf16[8,512,128]{2,1,0:T(8,128)(2,1)} %copy-done.1, bf16[8,32,128]{2,1,0:T(8,128)(2,1)} %get-tuple-element.25.low, bf16[8,272,128]{2,1,0:T(8,128)(2,1)} %copy-done.4, bf16[8,2048]{1,0:T(8,128)(2,1)} %qu.3, bf16[8,2048]{1,0:T(8,128)(2,1)} %ku.3, ...), custom_call_target="tpu_custom_call" | custom-call | flops 4831838208 | bytes 3145728 | tf_op jit(solution)/shard_map/pallas_call | solution.py:45
  68.0 16.5 %all_to_all.25.terms = f32[16,32,128]{2,1,0:T(8,128)} all-to-all(f32[16,32,128]{2,1,0:T(8,128)} %get-tuple-element.27), channel_id=1, replica_groups=mesh['ctx'=16,'dp'=2] {'ctx'}, dimensions={0} | all-to-all | bytes 524288 | tf_op jit(solution)/shard_map/all_to_all | solution.py:410
  84.5 2.8 %shard_map.201 = bf16[32,48,128]{2,1,0:T(8,128)(2,1)} custom-call(s32[5]{0:T(128)} %stack.23.info, f32[16,32,128]{2,1,0:T(8,128)} %all_to_all.25.terms, bf16[128,4096]{1,0:T(8,128)(2,1)} %bitcast.20, bf16[128,4096]{1,0:T(8,128)(2,1)} %bitcast.22, f32[32,128]{1,0:T(8,128)} %get-tuple-element.28.refs_2_, f32[32,128]{1,0:T(8,128)} %get-tuple-element.29.refs_3_), custom_call_target="tpu_custom_call" | custom-call | flops 33554432 | bytes 3145728 | tf_op jit(solution)/shard_map/pallas_call | solution.py:45
  87.3 16.5 %all_to_all.26.parts = bf16[32,48,128]{2,1,0:T(8,128)(2,1)} all-to-all(bf16[32,48,128]{2,1,0:T(8,128)(2,1)} %shard_map.201), channel_id=1, replica_groups=mesh['ctx'=16,'dp'=2] {'ctx','dp'}, dimensions={0} | all-to-all | bytes 786432 | tf_op jit(solution)/shard_map/all_to_all | solution.py:437
  103.8 1.8 %shard_map.202 = bf16[16,48,128]{2,1,0:T(8,128)(2,1)} custom-call(s32[5]{0:T(128)} %stack.23.info, bf16[32,48,128]{2,1,0:T(8,128)(2,1)} %all_to_all.26.parts), custom_call_target="tpu_custom_call" | custom-call | bytes 1048576 | tf_op jit(solution)/shard_map/pallas_call | solution.py:45
  105.5 12.2 %all_to_all.27.refs_0_ = bf16[16,48,128]{2,1,0:T(8,128)(2,1)S(1)} all-to-all(bf16[16,48,128]{2,1,0:T(8,128)(2,1)} %shard_map.202), channel_id=1, replica_groups=mesh['ctx'=16,'dp'=2] {'ctx'}, dimensions={0} | all-to-all | bytes 393216 | tf_op jit(solution)/shard_map/all_to_all | solution.py:446
  117.7 0.0 copy-start.2
  117.7 0.0 collective-permute-start.1
  117.7 1.4 %collective-permute-done.1.refs_1_ = bf16[16,48,128]{2,1,0:T(8,128)(2,1)S(1)} collective-permute-done((bf16[16,48,128]{2,1,0:T(8,128)(2,1)S(1)}, bf16[16,48,128]{2,1,0:T(8,128)(2,1)S(1)}, u32[]{:S(2)}, u32[]{:S(2)}) %collective-permute-start.1) | collective-permute-done | bytes 196640 | tf_op jit(solution)/shard_map/ppermute | solution.py:447
  119.1 0.0 copy-done.2
  119.1 0.0 copy-start.3
  119.1 0.7 copy-done.3
  119.8 1.9 %shard_map.203 = (f32[8,4096]{1,0:T(8,128)}, f32[8,2048]{1,0:T(8,128)}, f32[8,4096]{1,0:T(8,128)}, f32[8,2048]{1,0:T(8,128)}, f32[8,4096]{1,0:T(8,128)}, /*index...) custom-call(s32[5]{0:T(128)} %stack.23.info, bf16[16,48,128]{2,1,0:T(8,128)(2,1)} %copy-done.2, ...), custom_call_target="tpu_custom_call" | custom-call | bytes 2097152 | tf_op jit(solution)/shard_map/pallas_call | solution.py:45
  (1 shorter events, 0.0 us)
Async XLA Ops:
  5.8 21.6 %all-to-all-start.1 = ((bf16[8,544,128]{2,1,0:T(8,128)(2,1)}), bf16[8,544,128]{2,1,0:T(8,128)(2,1)S(1)}, u32[]{:S(2)}, u32[]{:S(2)}) async-start(bf16[8,544,128]{2,1,0:T(8,128)(2,1)} %get-tuple-element.24), calls=%async_computation.1 | async-start | bytes 2228224 | tf_op jit(solution)/shard_map/all_to_all | solution.py:344
  27.4 3.6 %copy-start = (bf16[8,544,128]{2,1,0:T(8,128)(2,1)}, bf16[8,544,128]{2,1,0:T(8,128)(2,1)S(1)}, u32[]{:S(2)}) copy-start(bf16[8,544,128]{2,1,0:T(8,128)(2,1)S(1)} %all-to-all-done.1.r1) | copy-start | bytes 3342340
  27.4 29.2 %all-to-all-start = ((bf16[8,512,128]{2,1,0:T(8,128)(2,1)}), bf16[8,512,128]{2,1,0:T(8,128)(2,1)S(1)}, u32[]{:S(2)}, u32[]{:S(2)}) async-start(bf16[8,512,128]{2,1,0:T(8,128)(2,1)} %shard_map.198), calls=%async_computation | async-start | bytes 2097152 | tf_op jit(solution)/shard_map/all_to_all | solution.py:344
  31.1 25.6 %collective-permute-start = (bf16[8,272,128]{2,1,0:T(8,128)(2,1)S(1)}, bf16[8,272,128]{2,1,0:T(8,128)(2,1)S(1)}, u32[]{:S(2)}, u32[]{:S(2)}) collective-permute-start(bf16[8,272,128]{2,1,0:T(8,128)(2,1)S(1)} %slice.4), channel_id=1, source_target_pairs={{0,16},{2,18},{4,20},{6,22},{8,24},{10,26},{12,28},{14,30},{16,0},... | collective-permute-start | bytes 1671176 | tf_op jit(solution)/shard_map/ppermute | solution.py:370
  56.7 1.0 copy-start.1
  56.7 1.2 copy-start.4
  117.7 1.4 %copy-start.2 = (bf16[16,48,128]{2,1,0:T(8,128)(2,1)}, bf16[16,48,128]{2,1,0:T(8,128)(2,1)S(1)}, u32[]{:S(2)}) copy-start(bf16[16,48,128]{2,1,0:T(8,128)(2,1)S(1)} %all_to_all.27.refs_0_) | copy-start | bytes 589828
  117.7 1.4 %collective-permute-start.1 = (bf16[16,48,128]{2,1,0:T(8,128)(2,1)S(1)}, bf16[16,48,128]{2,1,0:T(8,128)(2,1)S(1)}, u32[]{:S(2)}, u32[]{:S(2)}) collective-permute-start(bf16[16,48,128]{2,1,0:T(8,128)(2,1)S(1)} %all_to_all.27.refs_0_), channel_id=1, source_target_pairs={{0,1},{1,0},{2,3},{3,2},{4,5},{5,4},{6,7},{7,6},{8,9},{9,8},{10,11... | collective-permute-start | bytes 589832 | tf_op jit(solution)/shard_map/ppermute | solution.py:447
  119.1 0.7 copy-start.3

commit v3 on v2

--- a/solution.py
+++ b/solution.py
@@ -22,7 +22,8 @@
 BF16 = jnp.bfloat16
 NT = (((1,), (1,)), ((), ()))
 BLOCK = 256
-VMEM_LIMIT = 56 * 1024 * 1024
+VMEM_LIMIT = 24 * 1024 * 1024
+VMEM_WHOLE = 56 * 1024 * 1024
 
 
 def dot(a, b):
@@ -71,29 +72,33 @@
     low_b = low.astype(BF16)
     by_token = tokens_first(low_b.astype(F32)).astype(BF16)
     grads_low[...] = by_token
-    pack_heads(by_token, q, k, v, f, od, out, 2 * tok + 32)
-    for j in range(HALF_HEADS):
-        out[j, 2 * tok:2 * tok + 32, :] = low_b
-
-
-def pack_second_kernel(info, by_token, q, k, v, f, od, out):
-    pack_heads(by_token[...], q, k, v, f, od, out, 2 * q.shape[0])
-
-
-def pack_heads(by_token, q, k, v, f, od, out, keys_at):
-    tok = q.shape[0]
-    width = od.shape[1]
-    up = jnp.concatenate([jnp.zeros((8, width), BF16), od[...], jnp.zeros((16, width), BF16)], axis=0)
-    grads = (f[...].astype(F32) + dot(by_token[:, :32], up)).astype(BF16)
+    grads = all_grads(by_token, f, od)
     for j in range(HALF_HEADS):
         columns = slice(j * HEAD_WIDTH, (j + 1) * HEAD_WIDTH)
         out[j, :tok, :] = q[:, columns]
         out[j, tok:2 * tok, :] = grads[:, columns]
-        out[j, keys_at:keys_at + tok, :] = k[:, columns]
-        out[j, keys_at + tok:keys_at + 2 * tok, :] = v[:, columns]
-
-
-def call_on_half(kernel, second, out_shape, info, inputs, halved, moved):
+        out[j, 2 * tok:2 * tok + 32, :] = low_b
+        out[j, 2 * tok + 32:3 * tok + 32, :] = k[:, columns]
+        out[j, 3 * tok + 32:4 * tok + 32, :] = v[:, columns]
+
+
+def pack_second_kernel(info, by_token, q, k, v, f, od, *outs):
+    *outs, grads = outs
+    tok = q.shape[0]
+    grads[...] = all_grads(by_token[...], f, od)
+    for d, out in enumerate(outs):
+        peer = jnp.bitwise_xor(info[3], d)
+        for i, array in enumerate((q, grads, k, v)):
+            out[i * tok:(i + 1) * tok, :] = head_columns(array, peer)
+
+
+def all_grads(by_token, f, od):
+    width = od.shape[1]
+    up = jnp.concatenate([jnp.zeros((8, width), BF16), od[...], jnp.zeros((16, width), BF16)], axis=0)
+    return (f[...].astype(F32) + dot(by_token[:, :32], up)).astype(BF16)
+
+
+def call_on_half(kernel, second, out_shape, info, inputs, halved, moved, scratch=()):
     def spec(i, array):
         if i in halved:
             block = (array.shape[0], HALF_COLUMNS)
@@ -111,17 +116,18 @@
             in_specs=[spec(i, array) for i, array in enumerate(inputs)],
             out_specs=jax.tree.map(
                 lambda o: pl.BlockSpec(o.shape, lambda _, s, n=len(o.shape): (0,) * n), out_shape),
+            scratch_shapes=list(scratch),
         ),
-        compiler_params=pltpu.CompilerParams(vmem_limit_bytes=VMEM_LIMIT),
+        compiler_params=pltpu.CompilerParams(vmem_limit_bytes=VMEM_LIMIT if second else VMEM_WHOLE),
         cost_estimate=pl.CostEstimate(flops=1 << 28, bytes_accessed=moved, transcendentals=0),
     )(info, *inputs)
 
 
-def attend(head, r1, keys_at, low_rows, cross, qu, ku, vu, od, kext, vext, sums, emit_terms, emit_head):
+def attend(head, low_rows, cross, qu, ku, vu, od, queries, grads, kext, vext, sums, emit):
     prev = cross is not None
-    peers = r1.shape[0]
     tok = HEAD_WIDTH
-    length = peers * tok
+    length = queries.shape[0]
+    peers = length // tok
     lead = length if prev else 0
     low = []
     for p in range(peers):
@@ -129,8 +135,6 @@
         low.append(rows)
         t = tokens_first(rows.astype(F32)).astype(BF16)
         at = lead + p * tok
-        kext[at:at + tok, :tok] = r1[p, keys_at:keys_at + tok, :]
-        vext[at:at + tok, :tok] = r1[p, keys_at + tok:keys_at + 2 * tok, :]
         kext[at:at + tok, tok:] = t
         vext[at:at + tok, tok:] = t
         if prev:
@@ -157,11 +161,10 @@
     columns_of = lax.broadcasted_iota(jnp.int32, (BLOCK, BLOCK), 1)
     causal = columns_of <= rows_of
     per = BLOCK // tok
+    pairs = []
     for b in range(length // BLOCK):
-        def block(a):
-            return jnp.concatenate(
-                [r1[p, a * tok:(a + 1) * tok, :] for p in range(b * per, (b + 1) * per)], axis=0)
-        qb, gb = block(0), block(1)
+        qb = queries[b * BLOCK:(b + 1) * BLOCK, :]
+        gb = grads[b * BLOCK:(b + 1) * BLOCK, :]
         past = lead + b * BLOCK
         reach = past + BLOCK
         scores = dot_nt(qb, kext[:reach, :tok])
@@ -190,59 +193,60 @@
         ao += dot(low_o[:, b * BLOCK:(b + 1) * BLOCK], ob)
         low_dq = dot_nt(up_q, dq)
         out_red = dot_nt(down, ob)
-        for i in range(per):
-            emit_terms(b * per + i, 0, low_dq[:, i * tok:(i + 1) * tok])
-            emit_terms(b * per + i, 8, out_red[:, i * tok:(i + 1) * tok])
+        pair = jnp.concatenate([low_dq, out_red], axis=0)
+        pairs += [pair[:, i * tok:(i + 1) * tok] for i in range(per)]
     for p in range(peers):
         at = lead + p * tok
-        emit_terms(p, 16, sums[:, at:at + tok])
-        if prev:
-            emit_terms(p, 32, sums[:, p * tok:(p + 1) * tok])
-    emit_head(jnp.concatenate([bq, bk, bv, ao], axis=0))
-
-
-def first_kernel(info, r1, qu, ku, vu, od, terms, head, low, kext, vext, sums):
-    def emit_terms(p, row, value):
-        terms[p, row:row + value.shape[0], :] = value
-
-    def emit_head(value):
-        head[...] = value
-
-    def low_rows(p):
-        rows = r1[p, 2 * HEAD_WIDTH:2 * HEAD_WIDTH + 32, :]
-        low[p] = rows
-        return rows
-
-    attend(info[1], r1, 2 * HEAD_WIDTH + 32, low_rows, None, qu, ku, vu, od, kext, vext, sums, emit_terms, emit_head)
-
-
-def second_kernel(near, info, r1, low, cross, qu, ku, vu, od, first_terms, terms, head, kext, vext, sums):
-    peers = r1.shape[0]
-    if near:
-        own = info[0] * peers
-        other = peers - own
-        for p in range(peers):
-            terms[other + p, :16, :] = jnp.zeros((16, HEAD_WIDTH), F32)
-
-    def emit_terms(p, row, value):
-        rows = value.shape[0]
-        if row < 32:
-            value = value + first_terms[p, row:row + rows, :]
-        if not near:
-            terms[p, row:row + rows, :] = value
-        elif row < 32:
-            terms[own + p, row:row + rows, :] = value
+        own = jnp.concatenate([pairs[p], sums[:, at:at + tok]], axis=0)
+        emit(p, own, sums[:, p * tok:(p + 1) * tok] if prev else None)
+    return jnp.concatenate([bq, bk, bv, ao], axis=0)
+
+
+def first_kernel(info, r1, qu, ku, vu, od, terms, head, low, queries, grads, kext, vext, sums):
+    tok = HEAD_WIDTH
+    for p in range(r1.shape[0]):
+        at = slice(p * tok, (p + 1) * tok)
+        queries[at, :] = r1[p, :tok, :]
+        grads[at, :] = r1[p, tok:2 * tok, :]
+        low[p] = r1[p, 2 * tok:2 * tok + 32, :]
+        kext[at, :tok] = r1[p, 2 * tok + 32:3 * tok + 32, :]
+        vext[at, :tok] = r1[p, 3 * tok + 32:4 * tok + 32, :]
+
+    def emit(p, own, previous):
+        terms[p] = own
+
+    head[...] = attend(info[1], lambda p: r1[p, 2 * tok:2 * tok + 32, :], None, qu, ku, vu, od,
+                       queries, grads, kext, vext, sums, emit)
+
+
+def second_kernel(near, info, *refs):
+    peers = HALF_HEADS
+    parts, refs = refs[:peers], refs[peers:]
+    low, cross, qu, ku, vu, od, first_terms, terms, head, queries, grads, kext, vext, sums = refs
+    tok = HEAD_WIDTH
+    length = peers * tok
+    for d, part in enumerate(parts):
+        at = pl.multiple_of(jnp.bitwise_xor(info[3], d) * tok, tok)
+        queries[pl.ds(at, tok), :] = part[:tok, :]
+        grads[pl.ds(at, tok), :] = part[tok:2 * tok, :]
+        kext[pl.ds(length + at, tok), :tok] = part[2 * tok:3 * tok, :]
+        vext[pl.ds(length + at, tok), :tok] = part[3 * tok:, :]
+    mine = info[0] * peers
+    other = peers - mine
+
+    def emit(p, own, previous):
+        own = own + first_terms[p]
+        if near:
+            terms[mine + p] = own.astype(BF16)
+            terms[other + p] = jnp.concatenate([jnp.zeros((16, tok), F32), previous], axis=0).astype(BF16)
         else:
-            terms[other + p, row - 16:row - 16 + rows, :] = value
-
-    def emit_head(value):
-        head[...] = value
-
-    attend(info[2], r1, 2 * HEAD_WIDTH, lambda p: low[p], cross, qu, ku, vu, od, kext, vext, sums, emit_terms, emit_head)
+            terms[p] = jnp.concatenate([own, previous], axis=0).astype(BF16)
+
+    head[...] = attend(info[2], lambda p: low[p], cross, qu, ku, vu, od, queries, grads, kext, vext, sums, emit)
 
 
 def product_kernel(direct, near, info, terms, *refs):
-    own = jnp.sum(terms[:, :32, :], axis=0)
+    own = jnp.sum(terms[:, :32, :].astype(F32), axis=0)
     mixed = own[16:32]
     if not near:
         mixed = mixed + refs[0][...]
@@ -360,20 +364,24 @@
     second = call_on_half(
         pack_second_kernel,
         True,
-        jax.ShapeDtypeStruct((peers, 4 * tok, HEAD_WIDTH), BF16),
+        (jax.ShapeDtypeStruct((4 * tok, HEAD_WIDTH), BF16),) * peers,
         info,
         (by_token,) + by_head + (down_t,),
         (1, 2, 3, 4, 5),
         2 << 20,
+        (pltpu.VMEM((tok, HALF_COLUMNS), BF16),),
     )
     r1 = swap(payload)
     cross = lax.ppermute(r1[:, 2 * tok + 16:, :], "ctx", ahead)
-    r2 = swap(second)
+    r2 = second[:1] + tuple(
+        lax.ppermute(second[d], "ctx", [(s, s ^ d) for s in range(count)]) for d in range(1, peers))
     length = peers * tok
     ups = (query_up_weight, key_up_weight, value_up_weight, down_t)
 
     def scratch(keys):
         return (
+            pltpu.VMEM((length, HEAD_WIDTH), BF16),
+            pltpu.VMEM((length, HEAD_WIDTH), BF16),
             pltpu.VMEM((keys, 2 * HEAD_WIDTH), BF16),
             pltpu.VMEM((keys, 2 * HEAD_WIDTH), BF16),
             pltpu.VMEM((16, keys), F32),
@@ -396,10 +404,10 @@
     terms, head_s = call(
         functools.partial(second_kernel, near),
         (
-            jax.ShapeDtypeStruct((count, 32, HEAD_WIDTH) if near else (peers, 48, HEAD_WIDTH), F32),
+            jax.ShapeDtypeStruct((count, 32, HEAD_WIDTH) if near else (peers, 48, HEAD_WIDTH), BF16),
             jax.ShapeDtypeStruct((32, HEAD_WIDTH), F32),
         ),
-        (info, r2, low, cross) + ups + (first_terms,),
+        (info,) + r2 + (low, cross) + ups + (first_terms,),
         scratch(2 * length),
         flops=3 * pairs * 6 * 256,
         moved=3 << 20,
@@ -410,7 +418,7 @@
         terms = lax.all_to_all(terms, "ctx", 0, 0)
     else:
         terms = swap(terms)
-        back = (lax.ppermute(jnp.sum(terms[:, 32:, :], axis=0), "ctx", behind),)
+        back = (lax.ppermute(jnp.sum(terms[:, 32:, :].astype(F32), axis=0), "ctx", behind),)
     wide = width // HEAD_WIDTH
     share = HALF_HEADS * 64 // devices
     direct = devices == wide and share % 16 == 0

time: 122 us -> 111 us (0.910)
  blocking collectives: 45.1 us -> 61.5 us
  waiting for transfers between devices: 30.4 us -> 14.6 us
  Pallas kernels: 30.6 us -> 21.9 us
  local copies, waits for them, and re-layouts: 2.5 us -> 0.69 us
    all_to_all x2 -> x0, waiting for transfers between devices: 28.9 us -> none  [swap(): return lax.all_to_all(array, 'ctx', 0, 0, axis_index_groups=groups)]
    all_to_all x0 -> x1, blocking collectives: none -> 22.3 us  [swap(): return lax.all_to_all(array, 'ctx', 0, 0, axis_index_groups=groups)]
    ppermute x0 -> x7, waiting for transfers between devices: none -> 13.2 us  [per_device(): lax.ppermute(second[d], 'ctx', [(s, s ^ d) for s in range(count)])]
    all_to_all x2 -> x0, starting transfers between devices: 9.74 us -> none  [swap(): return lax.all_to_all(array, 'ctx', 0, 0, axis_index_groups=groups)]
    ppermute x0 -> x7, starting transfers between devices: none -> 8.9 us  [per_device(): lax.ppermute(second[d], 'ctx', [(s, s ^ d) for s in range(count)])]
    pallas_call x5, Pallas kernels: 22.9 us -> 16.4 us  [call(): pl.pallas_call(kernel, out_shape=out_shape, in_specs=[scalars() if i == 0...]
    all_to_all x1, blocking collectives: 16.5 us -> 12.3 us  [per_device(): terms = lax.all_to_all(terms, 'ctx', 0, 0)]
    pallas_call x2, Pallas kernels: 7.71 us -> 5.57 us  [call_on_half(): pl.pallas_call(kernel, out_shape=out_shape, grid_spec=pltpu.PrefetchScala...]
  transfers between devices with their start and end apart: 4 -> 9, of which waited for: 3 -> 6; matrix products, arithmetic and copies ran while one was open for 0% -> 0% of each run, Pallas kernels for 8% -> 5%
where the time goes in v3:
time: 111 us
  blocking collectives  61.5 us (55%)
  Pallas kernels  21.9 us (20%)
  waiting for transfers between devices  14.6 us (13%)
  starting transfers between devices  11.6 us (10%)
    all_to_all x1, blocking collectives, swap(): return lax.all_to_all(array, 'ctx', 0, 0, axis_index_groups=groups)  22.3 us
    pallas_call x5, Pallas kernels, call(): pl.pallas_call(kernel, out_shape=out_shape, in_specs=[scalars() if i == 0...  16.4 us
    all_to_all x1, blocking collectives, per_device(): parts = lax.all_to_all(parts, ('ctx', 'dp'), 0, 0)  14.9 us
    ppermute x7, waiting for transfers between devices, per_device(): lax.ppermute(second[d], 'ctx', [(s, s ^ d) for s in range(count)])  13.2 us
    all_to_all x1, blocking collectives, per_device(): terms = lax.all_to_all(terms, 'ctx', 0, 0)  12.3 us
    all_to_all x1, blocking collectives, per_device(): mine = lax.all_to_all(shared, 'ctx', 0, 0)  12 us
    ppermute x7, starting transfers between devices, per_device(): lax.ppermute(second[d], 'ctx', [(s, s ^ d) for s in range(count)])  8.9 us
    pallas_call x2, Pallas kernels, call_on_half(): pl.pallas_call(kernel, out_shape=out_shape, grid_spec=pltpu.PrefetchScala...  5.57 us
  transfers between devices with their start and end apart: 9, of which 6 were waited for; matrix products, arithmetic and copies ran while one was open for 0% of the time, Pallas kernels for 5%

profile of v3, /device:TPU:0, one launch (start us, length us, event | category | flops | bytes accessed | tf_op | source)
XLA Modules:
  0.0 111.1 jit_solution(6296801073827708463)
XLA Ops:
  0.7 0.6 stack.23.info
  1.3 4.5 %shard_map.197 = (bf16[8,544,128]{2,1,0:T(8,128)(2,1)}, bf16[128,128]{1,0:T(8,128)(2,1)}) custom-call(s32[5]{0:T(128)} %stack.23.info, bf16[128,4096]{1,0:T(8,128)(2,1)} %bitcast.19, bf16[128,4096]{1,0:T(8,128)(2,1)} %bitcast.21, bf16[128,2048]{1,0:T(8,128)(2,1)} %bitcast.23, bf16[128,2048]{1,0:T(8,128)(2,1)} %bitcast.25, bf16[128,2048]{1,0:T(8,128)(2,1)} %bitcast.27, ...), custom_call_target="tpu_custom_call" | custom-call | flops 268435456 | bytes 5242880 | tf_op jit(solution)/shard_map/pallas_call | solution.py:110
  5.8 0.0 copy-start.4
  5.8 0.0 copy-start.5
  5.8 22.3 %all_to_all.20.r1 = bf16[8,544,128]{2,1,0:T(8,128)(2,1)S(1)} all-to-all(bf16[8,544,128]{2,1,0:T(8,128)(2,1)} %get-tuple-element.40), channel_id=1, replica_groups={{0,2,4,6,8,10,12,14},{16,18,20,22,24,26,28,30},{1,3,5,7,9,11,13,15},{17..., dimensions={0} | all-to-all | bytes 2228224 | tf_op jit(solution)/shard_map/all_to_all | solution.py:348
  28.1 0.0 copy-start.2
  28.1 0.0 copy-start.3
  28.2 0.0 copy-start.6
  28.2 0.0 copy-start.7
  28.2 0.0 copy-start.8
  28.2 0.0 copy-start.9
  28.2 0.0 copy-start.10
  28.2 0.0 copy-start.11
  28.3 2.7 %collective-permute-start.7 = (bf16[8,272,128]{2,1,0:T(8,128)(2,1)S(1)}, bf16[8,272,128]{2,1,0:T(8,128)(2,1)S(1)}, u32[]{:S(2)}, u32[]{:S(2)}) collective-permute-start(bf16[8,272,128]{2,1,0:T(8,128)(2,1)S(1)} %slice.4), channel_id=1, source_target_pairs={{0,16},{2,18},{4,20},{6,22},{8,24},{10,26},{12,28},{14,30},{16,0},... | collective-permute-start | bytes 1671176 | tf_op jit(solution)/shard_map/ppermute | solution.py:375
  30.9 0.0 copy-done.4
  30.9 0.0 copy-done.5
  30.9 0.0 copy-done.2
  30.9 0.0 copy-done.3
  30.9 0.0 copy-done.6
  30.9 0.0 copy-done.7
  30.9 0.0 copy-done.8
  31.0 1.0 shard_map.198
  32.0 0.5 collective-permute-start
  32.5 0.7 collective-permute-start.1
  33.3 2.3 %collective-permute-start.2 = (bf16[512,128]{1,0:T(8,128)(2,1)S(1)}, bf16[512,128]{1,0:T(8,128)(2,1)S(1)}, u32[]{:S(2)}, u32[]{:S(2)}) collective-permute-start(bf16[512,128]{1,0:T(8,128)(2,1)S(1)} %get-tuple-element.35), channel_id=1, source_target_pairs={{0,6},{2,4},{4,2},{6,0},{8,14},{10,12},{12,10},{14,8},{16,22},{18,... | collective-permute-start | bytes 393224 | tf_op jit(solution)/shard_map/ppermute | solution.py:377
  35.5 0.6 collective-permute-start.3
  36.2 0.8 collective-permute-done.refs_1_
  37.0 1.7 %collective-permute-start.4 = (bf16[512,128]{1,0:T(8,128)(2,1)S(1)}, bf16[512,128]{1,0:T(8,128)(2,1)S(1)}, u32[]{:S(2)}, u32[]{:S(2)}) collective-permute-start(bf16[512,128]{1,0:T(8,128)(2,1)S(1)} %get-tuple-element.37), channel_id=1, source_target_pairs={{0,10},{2,8},{4,14},{6,12},{8,2},{10,0},{12,6},{14,4},{16,26},{18,... | collective-permute-start | bytes 393224 | tf_op jit(solution)/shard_map/ppermute | solution.py:377
  38.7 0.0 collective-permute-done.1.refs_2_
  38.7 1.1 %collective-permute-start.5 = (bf16[512,128]{1,0:T(8,128)(2,1)S(1)}, bf16[512,128]{1,0:T(8,128)(2,1)S(1)}, u32[]{:S(2)}, u32[]{:S(2)}) collective-permute-start(bf16[512,128]{1,0:T(8,128)(2,1)S(1)} %get-tuple-element.38), channel_id=1, source_target_pairs={{0,12},{2,14},{4,8},{6,10},{8,4},{10,6},{12,0},{14,2},{16,28},{18,... | collective-permute-start | bytes 393224 | tf_op jit(solution)/shard_map/ppermute | solution.py:377
  39.8 0.8 collective-permute-done.2.refs_3_
  40.7 1.9 %collective-permute-start.6 = (bf16[512,128]{1,0:T(8,128)(2,1)S(1)}, bf16[512,128]{1,0:T(8,128)(2,1)S(1)}, u32[]{:S(2)}, u32[]{:S(2)}) collective-permute-start(bf16[512,128]{1,0:T(8,128)(2,1)S(1)} %get-tuple-element.39), channel_id=1, source_target_pairs={{0,14},{2,12},{4,10},{6,8},{8,6},{10,4},{12,2},{14,0},{16,30},{18,... | collective-permute-start | bytes 393224 | tf_op jit(solution)/shard_map/ppermute | solution.py:377
  42.6 0.0 copy-done.9
  42.6 0.0 copy-done.10
  42.6 0.0 copy-done.11
  42.6 4.9 %shard_map.199 = (f32[8,32,128]{2,1,0:T(8,128)S(1)}, f32[32,128]{1,0:T(8,128)S(1)}, bf16[8,32,128]{2,1,0:T(8,128)(2,1)S(1)}) custom-call(s32[5]{0:T(128)S(1)} %copy-done.8, bf16[8,544,128]{2,1,0:T(8,128)(2,1)S(1)} %all_to_all.20.r1, bf16[8,2048]{1,0:T(8,128)(2,1)S(1)} %copy-done.9, bf16[8,2048]{1,0:T(8,128)(2,1)S(1)} %copy-done.10, ...), custom_call_target="tpu_custom_call" | custom-call | flops 1610612736 | bytes 3145728 | tf_op jit(solution)/shard_map/pallas_call | solution.py:46
  47.5 0.0 collective-permute-done.3.refs_4_
  47.5 7.4 %collective-permute-done.4.refs_5_ = bf16[512,128]{1,0:T(8,128)(2,1)S(1)} collective-permute-done((bf16[512,128]{1,0:T(8,128)(2,1)S(1)}, bf16[512,128]{1,0:T(8,128)(2,1)S(1)}, u32[]{:S(2)}, u32[]{:S(2)}) %collective-permute-start.4) | collective-permute-done | bytes 131104 | tf_op jit(solution)/shard_map/ppermute | solution.py:377
  54.9 2.7 %collective-permute-done.5.refs_6_ = bf16[512,128]{1,0:T(8,128)(2,1)S(1)} collective-permute-done((bf16[512,128]{1,0:T(8,128)(2,1)S(1)}, bf16[512,128]{1,0:T(8,128)(2,1)S(1)}, u32[]{:S(2)}, u32[]{:S(2)}) %collective-permute-start.5) | collective-permute-done | bytes 131104 | tf_op jit(solution)/shard_map/ppermute | solution.py:377
  57.6 1.4 %collective-permute-done.6.refs_7_ = bf16[512,128]{1,0:T(8,128)(2,1)S(1)} collective-permute-done((bf16[512,128]{1,0:T(8,128)(2,1)S(1)}, bf16[512,128]{1,0:T(8,128)(2,1)S(1)}, u32[]{:S(2)}, u32[]{:S(2)}) %collective-permute-start.6) | collective-permute-done | bytes 131104 | tf_op jit(solution)/shard_map/ppermute | solution.py:377
  59.0 0.0 collective-permute-done.7.refs_9_
  59.0 0.0 copy-start
  59.0 0.0 copy-start.1
  59.0 8.5 %shard_map.200 = (bf16[16,32,128]{2,1,0:T(8,128)(2,1)S(1)}, f32[32,128]{1,0:T(8,128)S(1)}) custom-call(s32[5]{0:T(128)S(1)} %copy-done.8, bf16[512,128]{1,0:T(8,128)(2,1)S(1)} %get-tuple-element.32.refs_0_, bf16[512,128]{1,0:T(8,128)(2,1)S(1)} %collective-permute-done.refs_1_, bf16[512,128]{1,0:T(8,128)(2,1)S(1)} %collective-permute-done.1.refs_2_, ...), custom_call_target="tpu_custom_call" | custom-call | flops 4831838208 | bytes 3145728 | tf_op jit(solution)/shard_map/pallas_call | solution.py:46
  67.5 12.3 %all_to_all.21.terms = bf16[16,32,128]{2,1,0:T(8,128)(2,1)S(1)} all-to-all(bf16[16,32,128]{2,1,0:T(8,128)(2,1)S(1)} %get-tuple-element.43), channel_id=1, replica_groups=mesh['ctx'=16,'dp'=2] {'ctx'}, dimensions={0} | all-to-all | bytes 262144 | tf_op jit(solution)/shard_map/all_to_all | solution.py:418
  79.8 0.0 copy-done
  79.8 0.0 copy-done.1
  79.8 0.9 shard_map.201
  80.8 14.9 %all_to_all.22.parts = bf16[32,48,128]{2,1,0:T(8,128)(2,1)S(1)} all-to-all(bf16[32,48,128]{2,1,0:T(8,128)(2,1)S(1)} %shard_map.201), channel_id=1, replica_groups=mesh['ctx'=16,'dp'=2] {'ctx','dp'}, dimensions={0} | all-to-all | bytes 786432 | tf_op jit(solution)/shard_map/all_to_all | solution.py:445
  95.7 0.6 shard_map.202
  96.3 12.0 %all_to_all.23.refs_0_ = bf16[16,48,128]{2,1,0:T(8,128)(2,1)S(1)} all-to-all(bf16[16,48,128]{2,1,0:T(8,128)(2,1)S(1)} %shard_map.202), channel_id=1, replica_groups=mesh['ctx'=16,'dp'=2] {'ctx'}, dimensions={0} | all-to-all | bytes 393216 | tf_op jit(solution)/shard_map/all_to_all | solution.py:454
  108.2 0.0 collective-permute-start.8
  108.2 1.4 %collective-permute-done.8.refs_1_ = bf16[16,48,128]{2,1,0:T(8,128)(2,1)S(1)} collective-permute-done((bf16[16,48,128]{2,1,0:T(8,128)(2,1)S(1)}, bf16[16,48,128]{2,1,0:T(8,128)(2,1)S(1)}, u32[]{:S(2)}, u32[]{:S(2)}) %collective-permute-start.8) | collective-permute-done | bytes 196640 | tf_op jit(solution)/shard_map/ppermute | solution.py:455
  109.7 1.4 %shard_map.203 = (f32[8,4096]{1,0:T(8,128)}, f32[8,2048]{1,0:T(8,128)}, f32[8,4096]{1,0:T(8,128)}, f32[8,2048]{1,0:T(8,128)}, f32[8,4096]{1,0:T(8,128)}, /*index...) custom-call(s32[5]{0:T(128)S(1)} %copy-done.8, bf16[16,48,128]{2,1,0:T(8,128)(2,1)S(1)} %all_to_all.23.refs_0_, ...), custom_call_target="tpu_custom_call" | custom-call | bytes 2097152 | tf_op jit(solution)/shard_map/pallas_call | solution.py:46
  (1 shorter events, 0.0 us)
Async XLA Ops:
  5.8 25.1 %copy-start.4 = (bf16[1,128,2048]{2,1,0:T(8,128)(2,1)S(1)}, bf16[1,128,2048]{2,1,0:T(8,128)(2,1)}, u32[]{:S(2)}) copy-start(bf16[1,128,2048]{2,1,0:T(8,128)(2,1)} %param.18) | copy-start | bytes 1572868
  5.8 25.1 %copy-start.5 = (bf16[1,128,2048]{2,1,0:T(8,128)(2,1)S(1)}, bf16[1,128,2048]{2,1,0:T(8,128)(2,1)}, u32[]{:S(2)}) copy-start(bf16[1,128,2048]{2,1,0:T(8,128)(2,1)} %param.19) | copy-start | bytes 1572868
  28.1 2.8 %copy-start.2 = (bf16[1,128,2048]{2,1,0:T(8,128)(2,1)S(1)}, bf16[1,128,2048]{2,1,0:T(8,128)(2,1)}, u32[]{:S(2)}) copy-start(bf16[1,128,2048]{2,1,0:T(8,128)(2,1)} %param.16) | copy-start | bytes 1572868
  28.1 2.8 %copy-start.3 = (bf16[1,128,2048]{2,1,0:T(8,128)(2,1)S(1)}, bf16[1,128,2048]{2,1,0:T(8,128)(2,1)}, u32[]{:S(2)}) copy-start(bf16[1,128,2048]{2,1,0:T(8,128)(2,1)} %param.17) | copy-start | bytes 1572868
  28.2 2.8 %copy-start.6 = (bf16[2048,8]{0,1:T(8,128)(2,1)S(1)}, bf16[2048,8]{0,1:T(8,128)(2,1)}, u32[]{:S(2)}) copy-start(bf16[2048,8]{0,1:T(8,128)(2,1)} %param.26) | copy-start | bytes 98308
  28.2 2.8 %copy-start.7 = (bf16[128,128]{1,0:T(8,128)(2,1)S(1)}, bf16[128,128]{1,0:T(8,128)(2,1)}, u32[]{:S(2)}) copy-start(bf16[128,128]{1,0:T(8,128)(2,1)} %get-tuple-element.31.by_token) | copy-start | bytes 98308
  28.2 2.8 %copy-start.8 = (s32[5]{0:T(128)S(1)}, s32[5]{0:T(128)}, u32[]{:S(2)}) copy-start(s32[5]{0:T(128)} %stack.23.info) | copy-start | bytes 64
  28.2 14.3 %copy-start.9 = (bf16[8,2048]{1,0:T(8,128)(2,1)S(1)}, bf16[8,2048]{1,0:T(8,128)(2,1)}, u32[]{:S(2)}) copy-start(bf16[8,2048]{1,0:T(8,128)(2,1)} %refs_10_.1) | copy-start | bytes 98308
  28.2 14.3 %copy-start.10 = (bf16[8,2048]{1,0:T(8,128)(2,1)S(1)}, bf16[8,2048]{1,0:T(8,128)(2,1)}, u32[]{:S(2)}) copy-start(bf16[8,2048]{1,0:T(8,128)(2,1)} %refs_11_.1) | copy-start | bytes 98308
  28.2 14.3 %copy-start.11 = (bf16[8,2048]{1,0:T(8,128)(2,1)S(1)}, bf16[8,2048]{1,0:T(8,128)(2,1)}, u32[]{:S(2)}) copy-start(bf16[8,2048]{1,0:T(8,128)(2,1)} %refs_12_.1) | copy-start | bytes 98308
  28.3 30.7 %collective-permute-start.7 = (bf16[8,272,128]{2,1,0:T(8,128)(2,1)S(1)}, bf16[8,272,128]{2,1,0:T(8,128)(2,1)S(1)}, u32[]{:S(2)}, u32[]{:S(2)}) collective-permute-start(bf16[8,272,128]{2,1,0:T(8,128)(2,1)S(1)} %slice.4), channel_id=1, source_target_pairs={{0,16},{2,18},{4,20},{6,22},{8,24},{10,26},{12,28},{14,30},{16,0},... | collective-permute-start | bytes 1671176 | tf_op jit(solution)/shard_map/ppermute | solution.py:375
  32.0 5.0 %collective-permute-start = (bf16[512,128]{1,0:T(8,128)(2,1)S(1)}, bf16[512,128]{1,0:T(8,128)(2,1)S(1)}, u32[]{:S(2)}, u32[]{:S(2)}) collective-permute-start(bf16[512,128]{1,0:T(8,128)(2,1)S(1)} %get-tuple-element.33), channel_id=1, source_target_pairs={{0,2},{2,0},{4,6},{6,4},{8,10},{10,8},{12,14},{14,12},{16,18},{18,... | collective-permute-start | bytes 393224 | tf_op jit(solution)/shard_map/ppermute | solution.py:377
  32.5 6.2 %collective-permute-start.1 = (bf16[512,128]{1,0:T(8,128)(2,1)S(1)}, bf16[512,128]{1,0:T(8,128)(2,1)S(1)}, u32[]{:S(2)}, u32[]{:S(2)}) collective-permute-start(bf16[512,128]{1,0:T(8,128)(2,1)S(1)} %get-tuple-element.34), channel_id=1, source_target_pairs={{0,4},{2,6},{4,0},{6,2},{8,12},{10,14},{12,8},{14,10},{16,20},{18,... | collective-permute-start | bytes 393224 | tf_op jit(solution)/shard_map/ppermute | solution.py:377
  33.3 7.4 %collective-permute-start.2 = (bf16[512,128]{1,0:T(8,128)(2,1)S(1)}, bf16[512,128]{1,0:T(8,128)(2,1)S(1)}, u32[]{:S(2)}, u32[]{:S(2)}) collective-permute-start(bf16[512,128]{1,0:T(8,128)(2,1)S(1)} %get-tuple-element.35), channel_id=1, source_target_pairs={{0,6},{2,4},{4,2},{6,0},{8,14},{10,12},{12,10},{14,8},{16,22},{18,... | collective-permute-start | bytes 393224 | tf_op jit(solution)/shard_map/ppermute | solution.py:377
  35.5 11.9 %collective-permute-start.3 = (bf16[512,128]{1,0:T(8,128)(2,1)S(1)}, bf16[512,128]{1,0:T(8,128)(2,1)S(1)}, u32[]{:S(2)}, u32[]{:S(2)}) collective-permute-start(bf16[512,128]{1,0:T(8,128)(2,1)S(1)} %get-tuple-element.36), channel_id=1, source_target_pairs={{0,8},{2,10},{4,12},{6,14},{8,0},{10,2},{12,4},{14,6},{16,24},{18,... | collective-permute-start | bytes 393224 | tf_op jit(solution)/shard_map/ppermute | solution.py:377
  37.0 17.8 %collective-permute-start.4 = (bf16[512,128]{1,0:T(8,128)(2,1)S(1)}, bf16[512,128]{1,0:T(8,128)(2,1)S(1)}, u32[]{:S(2)}, u32[]{:S(2)}) collective-permute-start(bf16[512,128]{1,0:T(8,128)(2,1)S(1)} %get-tuple-element.37), channel_id=1, source_target_pairs={{0,10},{2,8},{4,14},{6,12},{8,2},{10,0},{12,6},{14,4},{16,26},{18,... | collective-permute-start | bytes 393224 | tf_op jit(solution)/shard_map/ppermute | solution.py:377
  38.7 18.9 %collective-permute-start.5 = (bf16[512,128]{1,0:T(8,128)(2,1)S(1)}, bf16[512,128]{1,0:T(8,128)(2,1)S(1)}, u32[]{:S(2)}, u32[]{:S(2)}) collective-permute-start(bf16[512,128]{1,0:T(8,128)(2,1)S(1)} %get-tuple-element.38), channel_id=1, source_target_pairs={{0,12},{2,14},{4,8},{6,10},{8,4},{10,6},{12,0},{14,2},{16,28},{18,... | collective-permute-start | bytes 393224 | tf_op jit(solution)/shard_map/ppermute | solution.py:377
  40.7 18.3 %collective-permute-start.6 = (bf16[512,128]{1,0:T(8,128)(2,1)S(1)}, bf16[512,128]{1,0:T(8,128)(2,1)S(1)}, u32[]{:S(2)}, u32[]{:S(2)}) collective-permute-start(bf16[512,128]{1,0:T(8,128)(2,1)S(1)} %get-tuple-element.39), channel_id=1, source_target_pairs={{0,14},{2,12},{4,10},{6,8},{8,6},{10,4},{12,2},{14,0},{16,30},{18,... | collective-permute-start | bytes 393224 | tf_op jit(solution)/shard_map/ppermute | solution.py:377
  59.0 20.8 %copy-start = (bf16[1,128,4096]{2,1,0:T(8,128)(2,1)S(1)}, bf16[1,128,4096]{2,1,0:T(8,128)(2,1)}, u32[]{:S(2)}) copy-start(bf16[1,128,4096]{2,1,0:T(8,128)(2,1)} %param.14) | copy-start | bytes 3145732
  59.0 20.8 %copy-start.1 = (bf16[1,128,4096]{2,1,0:T(8,128)(2,1)S(1)}, bf16[1,128,4096]{2,1,0:T(8,128)(2,1)}, u32[]{:S(2)}) copy-start(bf16[1,128,4096]{2,1,0:T(8,128)(2,1)} %param.15) | copy-start | bytes 3145732
  108.2 1.4 %collective-permute-start.8 = (bf16[16,48,128]{2,1,0:T(8,128)(2,1)S(1)}, bf16[16,48,128]{2,1,0:T(8,128)(2,1)S(1)}, u32[]{:S(2)}, u32[]{:S(2)}) collective-permute-start(bf16[16,48,128]{2,1,0:T(8,128)(2,1)S(1)} %all_to_all.23.refs_0_), channel_id=1, source_target_pairs={{0,1},{1,0},{2,3},{3,2},{4,5},{5,4},{6,7},{7,6},{8,9},{9,8},{10,11... | collective-permute-start | bytes 589832 | tf_op jit(solution)/shard_map/ppermute | solution.py:455

commit v4 on v3

v4 whole, which is shorter than its diff:
```python
import functools
import math

import jax
import jax.numpy as jnp
from jax import lax
from jax.experimental import pallas as pl
from jax.experimental.pallas import tpu as pltpu
from jax.sharding import PartitionSpec as P

SHIFT_HEADS = 16
HEAD_WIDTH = 128
ADAPTER_RANK = 8
GROUP = 2048

HALF_HEADS = SHIFT_HEADS // 2
HALF_COLUMNS = HALF_HEADS * HEAD_WIDTH
SCALE = HEAD_WIDTH ** (-0.5)
LOG2E = math.log2(math.e)
MASKED = -1e30
F32 = jnp.float32
BF16 = jnp.bfloat16
NT = (((1,), (1,)), ((), ()))
ORDERS = ((0, 1, 2, 4, 3, 5, 6, 7), (0, 2, 4, 1, 6, 3, 5, 7))
BLOCK = 256
VMEM_LIMIT = 24 * 1024 * 1024
VMEM_PACK = 56 * 1024 * 1024


def dot(a, b):
    return jnp.dot(a, b, preferred_element_type=F32)


def dot_nt(a, b):
    return lax.dot_general(a, b, NT, preferred_element_type=F32)


def call(kernel, out_shape, inputs, scratch=(), flops=0, moved=0, exps=0, limit=VMEM_LIMIT, far=0):
    return pl.pallas_call(
        kernel,
        out_shape=out_shape,
        in_specs=[pl.BlockSpec(memory_space=pltpu.HBM if i < far else pltpu.VMEM) for i in range(len(inputs))],
        out_specs=jax.tree.map(lambda _: pl.BlockSpec(memory_space=pltpu.VMEM), out_shape),
        scratch_shapes=list(scratch),
        compiler_params=pltpu.CompilerParams(vmem_limit_bytes=limit),
        cost_estimate=pl.CostEstimate(flops=flops, bytes_accessed=moved, transcendentals=exps),
    )(*inputs)


MIRROR = HALF_HEADS // 2


def place():
    index = lax.axis_index("ctx")
    return lax.rem(lax.div(index, HALF_HEADS), 2), lax.rem(index, HALF_HEADS)


def partners():
    _, slot = place()
    core = lax.rem(lax.axis_index("dp"), 2)
    return [jnp.bitwise_xor(slot, jnp.where(core == 0, a, b)) for a, b in zip(*ORDERS)]


def rows_at(index):
    return pl.ds(pl.multiple_of(index * HEAD_WIDTH, HEAD_WIDTH), HEAD_WIDTH)


def head_columns(ref, head):
    return ref[:, pl.ds(pl.multiple_of(head * HEAD_WIDTH, HEAD_WIDTH), HEAD_WIDTH)]


def tokens_first(rows):
    pad = jnp.zeros((HEAD_WIDTH - rows.shape[0], rows.shape[1]), F32)
    return jnp.transpose(jnp.concatenate([rows, pad], axis=0))


def pack_kernel(q, k, v, x, pog, f, qd, kd, vd, ou, od, *refs):
    outs, bufs, sems = refs[:-12], refs[-12:-1], refs[-1]
    firsts, seconds = outs[:HALF_HEADS], outs[HALF_HEADS:]
    qs, ks, vs, xs, ps, fs, qds, kds, vds, ous, ods = bufs
    odd, _ = place()
    tok, width = x.shape
    chunks = 4
    step = width // chunks
    sources = (q, k, v, x, pog, f, qd, kd, vd, ou, od)
    whole = {i: pltpu.make_async_copy(sources[i], bufs[i], sems.at[i]) for i in (0, 1, 2, 5, 6, 7, 8, 9, 10)}
    wide = []
    for c in range(chunks):
        columns = pl.ds(c * step, step)
        wide.append([pltpu.make_async_copy(sources[i].at[:, columns], bufs[i].at[:, columns], sems.at[11 + (i - 3) * chunks + c])
                     for i in (3, 4)])
    for i in (6, 7, 8, 9):
        whole[i].start()
    for pair in wide[:2]:
        for copy in pair:
            copy.start()
    for i in (0, 1, 2):
        whole[i].start()
    for pair in wide[2:]:
        for copy in pair:
            copy.start()
    for i in (10, 5):
        whole[i].start()
    for i in (6, 7, 8, 9):
        whole[i].wait()
    down = jnp.concatenate([qds[...], kds[...], vds[...]], axis=0)
    low = jnp.zeros((24, tok), F32)
    low_out = jnp.zeros((8, tok), F32)
    peers = partners()
    spots = ((0, 0, 0), (1, 2 * tok + 32, 2 * tok), (2, 3 * tok + 32, 3 * tok))
    for c in range(chunks):
        columns = slice(c * step, (c + 1) * step)
        wide[c][0].wait()
        low += dot_nt(down[:, columns], xs[:, columns])
        wide[c][1].wait()
        low_out += dot_nt(ous[:, columns], ps[:, columns])
        if c > 0:
            i, at, late = spots[c - 1]
            whole[i].wait()
            spread(bufs[i], odd, peers, firsts, at, seconds, late)
    low_b = jnp.concatenate([low[0:8], low_out, low[8:24]], axis=0).astype(BF16)
    by_token = tokens_first(low_b.astype(F32)).astype(BF16)
    columns = od.shape[1]
    whole[10].wait()
    up = jnp.concatenate([jnp.zeros((8, columns), BF16), ods[...], jnp.zeros((16, columns), BF16)], axis=0)
    raised = dot(by_token[:, :32], up)
    whole[5].wait()
    fs[...] = (fs[...].astype(F32) + raised).astype(BF16)
    spread(fs, odd, peers, firsts, tok, seconds, tok)
    for first in firsts:
        first[2 * tok:2 * tok + 32, :] = low_b


def spread(array, odd, peers, firsts, at, seconds, late):
    tok = array.shape[0]
    for peer, first, second in zip(peers, firsts, seconds):
        first[at:at + tok, :] = head_columns(array, peer + HALF_HEADS * odd)
        second[late:late + tok, :] = head_columns(array, second_head(peer) + HALF_HEADS * (1 - odd))


def second_head(peer):
    return jnp.bitwise_xor(peer, MIRROR)


def assemble_kernel(*refs):
    parts, cross = refs[:-1], refs[-1]
    for peer, part in zip(partners(), parts):
        cross[peer] = part[2 * HEAD_WIDTH + 16:, :]


def attend(head, lead, low, qu, ku, vu, od, queries, grads, kext, vext, sums, emit):
    tok = HEAD_WIDTH
    length = queries.shape[0]
    peers = length // tok
    low = [low[p] for p in range(peers)]
    low = jnp.concatenate(low, axis=1).astype(F32)
    low_q = low[0:8].astype(BF16)
    low_o = low[8:16].astype(BF16)
    up_q = head_columns(qu, head)
    up_k = head_columns(ku, head)
    up_v = head_columns(vu, head)
    down = head_columns(od, head)
    total = lead + length
    sums[...] = jnp.zeros_like(sums)
    bq = jnp.zeros((8, HEAD_WIDTH), F32)
    bk, bv, ao = bq, bq, bq
    factor = SCALE * LOG2E
    rows_of = lax.broadcasted_iota(jnp.int32, (BLOCK, BLOCK), 0)
    columns_of = lax.broadcasted_iota(jnp.int32, (BLOCK, BLOCK), 1)
    causal = columns_of <= rows_of
    per = BLOCK // tok
    pairs = []
    for b in range(length // BLOCK):
        qb = queries[b * BLOCK:(b + 1) * BLOCK, :]
        gb = grads[b * BLOCK:(b + 1) * BLOCK, :]
        past = lead + b * BLOCK
        reach = past + BLOCK
        scores = dot_nt(qb, kext[:reach, :tok])
        diagonal = jnp.where(causal, scores[:, past:], MASKED)
        scores = jnp.concatenate([scores[:, :past], diagonal], axis=1) if past else diagonal
        summit = jnp.max(scores, axis=1, keepdims=True)
        e = jnp.exp2((scores - summit) * factor)
        inv = 1.0 / jnp.sum(e, axis=1, keepdims=True)
        p = e.astype(BF16)
        mixed = dot(p, vext[:reach, :])
        output = mixed[:, :tok] * inv
        delta = jnp.sum(gb.astype(F32) * output, axis=1, keepdims=True)
        dweights = dot_nt(gb, vext[:reach, :tok])
        ds = (e * (dweights - delta)).astype(BF16)
        dmixed = dot(ds, kext[:reach, :])
        row_scale = inv * SCALE
        dq = (dmixed[:, :tok] * row_scale).astype(BF16)
        qs = (qb.astype(F32) * row_scale).astype(BF16)
        gs = (gb.astype(F32) * inv).astype(BF16)
        ob = output.astype(BF16)
        sums[0:8, :reach] += dot(dot_nt(up_k, qs).astype(BF16), ds)
        sums[8:16, :reach] += dot(dot_nt(up_v, gs).astype(BF16), p)
        bk += dot(jnp.transpose(dmixed[:, tok:])[16:24].astype(BF16), qs)
        bv += dot(jnp.transpose(mixed[:, tok:])[24:32].astype(BF16), gs)
        bq += dot(low_q[:, b * BLOCK:(b + 1) * BLOCK], dq)
        ao += dot(low_o[:, b * BLOCK:(b + 1) * BLOCK], ob)
        low_dq = dot_nt(up_q, dq)
        out_red = dot_nt(down, ob)
        pair = jnp.concatenate([low_dq, out_red], axis=0)
        pairs += [pair[:, i * tok:(i + 1) * tok] for i in range(per)]
    for p in range(peers):
        at = lead + p * tok
        own = jnp.concatenate([pairs[p], sums[:, at:at + tok]], axis=0)
        emit(p, own, sums[:, p * tok:(p + 1) * tok] if lead else None)
    return jnp.concatenate([bq, bk, bv, ao], axis=0)


def first_kernel(*refs):
    parts, refs = refs[:HALF_HEADS], refs[HALF_HEADS:]
    qu, ku, vu, od, terms, head, low, token_low, queries, grads, kext, vext, sums = refs
    odd, slot = place()
    tok = HEAD_WIDTH
    for peer, part in zip(partners(), parts):
        at = rows_at(peer)
        queries[at, :] = part[:tok, :]
        grads[at, :] = part[tok:2 * tok, :]
        rows = part[2 * tok:2 * tok + 32, :]
        low[peer] = rows
        t = tokens_first(rows.astype(F32)).astype(BF16)
        token_low[at, :] = t
        kext[at, :tok] = part[2 * tok + 32:3 * tok + 32, :]
        vext[at, :tok] = part[3 * tok + 32:, :]
        kext[at, tok:] = t
        vext[at, tok:] = t

    def emit(p, own, previous):
        terms[p] = own

    head[...] = attend(slot + HALF_HEADS * odd, 0, low, qu, ku, vu, od, queries, grads, kext, vext, sums, emit)


def second_kernel(near, *refs):
    parts, refs = refs[:HALF_HEADS], refs[HALF_HEADS:]
    cross, low, token_low, first_terms, head_f, qu, ku, vu, od, terms, heads, queries, grads, kext, vext, sums = refs
    odd, slot = place()
    tok = HEAD_WIDTH
    length = token_low.shape[0]
    for peer, part in zip(partners(), parts):
        at = rows_at(peer)
        late = rows_at(peer + HALF_HEADS)
        queries[at, :] = part[:tok, :]
        grads[at, :] = part[tok:2 * tok, :]
        kext[late, :tok] = part[2 * tok:3 * tok, :]
        vext[late, :tok] = part[3 * tok:, :]
    kext[length:, tok:] = token_low[...]
    vext[length:, tok:] = token_low[...]
    for p in range(HALF_HEADS):
        at = slice(p * tok, (p + 1) * tok)
        rows = jnp.concatenate([jnp.zeros((16, tok), F32), cross[p, :16, :].astype(F32)], axis=0)
        t = tokens_first(rows).astype(BF16)
        kext[at, :tok] = cross[p, 16:16 + tok, :]
        vext[at, :tok] = cross[p, 16 + tok:, :]
        kext[at, tok:] = t
        vext[at, tok:] = t
    mine = odd * HALF_HEADS
    other = HALF_HEADS - mine

    def emit(p, own, previous):
        own = own + first_terms[p]
        if near:
            terms[mine + p] = own.astype(BF16)
            terms[other + p] = jnp.concatenate([jnp.zeros((16, tok), F32), previous], axis=0).astype(BF16)
        else:
            terms[p] = jnp.concatenate([own, previous], axis=0).astype(BF16)

    head_s = attend(second_head(slot) + HALF_HEADS * (1 - odd), length, low, qu, ku, vu, od, queries, grads, kext, vext, sums, emit)
    heads[:32, :] = head_f[...]
    heads[32:, :] = head_s


def product_kernel(direct, near, terms, *refs):
    own = jnp.sum(terms[:, :32, :].astype(F32), axis=0)
    mixed = own[16:32]
    if not near:
        mixed = mixed + refs[0][...]
        refs = refs[1:]
    x, pog, heads, *outs = refs
    left = jnp.concatenate([own[0:8], mixed], axis=0).astype(BF16)
    right = own[8:16].astype(BF16)
    wide = x.shape[1] // HEAD_WIDTH
    head = heads[...].astype(BF16)
    odd, slot = place()
    step = 4
    for c in range(0, wide, step):
        columns = slice(c * HEAD_WIDTH, (c + step) * HEAD_WIDTH)
        a = jnp.concatenate([dot(left, x[:, columns]), dot(right, pog[:, columns])], axis=0).astype(BF16)
        for i in range(step):
            outs[0][c + i, :32, :] = a[:, i * HEAD_WIDTH:(i + 1) * HEAD_WIDTH]
    spots = ((slot, odd), (second_head(slot), 1 - odd))
    if direct:
        per = wide // HALF_HEADS
        share = 64 // per
        outs[0][:, 32:, :] = jnp.zeros((wide, share, HEAD_WIDTH), BF16)
        for i in range(per):
            where, half = spots[2 * i // per]
            outs[0][where * per + half * (per // 2) + i % (per // 2), 32:, :] = head[i * share:(i + 1) * share]
    else:
        outs[1][...] = jnp.zeros(outs[1].shape, BF16)
        for i, (where, half) in enumerate(spots):
            outs[1][where, pl.ds(pl.multiple_of(32 * half, 32), 32), :] = head[32 * i:32 * i + 32]


def share_kernel(parts, out):
    summed = jnp.sum(parts[...].astype(F32), axis=0).astype(BF16)
    out[...] = jnp.broadcast_to(summed[None], out.shape)


def finish_kernel(kind, *refs):
    outs = refs[-8:]
    refs = refs[:-8]
    wide = outs[0].shape[1] // HEAD_WIDTH
    per = wide // HALF_HEADS
    zero = lax.axis_index("dp") == 0

    def chunk(c):
        if kind == "paired":
            mine, other = refs[0][c // 2], refs[1][c // 2]
            return jnp.where(zero, mine, other) if c % 2 == 0 else jnp.where(zero, other, mine)
        return refs[0][c]

    head = []
    for c in range(wide):
        rows = chunk(c).astype(F32)
        for i, o in enumerate((0, 2, 4, 7)):
            outs[o][:, c * HEAD_WIDTH:(c + 1) * HEAD_WIDTH] = rows[8 * i:8 * i + 8]
        if kind != "parts":
            head.append(rows[32:])
    for j in range(HALF_HEADS):
        if kind == "parts":
            rows = refs[1][j].astype(F32)
        else:
            rows = jnp.concatenate(head[j * per:(j + 1) * per], axis=0)
        for half in range(2):
            at = (j + half * HALF_HEADS) * HEAD_WIDTH
            for i, o in enumerate((1, 3, 5, 6)):
                outs[o][:, at:at + HEAD_WIDTH] = rows[32 * half + 8 * i:32 * half + 8 * i + 8]


def per_device(
    devices,
    normed_input,
    projection_output_gradient,
    query,
    key,
    value,
    frozen_output_gradient,
    query_down_weight,
    query_up_weight,
    key_down_weight,
    key_up_weight,
    value_down_weight,
    value_up_weight,
    output_down_weight,
    output_up_weight,
):
    x = normed_input[0]
    pog = projection_output_gradient[0]
    tok, width = x.shape
    peers = GROUP // 2 // tok
    count = lax.axis_size("ctx")
    groups = [list(range(s, s + peers)) for s in range(0, count, peers)]
    down_t = output_down_weight.T
    ahead = [(s, ((s ^ MIRROR) + peers) % count) for s in range(count)]
    behind = [((s + peers) % count, s) for s in range(count)]
    near = count == 2 * peers

    def swap(array):
        return lax.all_to_all(array, "ctx", 0, 0, axis_index_groups=groups)

    cores = lax.axis_size("dp")

    def exchange(parts):
        moved = [parts[0]]
        for k in range(1, peers):
            pairs = [(c * cores + d, (c ^ ORDERS[d % 2][k]) * cores + d) for c in range(count) for d in range(cores)]
            moved.append(lax.ppermute(parts[k], ("ctx", "dp"), pairs))
        return tuple(moved)

    weights = (query_down_weight.T, key_down_weight.T, value_down_weight.T, output_up_weight, down_t)
    sources = (query[0], key[0], value[0], x, pog, frozen_output_gradient[0]) + weights
    packed = call(
        pack_kernel,
        (jax.ShapeDtypeStruct((4 * tok + 32, HEAD_WIDTH), BF16),) * peers
        + (jax.ShapeDtypeStruct((4 * tok, HEAD_WIDTH), BF16),) * peers,
        sources,
        tuple(pltpu.VMEM(source.shape, BF16) for source in sources) + (pltpu.SemaphoreType.DMA((19,)),),
        flops=1 << 28,
        moved=4 << 20,
        far=len(sources),
        limit=VMEM_PACK,
    )
    firsts, seconds = packed[:peers], packed[peers:]
    firsts = exchange(firsts)
    cross = call(
        assemble_kernel,
        jax.ShapeDtypeStruct((peers, 2 * tok + 16, HEAD_WIDTH), BF16),
        firsts,
        moved=2 << 20,
    )
    cross = lax.ppermute(cross, "ctx", ahead)
    seconds = exchange(seconds)
    length = peers * tok
    ups = (query_up_weight, key_up_weight, value_up_weight, down_t)

    def scratch(keys):
        return (
            pltpu.VMEM((length, HEAD_WIDTH), BF16),
            pltpu.VMEM((length, HEAD_WIDTH), BF16),
            pltpu.VMEM((keys, 2 * HEAD_WIDTH), BF16),
            pltpu.VMEM((keys, 2 * HEAD_WIDTH), BF16),
            pltpu.VMEM((16, keys), F32),
        )

    pairs = length * length
    first_terms, head_f, low, low_tokens = call(
        first_kernel,
        (
            jax.ShapeDtypeStruct((peers, 32, HEAD_WIDTH), F32),
            jax.ShapeDtypeStruct((32, HEAD_WIDTH), F32),
            jax.ShapeDtypeStruct((peers, 32, HEAD_WIDTH), BF16),
            jax.ShapeDtypeStruct((length, HEAD_WIDTH), BF16),
        ),
        firsts + ups,
        scratch(length),
        flops=pairs * 6 * 256,
        moved=3 << 20,
        exps=pairs // 2,
    )
    terms, heads = call(
        functools.partial(second_kernel, near),
        (
            jax.ShapeDtypeStruct((count, 32, HEAD_WIDTH) if near else (peers, 48, HEAD_WIDTH), BF16),
            jax.ShapeDtypeStruct((64, HEAD_WIDTH), F32),
        ),
        seconds + (cross, low, low_tokens, first_terms, head_f) + ups,
        scratch(2 * length),
        flops=3 * pairs * 6 * 256,
        moved=3 << 20,
        exps=3 * pairs // 2,
    )
    if near:
        back = ()
        terms = lax.all_to_all(terms, "ctx", 0, 0)
    else:
        terms = swap(terms)
        back = (lax.ppermute(jnp.sum(terms[:, 32:, :].astype(F32), axis=0), "ctx", behind),)
    wide = width // HEAD_WIDTH
    share = HALF_HEADS * 64 // devices
    direct = devices == wide and share % 16 == 0
    if direct:
        shapes = (jax.ShapeDtypeStruct((wide, 32 + share, HEAD_WIDTH), BF16),)
    else:
        shapes = (
            jax.ShapeDtypeStruct((wide, 32, HEAD_WIDTH), BF16),
            jax.ShapeDtypeStruct((HALF_HEADS, 64, HEAD_WIDTH), BF16),
        )
    parts = call(
        functools.partial(product_kernel, direct, near),
        shapes,
        (terms,) + back + (x, pog, heads),
        flops=2 * 32 * tok * width,
        moved=3 << 20,
    )
    rows = [wide * 32 // devices, share]
    if direct:
        parts = parts[0]
    else:
        parts = jnp.concatenate(
            [part.reshape(devices, n, HEAD_WIDTH) for part, n in zip(parts, rows)], axis=1)
    parts = lax.all_to_all(parts, ("ctx", "dp"), 0, 0)
    paired = direct and lax.axis_size("dp") == 2
    shared = call(
        share_kernel,
        jax.ShapeDtypeStruct((count if paired else devices,) + parts.shape[1:], BF16),
        (parts,),
        moved=1 << 20,
    )
    if paired:
        mine = lax.all_to_all(shared, "ctx", 0, 0)
        gathered = (mine, lax.ppermute(mine, "dp", [(0, 1), (1, 0)]))
    else:
        gathered = (lax.all_to_all(shared, ("ctx", "dp"), 0, 0),)
    if not direct:
        gathered = (
            gathered[0][:, :rows[0]].reshape(wide, 32, HEAD_WIDTH),
            gathered[0][:, rows[0]:].reshape(HALF_HEADS, 64, HEAD_WIDTH),
        )
    kind = "paired" if paired else "whole" if direct else "parts"
    narrow = SHIFT_HEADS * HEAD_WIDTH
    columns = (width, narrow, width, narrow, width, narrow, narrow, width)
    outs = call(
        functools.partial(finish_kernel, kind),
        tuple(jax.ShapeDtypeStruct((ADAPTER_RANK, n), F32) for n in columns),
        gathered,
        moved=2 << 20,
    )
    return tuple(out.T if i in (0, 2, 4, 6) else out for i, out in enumerate(outs))


def solution(mesh):
    placed = (P("dp", "ctx", None),) * 6 + (P(),) * 8
    return jax.shard_map(
        functools.partial(per_device, mesh.size),
        mesh=mesh,
        in_specs=placed,
        out_specs=(P(),) * 8,
        check_vma=False,
    )
```

time: 111 us -> 105 us (0.946)
  blocking collectives: 61.5 us -> 38.4 us
  starting transfers between devices: 11.6 us -> 28.2 us
  Pallas kernels: 21.9 us -> 19.1 us
  waiting for transfers between devices: 14.6 us -> 17.1 us
    all_to_all x1 -> x0, blocking collectives: 22.3 us -> none  [swap(): return lax.all_to_all(array, 'ctx', 0, 0, axis_index_groups=groups)]
    ppermute x8 -> x15, starting transfers between devices: 11.6 us -> 28.2 us  [the longest x14 24.8 us: exchange(): moved.append(lax.ppermute(parts[k], ('ctx', 'dp'), pairs))]
    pallas_call x7, Pallas kernels: 21.9 us -> 19.1 us  [call(): pl.pallas_call(kernel, out_shape=out_shape, in_specs=[pl.BlockSpec(memory...]
    ppermute x8 -> x15, waiting for transfers between devices: 13.2 us -> 15.7 us  [the longest x14 15.7 us: exchange(): moved.append(lax.ppermute(parts[k], ('ctx', 'dp'), pairs))]
  transfers between devices with their start and end apart: 9 -> 16, of which waited for: 6 -> 5; matrix products, arithmetic and copies ran while one was open for 0% -> 0% of each run, Pallas kernels for 5% -> 4%
where the time goes in v4:
time: 105 us
  blocking collectives  38.4 us (37%)
  starting transfers between devices  28.2 us (27%)
  Pallas kernels  19.1 us (18%)
  waiting for transfers between devices  17.1 us (16%)
    ppermute x14, starting transfers between devices, exchange(): moved.append(lax.ppermute(parts[k], ('ctx', 'dp'), pairs))  24.8 us
    pallas_call x7, Pallas kernels, call(): pl.pallas_call(kernel, out_shape=out_shape, in_specs=[pl.BlockSpec(memory...  19.1 us
    ppermute x14, waiting for transfers between devices, exchange(): moved.append(lax.ppermute(parts[k], ('ctx', 'dp'), pairs))  15.7 us
    all_to_all x1, blocking collectives, per_device(): parts = lax.all_to_all(parts, ('ctx', 'dp'), 0, 0)  14.9 us
    all_to_all x1, blocking collectives, per_device(): mine = lax.all_to_all(shared, 'ctx', 0, 0)  12 us
    all_to_all x1, blocking collectives, per_device(): terms = lax.all_to_all(terms, 'ctx', 0, 0)  11.6 us
    ppermute x1, starting transfers between devices, per_device(): cross = lax.ppermute(cross, 'ctx', ahead)  3.34 us
  transfers between devices with their start and end apart: 16, of which 5 were waited for; matrix products, arithmetic and copies ran while one was open for 0% of the time, Pallas kernels for 4%

profile of v4, /device:TPU:0, one launch (start us, length us, event | category | flops | bytes accessed | tf_op | source)
XLA Modules:
  0.0 104.6 jit_solution(6230211274103578130)
XLA Ops:
  0.6 5.0 %shard_map.197 = (bf16[544,128]{1,0:T(8,128)(2,1)}, bf16[544,128]{1,0:T(8,128)(2,1)}, bf16[544,128]{1,0:T(8,128)(2,1)}, bf16[544,128]{1,0:T(8,128)(2,1)}, bf16[5...) custom-call(bf16[128,2048]{1,0:T(8,128)(2,1)} %bitcast.21, ...), custom_call_target="tpu_custom_call" | custom-call | flops 268435456 | bytes 4194304 | tf_op jit(solution)/shard_map/pallas_call | solution.py:39
  5.6 3.0 %collective-permute-start.7 = (bf16[544,128]{1,0:T(8,128)(2,1)}, bf16[544,128]{1,0:T(8,128)(2,1)S(1)}, u32[]{:S(2)}, u32[]{:S(2)}) collective-permute-start(bf16[544,128]{1,0:T(8,128)(2,1)} %get-tuple-element.47), channel_id=1, source_target_pairs={{0,2},{1,5},{2,0},{3,7},{4,6},{5,1},{6,4},{7,3},{8,10},{9,13},{10,... | collective-permute-start | bytes 417800 | tf_op jit(solution)/shard_map/ppermute | solution.py:381
  8.6 1.5 %collective-permute-start.8 = (bf16[544,128]{1,0:T(8,128)(2,1)}, bf16[544,128]{1,0:T(8,128)(2,1)S(1)}, u32[]{:S(2)}, u32[]{:S(2)}) collective-permute-start(bf16[544,128]{1,0:T(8,128)(2,1)} %get-tuple-element.48), channel_id=1, source_target_pairs={{0,4},{1,9},{2,6},{3,11},{4,0},{5,13},{6,2},{7,15},{8,12},{9,1},{1... | collective-permute-start | bytes 417800 | tf_op jit(solution)/shard_map/ppermute | solution.py:381
  10.2 1.6 %collective-permute-start.9 = (bf16[544,128]{1,0:T(8,128)(2,1)}, bf16[544,128]{1,0:T(8,128)(2,1)S(1)}, u32[]{:S(2)}, u32[]{:S(2)}) collective-permute-start(bf16[544,128]{1,0:T(8,128)(2,1)} %get-tuple-element.49), channel_id=1, source_target_pairs={{0,8},{1,3},{2,10},{3,1},{4,12},{5,7},{6,14},{7,5},{8,0},{9,11},{1... | collective-permute-start | bytes 417800 | tf_op jit(solution)/shard_map/ppermute | solution.py:381
  11.7 0.5 collective-permute-start.10
  12.2 1.4 %collective-permute-start.11 = (bf16[544,128]{1,0:T(8,128)(2,1)}, bf16[544,128]{1,0:T(8,128)(2,1)S(1)}, u32[]{:S(2)}, u32[]{:S(2)}) collective-permute-start(bf16[544,128]{1,0:T(8,128)(2,1)} %get-tuple-element.51), channel_id=1, source_target_pairs={{0,10},{1,7},{2,8},{3,5},{4,14},{5,3},{6,12},{7,1},{8,2},{9,15},{1... | collective-permute-start | bytes 417800 | tf_op jit(solution)/shard_map/ppermute | solution.py:381
  13.6 0.0 collective-permute-done.7.refs_1_
  13.6 2.5 %collective-permute-start.12 = (bf16[544,128]{1,0:T(8,128)(2,1)}, bf16[544,128]{1,0:T(8,128)(2,1)S(1)}, u32[]{:S(2)}, u32[]{:S(2)}) collective-permute-start(bf16[544,128]{1,0:T(8,128)(2,1)} %get-tuple-element.52), channel_id=1, source_target_pairs={{0,12},{1,11},{2,14},{3,9},{4,8},{5,15},{6,10},{7,13},{8,4},{9,3},... | collective-permute-start | bytes 417800 | tf_op jit(solution)/shard_map/ppermute | solution.py:381
  16.1 0.0 collective-permute-done.8.refs_2_
  16.1 3.5 %collective-permute-start.13 = (bf16[544,128]{1,0:T(8,128)(2,1)}, bf16[544,128]{1,0:T(8,128)(2,1)S(1)}, u32[]{:S(2)}, u32[]{:S(2)}) collective-permute-start(bf16[544,128]{1,0:T(8,128)(2,1)} %get-tuple-element.53), channel_id=1, source_target_pairs={{0,14},{1,15},{2,12},{3,13},{4,10},{5,11},{6,8},{7,9},{8,6},{9,7},... | collective-permute-start | bytes 417800 | tf_op jit(solution)/shard_map/ppermute | solution.py:381
  19.7 0.0 collective-permute-done.9.refs_3_
  19.7 5.8 %collective-permute-done.10.refs_4_ = bf16[544,128]{1,0:T(8,128)(2,1)S(1)} collective-permute-done((bf16[544,128]{1,0:T(8,128)(2,1)}, bf16[544,128]{1,0:T(8,128)(2,1)S(1)}, u32[]{:S(2)}, u32[]{:S(2)}) %collective-permute-start.10) | collective-permute-done | bytes 139296 | tf_op jit(solution)/shard_map/ppermute | solution.py:381
  25.5 0.0 collective-permute-done.11.refs_5_
  25.5 0.0 collective-permute-done.12.refs_6_
  25.5 0.0 collective-permute-done.13.refs_7_
  25.5 0.0 copy-start.2
  25.5 0.9 copy-done.2
  26.4 0.0 copy-start.11
  26.4 0.0 copy-start.10
  26.4 0.0 copy-start.9
  26.4 0.0 copy-start.3
  26.4 0.0 copy-start.4
  26.4 0.0 copy-start.6
  26.4 0.0 copy-start.7
  26.5 0.0 copy-start.8
  26.5 0.1 shard_map.198
  26.5 3.3 %collective-permute-start.14 = (bf16[8,272,128]{2,1,0:T(8,128)(2,1)S(1)}, bf16[8,272,128]{2,1,0:T(8,128)(2,1)S(1)}, u32[]{:S(2)}, u32[]{:S(2)}) collective-permute-start(bf16[8,272,128]{2,1,0:T(8,128)(2,1)S(1)} %shard_map.198), channel_id=1, source_target_pairs={{0,24},{2,26},{4,28},{6,30},{8,16},{10,18},{12,20},{14,22},{16,8},... | collective-permute-start | bytes 1671176 | tf_op jit(solution)/shard_map/ppermute | solution.py:405
  29.9 0.0 copy-done.15
  29.9 0.6 collective-permute-start
  30.5 0.0 copy-done.14
  30.5 1.5 %collective-permute-start.1 = (bf16[512,128]{1,0:T(8,128)(2,1)S(1)}, bf16[512,128]{1,0:T(8,128)(2,1)S(1)}, u32[]{:S(2)}, u32[]{:S(2)}) collective-permute-start(bf16[512,128]{1,0:T(8,128)(2,1)S(1)} %copy-done.14), channel_id=1, source_target_pairs={{0,4},{1,9},{2,6},{3,11},{4,0},{5,13},{6,2},{7,15},{8,12},{9,1},{1... | collective-permute-start | bytes 393224 | tf_op jit(solution)/shard_map/ppermute | solution.py:381
  32.0 0.0 copy-done.13
  32.0 0.0 collective-permute-start.2
  32.0 0.0 copy-done.12
  32.0 1.4 %collective-permute-start.3 = (bf16[512,128]{1,0:T(8,128)(2,1)S(1)}, bf16[512,128]{1,0:T(8,128)(2,1)S(1)}, u32[]{:S(2)}, u32[]{:S(2)}) collective-permute-start(bf16[512,128]{1,0:T(8,128)(2,1)S(1)} %copy-done.12), channel_id=1, source_target_pairs={{0,6},{1,13},{2,4},{3,15},{4,2},{5,9},{6,0},{7,11},{8,14},{9,5},{1... | collective-permute-start | bytes 393224 | tf_op jit(solution)/shard_map/ppermute | solution.py:381
  33.4 1.8 %collective-permute-done.refs_1_ = bf16[512,128]{1,0:T(8,128)(2,1)S(1)} collective-permute-done((bf16[512,128]{1,0:T(8,128)(2,1)S(1)}, bf16[512,128]{1,0:T(8,128)(2,1)S(1)}, u32[]{:S(2)}, u32[]{:S(2)}) %collective-permute-start) | collective-permute-done | bytes 131104 | tf_op jit(solution)/shard_map/ppermute | solution.py:381
  35.3 0.0 copy-done.11
  35.3 0.2 collective-permute-start.4
  35.5 0.0 collective-permute-done.1.refs_2_
  35.5 0.0 copy-done.10
  35.5 2.8 %collective-permute-start.5 = (bf16[512,128]{1,0:T(8,128)(2,1)S(1)}, bf16[512,128]{1,0:T(8,128)(2,1)S(1)}, u32[]{:S(2)}, u32[]{:S(2)}) collective-permute-start(bf16[512,128]{1,0:T(8,128)(2,1)S(1)} %copy-done.10), channel_id=1, source_target_pairs={{0,12},{1,11},{2,14},{3,9},{4,8},{5,15},{6,10},{7,13},{8,4},{9,3},... | collective-permute-start | bytes 393224 | tf_op jit(solution)/shard_map/ppermute | solution.py:381
  38.3 6.7 %collective-permute-done.2.refs_3_ = bf16[512,128]{1,0:T(8,128)(2,1)S(1)} collective-permute-done((bf16[512,128]{1,0:T(8,128)(2,1)S(1)}, bf16[512,128]{1,0:T(8,128)(2,1)S(1)}, u32[]{:S(2)}, u32[]{:S(2)}) %collective-permute-start.2) | collective-permute-done | bytes 131104 | tf_op jit(solution)/shard_map/ppermute | solution.py:381
  44.9 0.0 copy-done.9
  45.0 4.3 %collective-permute-start.6 = (bf16[512,128]{1,0:T(8,128)(2,1)S(1)}, bf16[512,128]{1,0:T(8,128)(2,1)S(1)}, u32[]{:S(2)}, u32[]{:S(2)}) collective-permute-start(bf16[512,128]{1,0:T(8,128)(2,1)S(1)} %copy-done.9), channel_id=1, source_target_pairs={{0,14},{1,15},{2,12},{3,13},{4,10},{5,11},{6,8},{7,9},{8,6},{9,7},... | collective-permute-start | bytes 393224 | tf_op jit(solution)/shard_map/ppermute | solution.py:381
  49.2 0.0 copy-done.3
  49.2 0.0 copy-done.4
  49.2 0.0 copy-done.6
  49.2 0.0 copy-done.7
  49.2 4.5 %shard_map.199 = (f32[8,32,128]{2,1,0:T(8,128)S(1)}, f32[32,128]{1,0:T(8,128)S(1)}, bf16[8,32,128]{2,1,0:T(8,128)(2,1)S(1)}, bf16[1024,128]{1,0:T(8,128)(2,1)S(1)}) custom-call(bf16[544,128]{1,0:T(8,128)(2,1)S(1)} %copy-done.3, bf16[544,128]{1,0:T(8,128)(2,1)S(1)} %collective-permute-done.7.refs_1_, bf16[544,128]{1,0:T(8,128)(2,1)S(1)} %collective-permute-done.8.refs_2_, ...), custom_call_target="tpu_custom_call" | custom-call | flops 1610612736 | bytes 3145728 | tf_op jit(solution)/shard_map/pallas_call | solution.py:39
  53.7 0.0 collective-permute-done.3.refs_4_
  53.7 0.0 collective-permute-done.4.refs_5_
  53.7 0.0 collective-permute-done.5.refs_6_
  53.7 1.4 %collective-permute-done.6.refs_7_ = bf16[512,128]{1,0:T(8,128)(2,1)S(1)} collective-permute-done((bf16[512,128]{1,0:T(8,128)(2,1)S(1)}, bf16[512,128]{1,0:T(8,128)(2,1)S(1)}, u32[]{:S(2)}, u32[]{:S(2)}) %collective-permute-start.6) | collective-permute-done | bytes 131104 | tf_op jit(solution)/shard_map/ppermute | solution.py:381
  55.1 0.0 collective-permute-done.14.refs_8_
  55.1 0.0 copy-start.1
  55.1 8.2 %shard_map.200 = (bf16[16,32,128]{2,1,0:T(8,128)(2,1)S(1)}, f32[64,128]{1,0:T(8,128)S(1)}) custom-call(bf16[512,128]{1,0:T(8,128)(2,1)S(1)} %copy-done.5, bf16[512,128]{1,0:T(8,128)(2,1)S(1)} %collective-permute-done.refs_1_, bf16[512,128]{1,0:T(8,128)(2,1)S(1)} %collective-permute-done.1.refs_2_, bf16[512,128]{1,0:T(8,128)(2,1)S(1)} %collective-permute-done.2.refs_3_, ...), custom_call_target="tpu_custom_call" | custom-call | flops 4831838208 | bytes 3145728 | tf_op jit(solution)/shard_map/pallas_call | solution.py:39
  63.3 11.6 %all_to_all.15.terms = bf16[16,32,128]{2,1,0:T(8,128)(2,1)S(1)} all-to-all(bf16[16,32,128]{2,1,0:T(8,128)(2,1)S(1)} %get-tuple-element.58), channel_id=1, replica_groups=mesh['ctx'=16,'dp'=2] {'ctx'}, dimensions={0} | all-to-all | bytes 262144 | tf_op jit(solution)/shard_map/all_to_all | solution.py:448
  74.9 0.4 shard_map.201
  75.3 14.9 %all_to_all.16.parts = bf16[32,48,128]{2,1,0:T(8,128)(2,1)S(1)} all-to-all(bf16[32,48,128]{2,1,0:T(8,128)(2,1)S(1)} %shard_map.201), channel_id=1, replica_groups=mesh['ctx'=16,'dp'=2] {'ctx','dp'}, dimensions={0} | all-to-all | bytes 786432 | tf_op jit(solution)/shard_map/all_to_all | solution.py:475
  90.2 0.1 shard_map.202
  90.3 12.0 %all_to_all.17.refs_0_ = bf16[16,48,128]{2,1,0:T(8,128)(2,1)S(1)} all-to-all(bf16[16,48,128]{2,1,0:T(8,128)(2,1)S(1)} %shard_map.202), channel_id=1, replica_groups=mesh['ctx'=16,'dp'=2] {'ctx'}, dimensions={0} | all-to-all | bytes 393216 | tf_op jit(solution)/shard_map/all_to_all | solution.py:484
  102.2 0.0 collective-permute-start.15
  102.2 1.4 %collective-permute-done.15.refs_1_ = bf16[16,48,128]{2,1,0:T(8,128)(2,1)S(1)} collective-permute-done((bf16[16,48,128]{2,1,0:T(8,128)(2,1)S(1)}, bf16[16,48,128]{2,1,0:T(8,128)(2,1)S(1)}, u32[]{:S(2)}, u32[]{:S(2)}) %collective-permute-start.15) | collective-permute-done | bytes 196640 | tf_op jit(solution)/shard_map/ppermute | solution.py:485
  103.7 0.9 shard_map.203
  (10 shorter events, 0.0 us)
Async XLA Ops:
  5.6 8.0 %collective-permute-start.7 = (bf16[544,128]{1,0:T(8,128)(2,1)}, bf16[544,128]{1,0:T(8,128)(2,1)S(1)}, u32[]{:S(2)}, u32[]{:S(2)}) collective-permute-start(bf16[544,128]{1,0:T(8,128)(2,1)} %get-tuple-element.47), channel_id=1, source_target_pairs={{0,2},{1,5},{2,0},{3,7},{4,6},{5,1},{6,4},{7,3},{8,10},{9,13},{10,... | collective-permute-start | bytes 417800 | tf_op jit(solution)/shard_map/ppermute | solution.py:381
  8.6 7.5 %collective-permute-start.8 = (bf16[544,128]{1,0:T(8,128)(2,1)}, bf16[544,128]{1,0:T(8,128)(2,1)S(1)}, u32[]{:S(2)}, u32[]{:S(2)}) collective-permute-start(bf16[544,128]{1,0:T(8,128)(2,1)} %get-tuple-element.48), channel_id=1, source_target_pairs={{0,4},{1,9},{2,6},{3,11},{4,0},{5,13},{6,2},{7,15},{8,12},{9,1},{1... | collective-permute-start | bytes 417800 | tf_op jit(solution)/shard_map/ppermute | solution.py:381
  10.2 9.5 %collective-permute-start.9 = (bf16[544,128]{1,0:T(8,128)(2,1)}, bf16[544,128]{1,0:T(8,128)(2,1)S(1)}, u32[]{:S(2)}, u32[]{:S(2)}) collective-permute-start(bf16[544,128]{1,0:T(8,128)(2,1)} %get-tuple-element.49), channel_id=1, source_target_pairs={{0,8},{1,3},{2,10},{3,1},{4,12},{5,7},{6,14},{7,5},{8,0},{9,11},{1... | collective-permute-start | bytes 417800 | tf_op jit(solution)/shard_map/ppermute | solution.py:381
  11.7 13.7 %collective-permute-start.10 = (bf16[544,128]{1,0:T(8,128)(2,1)}, bf16[544,128]{1,0:T(8,128)(2,1)S(1)}, u32[]{:S(2)}, u32[]{:S(2)}) collective-permute-start(bf16[544,128]{1,0:T(8,128)(2,1)} %get-tuple-element.50), channel_id=1, source_target_pairs={{0,6},{1,13},{2,4},{3,15},{4,2},{5,9},{6,0},{7,11},{8,14},{9,5},{1... | collective-permute-start | bytes 417800 | tf_op jit(solution)/shard_map/ppermute | solution.py:381
  12.2 13.2 %collective-permute-start.11 = (bf16[544,128]{1,0:T(8,128)(2,1)}, bf16[544,128]{1,0:T(8,128)(2,1)S(1)}, u32[]{:S(2)}, u32[]{:S(2)}) collective-permute-start(bf16[544,128]{1,0:T(8,128)(2,1)} %get-tuple-element.51), channel_id=1, source_target_pairs={{0,10},{1,7},{2,8},{3,5},{4,14},{5,3},{6,12},{7,1},{8,2},{9,15},{1... | collective-permute-start | bytes 417800 | tf_op jit(solution)/shard_map/ppermute | solution.py:381
  13.6 11.9 %collective-permute-start.12 = (bf16[544,128]{1,0:T(8,128)(2,1)}, bf16[544,128]{1,0:T(8,128)(2,1)S(1)}, u32[]{:S(2)}, u32[]{:S(2)}) collective-permute-start(bf16[544,128]{1,0:T(8,128)(2,1)} %get-tuple-element.52), channel_id=1, source_target_pairs={{0,12},{1,11},{2,14},{3,9},{4,8},{5,15},{6,10},{7,13},{8,4},{9,3},... | collective-permute-start | bytes 417800 | tf_op jit(solution)/shard_map/ppermute | solution.py:381
  16.1 9.3 %collective-permute-start.13 = (bf16[544,128]{1,0:T(8,128)(2,1)}, bf16[544,128]{1,0:T(8,128)(2,1)S(1)}, u32[]{:S(2)}, u32[]{:S(2)}) collective-permute-start(bf16[544,128]{1,0:T(8,128)(2,1)} %get-tuple-element.53), channel_id=1, source_target_pairs={{0,14},{1,15},{2,12},{3,13},{4,10},{5,11},{6,8},{7,9},{8,6},{9,7},... | collective-permute-start | bytes 417800 | tf_op jit(solution)/shard_map/ppermute | solution.py:381
  25.5 0.9 copy-start.2
  26.4 3.5 %copy-start.15 = (bf16[512,128]{1,0:T(8,128)(2,1)S(1)}, bf16[512,128]{1,0:T(8,128)(2,1)}, u32[]{:S(2)}) copy-start(bf16[512,128]{1,0:T(8,128)(2,1)} %get-tuple-element.39) | copy-start | bytes 393220
  26.4 4.1 %copy-start.14 = (bf16[512,128]{1,0:T(8,128)(2,1)S(1)}, bf16[512,128]{1,0:T(8,128)(2,1)}, u32[]{:S(2)}) copy-start(bf16[512,128]{1,0:T(8,128)(2,1)} %get-tuple-element.40) | copy-start | bytes 393220
  26.4 5.6 %copy-start.13 = (bf16[512,128]{1,0:T(8,128)(2,1)S(1)}, bf16[512,128]{1,0:T(8,128)(2,1)}, u32[]{:S(2)}) copy-start(bf16[512,128]{1,0:T(8,128)(2,1)} %get-tuple-element.41) | copy-start | bytes 393220
  26.4 5.6 %copy-start.12 = (bf16[512,128]{1,0:T(8,128)(2,1)S(1)}, bf16[512,128]{1,0:T(8,128)(2,1)}, u32[]{:S(2)}) copy-start(bf16[512,128]{1,0:T(8,128)(2,1)} %get-tuple-element.42) | copy-start | bytes 393220
  26.4 8.9 %copy-start.11 = (bf16[512,128]{1,0:T(8,128)(2,1)S(1)}, bf16[512,128]{1,0:T(8,128)(2,1)}, u32[]{:S(2)}) copy-start(bf16[512,128]{1,0:T(8,128)(2,1)} %get-tuple-element.43) | copy-start | bytes 393220
  26.4 9.1 %copy-start.10 = (bf16[512,128]{1,0:T(8,128)(2,1)S(1)}, bf16[512,128]{1,0:T(8,128)(2,1)}, u32[]{:S(2)}) copy-start(bf16[512,128]{1,0:T(8,128)(2,1)} %get-tuple-element.44) | copy-start | bytes 393220
  26.4 18.5 %copy-start.9 = (bf16[512,128]{1,0:T(8,128)(2,1)S(1)}, bf16[512,128]{1,0:T(8,128)(2,1)}, u32[]{:S(2)}) copy-start(bf16[512,128]{1,0:T(8,128)(2,1)} %get-tuple-element.45) | copy-start | bytes 393220
  26.4 22.8 %copy-start.3 = (bf16[544,128]{1,0:T(8,128)(2,1)S(1)}, bf16[544,128]{1,0:T(8,128)(2,1)}, u32[]{:S(2)}) copy-start(bf16[544,128]{1,0:T(8,128)(2,1)} %get-tuple-element.46.refs_0_) | copy-start | bytes 417796
  26.4 22.8 %copy-start.4 = (bf16[2048,8]{0,1:T(8,128)(2,1)S(1)}, bf16[2048,8]{0,1:T(8,128)(2,1)}, u32[]{:S(2)}) copy-start(bf16[2048,8]{0,1:T(8,128)(2,1)} %param.26) | copy-start | bytes 98308
  26.4 22.8 %copy-start.6 = (bf16[8,2048]{1,0:T(8,128)(2,1)S(1)}, bf16[8,2048]{1,0:T(8,128)(2,1)}, u32[]{:S(2)}) copy-start(bf16[8,2048]{1,0:T(8,128)(2,1)} %refs_13_.1) | copy-start | bytes 98308
  26.4 22.8 %copy-start.7 = (bf16[8,2048]{1,0:T(8,128)(2,1)S(1)}, bf16[8,2048]{1,0:T(8,128)(2,1)}, u32[]{:S(2)}) copy-start(bf16[8,2048]{1,0:T(8,128)(2,1)} %refs_14_.1) | copy-start | bytes 98308
  26.5 22.8 %copy-start.8 = (bf16[8,2048]{1,0:T(8,128)(2,1)S(1)}, bf16[8,2048]{1,0:T(8,128)(2,1)}, u32[]{:S(2)}) copy-start(bf16[8,2048]{1,0:T(8,128)(2,1)} %refs_15_.1) | copy-start | bytes 98308
  26.5 28.5 %collective-permute-start.14 = (bf16[8,272,128]{2,1,0:T(8,128)(2,1)S(1)}, bf16[8,272,128]{2,1,0:T(8,128)(2,1)S(1)}, u32[]{:S(2)}, u32[]{:S(2)}) collective-permute-start(bf16[8,272,128]{2,1,0:T(8,128)(2,1)S(1)} %shard_map.198), channel_id=1, source_target_pairs={{0,24},{2,26},{4,28},{6,30},{8,16},{10,18},{12,20},{14,22},{16,8},... | collective-permute-start | bytes 1671176 | tf_op jit(solution)/shard_map/ppermute | solution.py:405
  29.9 5.4 %collective-permute-start = (bf16[512,128]{1,0:T(8,128)(2,1)S(1)}, bf16[512,128]{1,0:T(8,128)(2,1)S(1)}, u32[]{:S(2)}, u32[]{:S(2)}) collective-permute-start(bf16[512,128]{1,0:T(8,128)(2,1)S(1)} %copy-done.15), channel_id=1, source_target_pairs={{0,2},{1,5},{2,0},{3,7},{4,6},{5,1},{6,4},{7,3},{8,10},{9,13},{10,... | collective-permute-start | bytes 393224 | tf_op jit(solution)/shard_map/ppermute | solution.py:381
  30.5 5.0 %collective-permute-start.1 = (bf16[512,128]{1,0:T(8,128)(2,1)S(1)}, bf16[512,128]{1,0:T(8,128)(2,1)S(1)}, u32[]{:S(2)}, u32[]{:S(2)}) collective-permute-start(bf16[512,128]{1,0:T(8,128)(2,1)S(1)} %copy-done.14), channel_id=1, source_target_pairs={{0,4},{1,9},{2,6},{3,11},{4,0},{5,13},{6,2},{7,15},{8,12},{9,1},{1... | collective-permute-start | bytes 393224 | tf_op jit(solution)/shard_map/ppermute | solution.py:381
  32.0 12.9 %collective-permute-start.2 = (bf16[512,128]{1,0:T(8,128)(2,1)S(1)}, bf16[512,128]{1,0:T(8,128)(2,1)S(1)}, u32[]{:S(2)}, u32[]{:S(2)}) collective-permute-start(bf16[512,128]{1,0:T(8,128)(2,1)S(1)} %copy-done.13), channel_id=1, source_target_pairs={{0,8},{1,3},{2,10},{3,1},{4,12},{5,7},{6,14},{7,5},{8,0},{9,11},{1... | collective-permute-start | bytes 393224 | tf_op jit(solution)/shard_map/ppermute | solution.py:381
  32.0 21.7 %collective-permute-start.3 = (bf16[512,128]{1,0:T(8,128)(2,1)S(1)}, bf16[512,128]{1,0:T(8,128)(2,1)S(1)}, u32[]{:S(2)}, u32[]{:S(2)}) collective-permute-start(bf16[512,128]{1,0:T(8,128)(2,1)S(1)} %copy-done.12), channel_id=1, source_target_pairs={{0,6},{1,13},{2,4},{3,15},{4,2},{5,9},{6,0},{7,11},{8,14},{9,5},{1... | collective-permute-start | bytes 393224 | tf_op jit(solution)/shard_map/ppermute | solution.py:381
  35.3 18.4 %collective-permute-start.4 = (bf16[512,128]{1,0:T(8,128)(2,1)S(1)}, bf16[512,128]{1,0:T(8,128)(2,1)S(1)}, u32[]{:S(2)}, u32[]{:S(2)}) collective-permute-start(bf16[512,128]{1,0:T(8,128)(2,1)S(1)} %copy-done.11), channel_id=1, source_target_pairs={{0,10},{1,7},{2,8},{3,5},{4,14},{5,3},{6,12},{7,1},{8,2},{9,15},{1... | collective-permute-start | bytes 393224 | tf_op jit(solution)/shard_map/ppermute | solution.py:381
  35.5 18.2 %collective-permute-start.5 = (bf16[512,128]{1,0:T(8,128)(2,1)S(1)}, bf16[512,128]{1,0:T(8,128)(2,1)S(1)}, u32[]{:S(2)}, u32[]{:S(2)}) collective-permute-start(bf16[512,128]{1,0:T(8,128)(2,1)S(1)} %copy-done.10), channel_id=1, source_target_pairs={{0,12},{1,11},{2,14},{3,9},{4,8},{5,15},{6,10},{7,13},{8,4},{9,3},... | collective-permute-start | bytes 393224 | tf_op jit(solution)/shard_map/ppermute | solution.py:381
  45.0 10.1 %copy-start.5 = (bf16[512,128]{1,0:T(8,128)(2,1)S(1)}, bf16[512,128]{1,0:T(8,128)(2,1)}, u32[]{:S(2)}) copy-start(bf16[512,128]{1,0:T(8,128)(2,1)} %get-tuple-element.38.refs_0_) | copy-start | bytes 393220
  45.0 10.1 %collective-permute-start.6 = (bf16[512,128]{1,0:T(8,128)(2,1)S(1)}, bf16[512,128]{1,0:T(8,128)(2,1)S(1)}, u32[]{:S(2)}, u32[]{:S(2)}) collective-permute-start(bf16[512,128]{1,0:T(8,128)(2,1)S(1)} %copy-done.9), channel_id=1, source_target_pairs={{0,14},{1,15},{2,12},{3,13},{4,10},{5,11},{6,8},{7,9},{8,6},{9,7},... | collective-permute-start | bytes 393224 | tf_op jit(solution)/shard_map/ppermute | solution.py:381
  55.1 19.8 %copy-start = (bf16[1,128,4096]{2,1,0:T(8,128)(2,1)S(1)}, bf16[1,128,4096]{2,1,0:T(8,128)(2,1)}, u32[]{:S(2)}) copy-start(bf16[1,128,4096]{2,1,0:T(8,128)(2,1)} %param.14) | copy-start | bytes 3145732
  55.1 19.8 %copy-start.1 = (bf16[1,128,4096]{2,1,0:T(8,128)(2,1)S(1)}, bf16[1,128,4096]{2,1,0:T(8,128)(2,1)}, u32[]{:S(2)}) copy-start(bf16[1,128,4096]{2,1,0:T(8,128)(2,1)} %param.15) | copy-start | bytes 3145732
  102.2 1.4 %collective-permute-start.15 = (bf16[16,48,128]{2,1,0:T(8,128)(2,1)S(1)}, bf16[16,48,128]{2,1,0:T(8,128)(2,1)S(1)}, u32[]{:S(2)}, u32[]{:S(2)}) collective-permute-start(bf16[16,48,128]{2,1,0:T(8,128)(2,1)S(1)} %all_to_all.17.refs_0_), channel_id=1, source_target_pairs={{0,1},{1,0},{2,3},{3,2},{4,5},{5,4},{6,7},{7,6},{8,9},{9,8},{10,11... | collective-permute-start | bytes 589832 | tf_op jit(solution)/shard_map/ppermute | solution.py:485

commit v5 on v4

--- a/solution.py
+++ b/solution.py
@@ -21,7 +21,7 @@
 F32 = jnp.float32
 BF16 = jnp.bfloat16
 NT = (((1,), (1,)), ((), ()))
-ORDERS = ((0, 1, 2, 4, 3, 5, 6, 7), (0, 2, 4, 1, 6, 3, 5, 7))
+ORDERS = ((0, 1, 6, 2, 5, 4, 3, 7), (0, 6, 1, 5, 2, 3, 4, 7))
 BLOCK = 256
 VMEM_LIMIT = 24 * 1024 * 1024
 VMEM_PACK = 56 * 1024 * 1024
@@ -103,27 +103,28 @@
         whole[i].start()
     for i in (6, 7, 8, 9):
         whole[i].wait()
-    down = jnp.concatenate([qds[...], kds[...], vds[...]], axis=0)
-    low = jnp.zeros((24, tok), F32)
-    low_out = jnp.zeros((8, tok), F32)
+    gap = jnp.zeros((8, width), BF16)
+    down = jnp.concatenate([qds[...], gap, kds[...], vds[...]], axis=0)
+    upper = jnp.concatenate([gap, ous[...], gap, gap], axis=0)
+    low = jnp.zeros((tok, 32), F32)
     peers = partners()
     spots = ((0, 0, 0), (1, 2 * tok + 32, 2 * tok), (2, 3 * tok + 32, 3 * tok))
     for c in range(chunks):
         columns = slice(c * step, (c + 1) * step)
         wide[c][0].wait()
-        low += dot_nt(down[:, columns], xs[:, columns])
+        low += dot_nt(xs[:, columns], down[:, columns])
         wide[c][1].wait()
-        low_out += dot_nt(ous[:, columns], ps[:, columns])
+        low += dot_nt(ps[:, columns], upper[:, columns])
         if c > 0:
             i, at, late = spots[c - 1]
             whole[i].wait()
             spread(bufs[i], odd, peers, firsts, at, seconds, late)
-    low_b = jnp.concatenate([low[0:8], low_out, low[8:24]], axis=0).astype(BF16)
-    by_token = tokens_first(low_b.astype(F32)).astype(BF16)
+    low_b = jnp.transpose(jnp.concatenate([low, jnp.zeros((tok, HEAD_WIDTH - 32), F32)], axis=1))[:32].astype(BF16)
+    by_token = low.astype(BF16)
     columns = od.shape[1]
     whole[10].wait()
     up = jnp.concatenate([jnp.zeros((8, columns), BF16), ods[...], jnp.zeros((16, columns), BF16)], axis=0)
-    raised = dot(by_token[:, :32], up)
+    raised = dot(by_token, up)
     whole[5].wait()
     fs[...] = (fs[...].astype(F32) + raised).astype(BF16)
     spread(fs, odd, peers, firsts, tok, seconds, tok)
@@ -140,6 +141,10 @@
 
 def second_head(peer):
     return jnp.bitwise_xor(peer, MIRROR)
+
+
+def keep_kernel(part, out):
+    out[...] = part[...]
 
 
 def assemble_kernel(*refs):
@@ -170,31 +175,42 @@
     causal = columns_of <= rows_of
     per = BLOCK // tok
     pairs = []
-    for b in range(length // BLOCK):
+    def scored(b):
         qb = queries[b * BLOCK:(b + 1) * BLOCK, :]
         gb = grads[b * BLOCK:(b + 1) * BLOCK, :]
         past = lead + b * BLOCK
         reach = past + BLOCK
         scores = dot_nt(qb, kext[:reach, :tok])
+        dweights = dot_nt(gb, vext[:reach, :tok])
+        return qb, gb, past, reach, scores, dweights
+
+    def softened(scores, past):
         diagonal = jnp.where(causal, scores[:, past:], MASKED)
         scores = jnp.concatenate([scores[:, :past], diagonal], axis=1) if past else diagonal
         summit = jnp.max(scores, axis=1, keepdims=True)
         e = jnp.exp2((scores - summit) * factor)
-        inv = 1.0 / jnp.sum(e, axis=1, keepdims=True)
+        return e, 1.0 / jnp.sum(e, axis=1, keepdims=True)
+
+    count = length // BLOCK
+    ahead = scored(0)
+    for b in range(count):
+        qb, gb, past, reach, scores, dweights = ahead
+        if b + 1 < count:
+            ahead = scored(b + 1)
+        e, inv = softened(scores, past)
         p = e.astype(BF16)
         mixed = dot(p, vext[:reach, :])
         output = mixed[:, :tok] * inv
+        gs = (gb.astype(F32) * inv).astype(BF16)
+        sums[8:16, :reach] += dot(dot_nt(up_v, gs).astype(BF16), p)
         delta = jnp.sum(gb.astype(F32) * output, axis=1, keepdims=True)
-        dweights = dot_nt(gb, vext[:reach, :tok])
         ds = (e * (dweights - delta)).astype(BF16)
         dmixed = dot(ds, kext[:reach, :])
         row_scale = inv * SCALE
         dq = (dmixed[:, :tok] * row_scale).astype(BF16)
         qs = (qb.astype(F32) * row_scale).astype(BF16)
-        gs = (gb.astype(F32) * inv).astype(BF16)
         ob = output.astype(BF16)
         sums[0:8, :reach] += dot(dot_nt(up_k, qs).astype(BF16), ds)
-        sums[8:16, :reach] += dot(dot_nt(up_v, gs).astype(BF16), p)
         bk += dot(jnp.transpose(dmixed[:, tok:])[16:24].astype(BF16), qs)
         bv += dot(jnp.transpose(mixed[:, tok:])[24:32].astype(BF16), gs)
         bq += dot(low_q[:, b * BLOCK:(b + 1) * BLOCK], dq)
@@ -273,7 +289,7 @@
     heads[32:, :] = head_s
 
 
-def product_kernel(direct, near, terms, *refs):
+def product_kernel(kind, near, terms, *refs):
     own = jnp.sum(terms[:, :32, :].astype(F32), axis=0)
     mixed = own[16:32]
     if not near:
@@ -286,23 +302,42 @@
     head = heads[...].astype(BF16)
     odd, slot = place()
     step = 4
+    zero = lax.axis_index("dp") == 0
+
+    def put(pair, rows, first, second):
+        outs[0][pair, rows, :] = jnp.where(zero, first, second)
+        outs[1][pair, rows, :] = jnp.where(zero, second, first)
+
     for c in range(0, wide, step):
         columns = slice(c * HEAD_WIDTH, (c + step) * HEAD_WIDTH)
         a = jnp.concatenate([dot(left, x[:, columns]), dot(right, pog[:, columns])], axis=0).astype(BF16)
+        a = [a[:, i * HEAD_WIDTH:(i + 1) * HEAD_WIDTH] for i in range(step)]
         for i in range(step):
-            outs[0][c + i, :32, :] = a[:, i * HEAD_WIDTH:(i + 1) * HEAD_WIDTH]
+            if kind != "paired":
+                outs[0][c + i, :32, :] = a[i]
+            elif i % 2 == 0:
+                put((c + i) // 2, slice(0, 32), a[i], a[i + 1])
     spots = ((slot, odd), (second_head(slot), 1 - odd))
-    if direct:
-        per = wide // HALF_HEADS
-        share = 64 // per
-        outs[0][:, 32:, :] = jnp.zeros((wide, share, HEAD_WIDTH), BF16)
-        for i in range(per):
-            where, half = spots[2 * i // per]
-            outs[0][where * per + half * (per // 2) + i % (per // 2), 32:, :] = head[i * share:(i + 1) * share]
-    else:
+    per = wide // HALF_HEADS
+    share = 64 // per
+    if kind == "parts":
         outs[1][...] = jnp.zeros(outs[1].shape, BF16)
         for i, (where, half) in enumerate(spots):
             outs[1][where, pl.ds(pl.multiple_of(32 * half, 32), 32), :] = head[32 * i:32 * i + 32]
+        return
+    for out in outs:
+        out[:, 32:, :] = jnp.zeros((out.shape[0], share, HEAD_WIDTH), BF16)
+    for i in range(per):
+        where, half = spots[2 * i // per]
+        at = where * per + half * (per // 2) + i % (per // 2)
+        if kind != "paired":
+            outs[0][at, 32:, :] = head[i * share:(i + 1) * share]
+        elif i % 2 == 0:
+            put(lax.div(at, 2), slice(32, 32 + share), head[i * share:(i + 1) * share], head[(i + 1) * share:(i + 2) * share])
+
+
+def add_kernel(a, b, out):
+    out[...] = (a[...].astype(F32) + b[...].astype(F32)).astype(BF16)
 
 
 def share_kernel(parts, out):
@@ -395,6 +430,7 @@
         limit=VMEM_PACK,
     )
     firsts, seconds = packed[:peers], packed[peers:]
+    firsts = (call(keep_kernel, jax.ShapeDtypeStruct(firsts[0].shape, BF16), firsts[:1]),) + tuple(firsts[1:])
     firsts = exchange(firsts)
     cross = call(
         assemble_kernel,
@@ -452,7 +488,12 @@
     wide = width // HEAD_WIDTH
     share = HALF_HEADS * 64 // devices
     direct = devices == wide and share % 16 == 0
-    if direct:
+    paired = direct and lax.axis_size("dp") == 2
+    kind = "paired" if paired else "whole" if direct else "parts"
+    other_core = [(0, 1), (1, 0)]
+    if paired:
+        shapes = (jax.ShapeDtypeStruct((count, 32 + share, HEAD_WIDTH), BF16),) * 2
+    elif direct:
         shapes = (jax.ShapeDtypeStruct((wide, 32 + share, HEAD_WIDTH), BF16),)
     else:
         shapes = (
@@ -460,29 +501,33 @@
             jax.ShapeDtypeStruct((HALF_HEADS, 64, HEAD_WIDTH), BF16),
         )
     parts = call(
-        functools.partial(product_kernel, direct, near),
+        functools.partial(product_kernel, kind, near),
         shapes,
         (terms,) + back + (x, pog, heads),
         flops=2 * 32 * tok * width,
         moved=3 << 20,
     )
     rows = [wide * 32 // devices, share]
-    if direct:
-        parts = parts[0]
+    if paired:
+        theirs = lax.ppermute(parts[1], "dp", other_core)
+        parts = call(add_kernel, shapes[0], (parts[0], theirs), moved=1 << 20)
+        parts = lax.all_to_all(parts, "ctx", 0, 0)
     else:
-        parts = jnp.concatenate(
-            [part.reshape(devices, n, HEAD_WIDTH) for part, n in zip(parts, rows)], axis=1)
-    parts = lax.all_to_all(parts, ("ctx", "dp"), 0, 0)
-    paired = direct and lax.axis_size("dp") == 2
+        if direct:
+            parts = parts[0]
+        else:
+            parts = jnp.concatenate(
+                [part.reshape(devices, n, HEAD_WIDTH) for part, n in zip(parts, rows)], axis=1)
+        parts = lax.all_to_all(parts, ("ctx", "dp"), 0, 0)
     shared = call(
         share_kernel,
-        jax.ShapeDtypeStruct((count if paired else devices,) + parts.shape[1:], BF16),
+        jax.ShapeDtypeStruct(parts.shape, BF16),
         (parts,),
         moved=1 << 20,
     )
     if paired:
         mine = lax.all_to_all(shared, "ctx", 0, 0)
-        gathered = (mine, lax.ppermute(mine, "dp", [(0, 1), (1, 0)]))
+        gathered = (mine, lax.ppermute(mine, "dp", other_core))
     else:
         gathered = (lax.all_to_all(shared, ("ctx", "dp"), 0, 0),)
     if not direct:
@@ -490,7 +535,6 @@
             gathered[0][:, :rows[0]].reshape(wide, 32, HEAD_WIDTH),
             gathered[0][:, rows[0]:].reshape(HALF_HEADS, 64, HEAD_WIDTH),
         )
-    kind = "paired" if paired else "whole" if direct else "parts"
     narrow = SHIFT_HEADS * HEAD_WIDTH
     columns = (width, narrow, width, narrow, width, narrow, narrow, width)
     outs = call(

time: 105 us -> 99.7 us (0.950)
  blocking collectives: 38.4 us -> 35.1 us
  waiting for transfers between devices: 17.1 us -> 14.8 us
  starting transfers between devices: 28.2 us -> 29.8 us
  Pallas kernels: 19.1 us -> 18 us
    ppermute x14, waiting for transfers between devices: 15.7 us -> 11.9 us  [exchange(): moved.append(lax.ppermute(parts[k], ('ctx', 'dp'), pairs))]
    all_to_all x1, blocking collectives: 14.9 us -> 11.5 us  [per_device(): parts = lax.all_to_all(parts, 'ctx', 0, 0)]
    ppermute x1, starting transfers between devices: 3.34 us -> 5.18 us  [per_device(): cross = lax.ppermute(cross, 'ctx', ahead)]
    ppermute x1 -> x2, waiting for transfers between devices: 1.44 us -> 2.87 us  [the longest x1 1.44 us: per_device(): gathered = (mine, lax.ppermute(mine, 'dp', other_core))]
    pallas_call x7 -> x9, Pallas kernels: 19.1 us -> 18 us  [call(): pl.pallas_call(kernel, out_shape=out_shape, in_specs=[pl.BlockSpec(memory...]
  transfers between devices with their start and end apart: 16 -> 17, of which waited for: 5 -> 5; matrix products, arithmetic and copies ran while one was open for 0% -> 0% of each run, Pallas kernels for 4% -> 4%
where the time goes in v5:
time: 99.7 us; the launch traced here: 99.4 us
  blocking collectives  35.1 us (35%)
  starting transfers between devices  29.8 us (30%)
  Pallas kernels  18 us (18%)
  waiting for transfers between devices  14.8 us (15%)
    ppermute x14, starting transfers between devices, exchange(): moved.append(lax.ppermute(parts[k], ('ctx', 'dp'), pairs))  24.5 us
    pallas_call x9, Pallas kernels, call(): pl.pallas_call(kernel, out_shape=out_shape, in_specs=[pl.BlockSpec(memory...  18 us
    all_to_all x1, blocking collectives, per_device(): terms = lax.all_to_all(terms, 'ctx', 0, 0)  12.1 us
    ppermute x14, waiting for transfers between devices, exchange(): moved.append(lax.ppermute(parts[k], ('ctx', 'dp'), pairs))  11.9 us
    all_to_all x1, blocking collectives, per_device(): mine = lax.all_to_all(shared, 'ctx', 0, 0)  11.5 us
    all_to_all x1, blocking collectives, per_device(): parts = lax.all_to_all(parts, 'ctx', 0, 0)  11.5 us
    ppermute x1, starting transfers between devices, per_device(): cross = lax.ppermute(cross, 'ctx', ahead)  5.18 us
  transfers between devices with their start and end apart: 17, of which 5 were waited for; matrix products, arithmetic and copies ran while one was open for 0% of the time, Pallas kernels for 4%

profile of v5, /device:TPU:0, one launch (start us, length us, event | category | flops | bytes accessed | tf_op | source)
XLA Modules:
  0.0 99.4 jit_solution(5505077898171837707)
XLA Ops:
  0.6 5.0 %shard_map.197 = (bf16[544,128]{1,0:T(8,128)(2,1)}, bf16[544,128]{1,0:T(8,128)(2,1)}, bf16[544,128]{1,0:T(8,128)(2,1)}, bf16[544,128]{1,0:T(8,128)(2,1)}, bf16[5...) custom-call(bf16[128,2048]{1,0:T(8,128)(2,1)} %bitcast.21, ...), custom_call_target="tpu_custom_call" | custom-call | flops 268435456 | bytes 4194304 | tf_op jit(solution)/shard_map/pallas_call | solution.py:39
  5.7 3.0 %collective-permute-start.7 = (bf16[544,128]{1,0:T(8,128)(2,1)}, bf16[544,128]{1,0:T(8,128)(2,1)S(1)}, u32[]{:S(2)}, u32[]{:S(2)}) collective-permute-start(bf16[544,128]{1,0:T(8,128)(2,1)} %get-tuple-element.49), channel_id=1, source_target_pairs={{0,2},{1,13},{2,0},{3,15},{4,6},{5,9},{6,4},{7,11},{8,10},{9,5},{1... | collective-permute-start | bytes 417800 | tf_op jit(solution)/shard_map/ppermute | solution.py:416
  8.7 2.5 %collective-permute-start.8 = (bf16[544,128]{1,0:T(8,128)(2,1)}, bf16[544,128]{1,0:T(8,128)(2,1)S(1)}, u32[]{:S(2)}, u32[]{:S(2)}) collective-permute-start(bf16[544,128]{1,0:T(8,128)(2,1)} %get-tuple-element.50), channel_id=1, source_target_pairs={{0,12},{1,3},{2,14},{3,1},{4,8},{5,7},{6,10},{7,5},{8,4},{9,11},{1... | collective-permute-start | bytes 417800 | tf_op jit(solution)/shard_map/ppermute | solution.py:416
  11.2 0.5 collective-permute-start.9
  11.7 0.0 collective-permute-start.10
  11.8 2.0 %collective-permute-start.11 = (bf16[544,128]{1,0:T(8,128)(2,1)}, bf16[544,128]{1,0:T(8,128)(2,1)S(1)}, u32[]{:S(2)}, u32[]{:S(2)}) collective-permute-start(bf16[544,128]{1,0:T(8,128)(2,1)} %get-tuple-element.53), channel_id=1, source_target_pairs={{0,8},{1,7},{2,10},{3,5},{4,12},{5,3},{6,14},{7,1},{8,0},{9,15},{1... | collective-permute-start | bytes 417800 | tf_op jit(solution)/shard_map/ppermute | solution.py:416
  13.7 0.0 collective-permute-done.7.refs_1_
  13.7 4.0 %collective-permute-start.12 = (bf16[544,128]{1,0:T(8,128)(2,1)}, bf16[544,128]{1,0:T(8,128)(2,1)S(1)}, u32[]{:S(2)}, u32[]{:S(2)}) collective-permute-start(bf16[544,128]{1,0:T(8,128)(2,1)} %get-tuple-element.54), channel_id=1, source_target_pairs={{0,6},{1,9},{2,4},{3,11},{4,2},{5,13},{6,0},{7,15},{8,14},{9,1},{1... | collective-permute-start | bytes 417800 | tf_op jit(solution)/shard_map/ppermute | solution.py:416
  17.8 0.0 collective-permute-done.8.refs_2_
  17.8 2.3 %collective-permute-start.13 = (bf16[544,128]{1,0:T(8,128)(2,1)}, bf16[544,128]{1,0:T(8,128)(2,1)S(1)}, u32[]{:S(2)}, u32[]{:S(2)}) collective-permute-start(bf16[544,128]{1,0:T(8,128)(2,1)} %get-tuple-element.55), channel_id=1, source_target_pairs={{0,14},{1,15},{2,12},{3,13},{4,10},{5,11},{6,8},{7,9},{8,6},{9,7},... | collective-permute-start | bytes 417800 | tf_op jit(solution)/shard_map/ppermute | solution.py:416
  20.1 0.9 copy-done.2
  21.0 0.0 copy-start.14
  21.0 0.0 copy-start.13
  21.0 0.0 copy-start.12
  21.0 0.0 copy-start.11
  21.0 0.0 copy-start.10
  21.0 0.0 copy-start.9
  21.0 0.0 copy-start.8
  21.1 0.0 copy-start.3
  21.1 0.0 copy-start.5
  21.1 0.0 copy-start.6
  21.1 0.0 copy-start.7
  21.1 0.0 collective-permute-done.9.refs_3_
  21.1 0.0 collective-permute-done.10.refs_4_
  21.1 0.0 collective-permute-done.11.refs_5_
  21.1 2.5 %collective-permute-done.12.refs_6_ = bf16[544,128]{1,0:T(8,128)(2,1)S(1)} collective-permute-done((bf16[544,128]{1,0:T(8,128)(2,1)}, bf16[544,128]{1,0:T(8,128)(2,1)S(1)}, u32[]{:S(2)}, u32[]{:S(2)}) %collective-permute-start.12) | collective-permute-done | bytes 139296 | tf_op jit(solution)/shard_map/ppermute | solution.py:416
  23.7 1.2 %collective-permute-done.13.refs_7_ = bf16[544,128]{1,0:T(8,128)(2,1)S(1)} collective-permute-done((bf16[544,128]{1,0:T(8,128)(2,1)}, bf16[544,128]{1,0:T(8,128)(2,1)S(1)}, u32[]{:S(2)}, u32[]{:S(2)}) %collective-permute-start.13) | collective-permute-done | bytes 139296 | tf_op jit(solution)/shard_map/ppermute | solution.py:416
  24.9 0.1 shard_map.199
  24.9 5.2 %collective-permute-start.14 = (bf16[8,272,128]{2,1,0:T(8,128)(2,1)S(1)}, bf16[8,272,128]{2,1,0:T(8,128)(2,1)S(1)}, u32[]{:S(2)}, u32[]{:S(2)}) collective-permute-start(bf16[8,272,128]{2,1,0:T(8,128)(2,1)S(1)} %shard_map.199), channel_id=1, source_target_pairs={{0,24},{2,26},{4,28},{6,30},{8,16},{10,18},{12,20},{14,22},{16,8},... | collective-permute-start | bytes 1671176 | tf_op jit(solution)/shard_map/ppermute | solution.py:441
  30.1 0.0 copy-done.14
  30.1 0.0 collective-permute-start
  30.1 0.0 copy-done.13
  30.1 0.1 collective-permute-start.1
  30.2 0.0 copy-done.12
  30.2 0.8 collective-permute-start.2
  31.1 0.0 copy-done.11
  31.1 4.0 %collective-permute-start.3 = (bf16[512,128]{1,0:T(8,128)(2,1)S(1)}, bf16[512,128]{1,0:T(8,128)(2,1)S(1)}, u32[]{:S(2)}, u32[]{:S(2)}) collective-permute-start(bf16[512,128]{1,0:T(8,128)(2,1)S(1)} %copy-done.11), channel_id=1, source_target_pairs={{0,10},{1,5},{2,8},{3,7},{4,14},{5,1},{6,12},{7,3},{8,2},{9,13},{1... | collective-permute-start | bytes 393224 | tf_op jit(solution)/shard_map/ppermute | solution.py:416
  35.1 0.0 collective-permute-done.refs_1_
  35.1 0.0 copy-done.10
  35.1 0.0 collective-permute-start.4
  35.1 8.1 %collective-permute-done.1.refs_2_ = bf16[512,128]{1,0:T(8,128)(2,1)S(1)} collective-permute-done((bf16[512,128]{1,0:T(8,128)(2,1)S(1)}, bf16[512,128]{1,0:T(8,128)(2,1)S(1)}, u32[]{:S(2)}, u32[]{:S(2)}) %collective-permute-start.1) | collective-permute-done | bytes 131104 | tf_op jit(solution)/shard_map/ppermute | solution.py:416
  43.2 0.0 copy-done.9
  43.2 0.6 collective-permute-start.5
  43.8 0.0 collective-permute-done.2.refs_3_
  43.8 0.0 copy-done.8
  43.8 4.6 %collective-permute-start.6 = (bf16[512,128]{1,0:T(8,128)(2,1)S(1)}, bf16[512,128]{1,0:T(8,128)(2,1)S(1)}, u32[]{:S(2)}, u32[]{:S(2)}) collective-permute-start(bf16[512,128]{1,0:T(8,128)(2,1)S(1)} %copy-done.8), channel_id=1, source_target_pairs={{0,14},{1,15},{2,12},{3,13},{4,10},{5,11},{6,8},{7,9},{8,6},{9,7},... | collective-permute-start | bytes 393224 | tf_op jit(solution)/shard_map/ppermute | solution.py:416
  48.4 4.1 %shard_map.200 = (f32[8,32,128]{2,1,0:T(8,128)S(1)}, f32[32,128]{1,0:T(8,128)S(1)}, bf16[8,32,128]{2,1,0:T(8,128)(2,1)S(1)}, bf16[1024,128]{1,0:T(8,128)(2,1)S(1)}) custom-call(bf16[544,128]{1,0:T(8,128)(2,1)S(1)} %shard_map.198.refs_0_, bf16[544,128]{1,0:T(8,128)(2,1)S(1)} %collective-permute-done.7.refs_1_, ...), custom_call_target="tpu_custom_call" | custom-call | flops 1610612736 | bytes 3145728 | tf_op jit(solution)/shard_map/pallas_call | solution.py:39
  52.5 0.0 collective-permute-done.3.refs_4_
  52.5 0.0 collective-permute-done.4.refs_5_
  52.5 0.0 collective-permute-done.5.refs_6_
  52.6 0.0 collective-permute-done.6.refs_7_
  52.6 0.0 collective-permute-done.14.refs_8_
  52.6 0.0 copy-start
  52.6 0.0 copy-start.1
  52.6 7.4 %shard_map.201 = (bf16[16,32,128]{2,1,0:T(8,128)(2,1)S(1)}, f32[64,128]{1,0:T(8,128)S(1)}) custom-call(bf16[512,128]{1,0:T(8,128)(2,1)S(1)} %copy-done.4, bf16[512,128]{1,0:T(8,128)(2,1)S(1)} %collective-permute-done.refs_1_, bf16[512,128]{1,0:T(8,128)(2,1)S(1)} %collective-permute-done.1.refs_2_, bf16[512,128]{1,0:T(8,128)(2,1)S(1)} %collective-permute-done.2.refs_3_, ...), custom_call_target="tpu_custom_call" | custom-call | flops 4831838208 | bytes 3145728 | tf_op jit(solution)/shard_map/pallas_call | solution.py:39
  60.0 12.1 %all_to_all.15.terms = bf16[16,32,128]{2,1,0:T(8,128)(2,1)S(1)} all-to-all(bf16[16,32,128]{2,1,0:T(8,128)(2,1)S(1)} %get-tuple-element.60), channel_id=1, replica_groups=mesh['ctx'=16,'dp'=2] {'ctx'}, dimensions={0} | all-to-all | bytes 262144 | tf_op jit(solution)/shard_map/all_to_all | solution.py:484
  72.1 0.4 shard_map.202
  72.5 0.1 collective-permute-start.15
  72.5 1.4 %collective-permute-done.15.b = bf16[16,48,128]{2,1,0:T(8,128)(2,1)S(1)} collective-permute-done((bf16[16,48,128]{2,1,0:T(8,128)(2,1)S(1)}, bf16[16,48,128]{2,1,0:T(8,128)(2,1)S(1)}, u32[]{:S(2)}, u32[]{:S(2)}) %collective-permute-start.15) | collective-permute-done | bytes 196640 | tf_op jit(solution)/shard_map/ppermute | solution.py:512
  74.0 11.5 %all_to_all.16.parts = bf16[16,48,128]{2,1,0:T(8,128)(2,1)S(1)} all-to-all(bf16[16,48,128]{2,1,0:T(8,128)(2,1)S(1)} %shard_map.203), channel_id=1, replica_groups=mesh['ctx'=16,'dp'=2] {'ctx'}, dimensions={0} | all-to-all | bytes 393216 | tf_op jit(solution)/shard_map/all_to_all | solution.py:514
  85.6 11.5 %all_to_all.17.refs_0_ = bf16[16,48,128]{2,1,0:T(8,128)(2,1)S(1)} all-to-all(bf16[16,48,128]{2,1,0:T(8,128)(2,1)S(1)} %shard_map.204), channel_id=1, replica_groups=mesh['ctx'=16,'dp'=2] {'ctx'}, dimensions={0} | all-to-all | bytes 393216 | tf_op jit(solution)/shard_map/all_to_all | solution.py:529
  97.1 0.0 collective-permute-start.16
  97.1 1.4 %collective-permute-done.16.refs_1_ = bf16[16,48,128]{2,1,0:T(8,128)(2,1)S(1)} collective-permute-done((bf16[16,48,128]{2,1,0:T(8,128)(2,1)S(1)}, bf16[16,48,128]{2,1,0:T(8,128)(2,1)S(1)}, u32[]{:S(2)}, u32[]{:S(2)}) %collective-permute-start.16) | collective-permute-done | bytes 196640 | tf_op jit(solution)/shard_map/ppermute | solution.py:530
  98.5 0.9 shard_map.205
  (12 shorter events, 0.1 us)
Async XLA Ops:
  5.7 8.1 %collective-permute-start.7 = (bf16[544,128]{1,0:T(8,128)(2,1)}, bf16[544,128]{1,0:T(8,128)(2,1)S(1)}, u32[]{:S(2)}, u32[]{:S(2)}) collective-permute-start(bf16[544,128]{1,0:T(8,128)(2,1)} %get-tuple-element.49), channel_id=1, source_target_pairs={{0,2},{1,13},{2,0},{3,15},{4,6},{5,9},{6,4},{7,11},{8,10},{9,5},{1... | collective-permute-start | bytes 417800 | tf_op jit(solution)/shard_map/ppermute | solution.py:416
  8.7 9.1 %collective-permute-start.8 = (bf16[544,128]{1,0:T(8,128)(2,1)}, bf16[544,128]{1,0:T(8,128)(2,1)S(1)}, u32[]{:S(2)}, u32[]{:S(2)}) collective-permute-start(bf16[544,128]{1,0:T(8,128)(2,1)} %get-tuple-element.50), channel_id=1, source_target_pairs={{0,12},{1,3},{2,14},{3,1},{4,8},{5,7},{6,10},{7,5},{8,4},{9,11},{1... | collective-permute-start | bytes 417800 | tf_op jit(solution)/shard_map/ppermute | solution.py:416
  11.2 9.9 %collective-permute-start.9 = (bf16[544,128]{1,0:T(8,128)(2,1)}, bf16[544,128]{1,0:T(8,128)(2,1)S(1)}, u32[]{:S(2)}, u32[]{:S(2)}) collective-permute-start(bf16[544,128]{1,0:T(8,128)(2,1)} %get-tuple-element.51), channel_id=1, source_target_pairs={{0,4},{1,11},{2,6},{3,9},{4,0},{5,15},{6,2},{7,13},{8,12},{9,3},{1... | collective-permute-start | bytes 417800 | tf_op jit(solution)/shard_map/ppermute | solution.py:416
  11.7 9.4 %collective-permute-start.10 = (bf16[544,128]{1,0:T(8,128)(2,1)}, bf16[544,128]{1,0:T(8,128)(2,1)S(1)}, u32[]{:S(2)}, u32[]{:S(2)}) collective-permute-start(bf16[544,128]{1,0:T(8,128)(2,1)} %get-tuple-element.52), channel_id=1, source_target_pairs={{0,10},{1,5},{2,8},{3,7},{4,14},{5,1},{6,12},{7,3},{8,2},{9,13},{1... | collective-permute-start | bytes 417800 | tf_op jit(solution)/shard_map/ppermute | solution.py:416
  11.8 9.4 %collective-permute-start.11 = (bf16[544,128]{1,0:T(8,128)(2,1)}, bf16[544,128]{1,0:T(8,128)(2,1)S(1)}, u32[]{:S(2)}, u32[]{:S(2)}) collective-permute-start(bf16[544,128]{1,0:T(8,128)(2,1)} %get-tuple-element.53), channel_id=1, source_target_pairs={{0,8},{1,7},{2,10},{3,5},{4,12},{5,3},{6,14},{7,1},{8,0},{9,15},{1... | collective-permute-start | bytes 417800 | tf_op jit(solution)/shard_map/ppermute | solution.py:416
  13.7 9.9 %collective-permute-start.12 = (bf16[544,128]{1,0:T(8,128)(2,1)}, bf16[544,128]{1,0:T(8,128)(2,1)S(1)}, u32[]{:S(2)}, u32[]{:S(2)}) collective-permute-start(bf16[544,128]{1,0:T(8,128)(2,1)} %get-tuple-element.54), channel_id=1, source_target_pairs={{0,6},{1,9},{2,4},{3,11},{4,2},{5,13},{6,0},{7,15},{8,14},{9,1},{1... | collective-permute-start | bytes 417800 | tf_op jit(solution)/shard_map/ppermute | solution.py:416
  17.8 7.1 %collective-permute-start.13 = (bf16[544,128]{1,0:T(8,128)(2,1)}, bf16[544,128]{1,0:T(8,128)(2,1)S(1)}, u32[]{:S(2)}, u32[]{:S(2)}) collective-permute-start(bf16[544,128]{1,0:T(8,128)(2,1)} %get-tuple-element.55), channel_id=1, source_target_pairs={{0,14},{1,15},{2,12},{3,13},{4,10},{5,11},{6,8},{7,9},{8,6},{9,7},... | collective-permute-start | bytes 417800 | tf_op jit(solution)/shard_map/ppermute | solution.py:416
  20.1 0.9 copy-start.2
  21.0 9.1 %copy-start.14 = (bf16[512,128]{1,0:T(8,128)(2,1)S(1)}, bf16[512,128]{1,0:T(8,128)(2,1)}, u32[]{:S(2)}) copy-start(bf16[512,128]{1,0:T(8,128)(2,1)} %get-tuple-element.41) | copy-start | bytes 393220
  21.0 9.1 %copy-start.13 = (bf16[512,128]{1,0:T(8,128)(2,1)S(1)}, bf16[512,128]{1,0:T(8,128)(2,1)}, u32[]{:S(2)}) copy-start(bf16[512,128]{1,0:T(8,128)(2,1)} %get-tuple-element.42) | copy-start | bytes 393220
  21.0 9.2 %copy-start.12 = (bf16[512,128]{1,0:T(8,128)(2,1)S(1)}, bf16[512,128]{1,0:T(8,128)(2,1)}, u32[]{:S(2)}) copy-start(bf16[512,128]{1,0:T(8,128)(2,1)} %get-tuple-element.43) | copy-start | bytes 393220
  21.0 10.0 %copy-start.11 = (bf16[512,128]{1,0:T(8,128)(2,1)S(1)}, bf16[512,128]{1,0:T(8,128)(2,1)}, u32[]{:S(2)}) copy-start(bf16[512,128]{1,0:T(8,128)(2,1)} %get-tuple-element.44) | copy-start | bytes 393220
  21.0 14.0 %copy-start.10 = (bf16[512,128]{1,0:T(8,128)(2,1)S(1)}, bf16[512,128]{1,0:T(8,128)(2,1)}, u32[]{:S(2)}) copy-start(bf16[512,128]{1,0:T(8,128)(2,1)} %get-tuple-element.45) | copy-start | bytes 393220
  21.0 22.1 %copy-start.9 = (bf16[512,128]{1,0:T(8,128)(2,1)S(1)}, bf16[512,128]{1,0:T(8,128)(2,1)}, u32[]{:S(2)}) copy-start(bf16[512,128]{1,0:T(8,128)(2,1)} %get-tuple-element.46) | copy-start | bytes 393220
  21.0 22.8 %copy-start.8 = (bf16[512,128]{1,0:T(8,128)(2,1)S(1)}, bf16[512,128]{1,0:T(8,128)(2,1)}, u32[]{:S(2)}) copy-start(bf16[512,128]{1,0:T(8,128)(2,1)} %get-tuple-element.47) | copy-start | bytes 393220
  21.1 27.4 %copy-start.3 = (bf16[2048,8]{0,1:T(8,128)(2,1)S(1)}, bf16[2048,8]{0,1:T(8,128)(2,1)}, u32[]{:S(2)}) copy-start(bf16[2048,8]{0,1:T(8,128)(2,1)} %param.26) | copy-start | bytes 98308
  21.1 27.3 %copy-start.5 = (bf16[8,2048]{1,0:T(8,128)(2,1)S(1)}, bf16[8,2048]{1,0:T(8,128)(2,1)}, u32[]{:S(2)}) copy-start(bf16[8,2048]{1,0:T(8,128)(2,1)} %refs_13_.1) | copy-start | bytes 98308
  21.1 27.3 %copy-start.6 = (bf16[8,2048]{1,0:T(8,128)(2,1)S(1)}, bf16[8,2048]{1,0:T(8,128)(2,1)}, u32[]{:S(2)}) copy-start(bf16[8,2048]{1,0:T(8,128)(2,1)} %refs_14_.1) | copy-start | bytes 98308
  21.1 27.3 %copy-start.7 = (bf16[8,2048]{1,0:T(8,128)(2,1)S(1)}, bf16[8,2048]{1,0:T(8,128)(2,1)}, u32[]{:S(2)}) copy-start(bf16[8,2048]{1,0:T(8,128)(2,1)} %refs_15_.1) | copy-start | bytes 98308
  24.9 27.7 %collective-permute-start.14 = (bf16[8,272,128]{2,1,0:T(8,128)(2,1)S(1)}, bf16[8,272,128]{2,1,0:T(8,128)(2,1)S(1)}, u32[]{:S(2)}, u32[]{:S(2)}) collective-permute-start(bf16[8,272,128]{2,1,0:T(8,128)(2,1)S(1)} %shard_map.199), channel_id=1, source_target_pairs={{0,24},{2,26},{4,28},{6,30},{8,16},{10,18},{12,20},{14,22},{16,8},... | collective-permute-start | bytes 1671176 | tf_op jit(solution)/shard_map/ppermute | solution.py:441
  30.1 5.0 %collective-permute-start = (bf16[512,128]{1,0:T(8,128)(2,1)S(1)}, bf16[512,128]{1,0:T(8,128)(2,1)S(1)}, u32[]{:S(2)}, u32[]{:S(2)}) collective-permute-start(bf16[512,128]{1,0:T(8,128)(2,1)S(1)} %copy-done.14), channel_id=1, source_target_pairs={{0,2},{1,13},{2,0},{3,15},{4,6},{5,9},{6,4},{7,11},{8,10},{9,5},{1... | collective-permute-start | bytes 393224 | tf_op jit(solution)/shard_map/ppermute | solution.py:416
  30.1 13.1 %collective-permute-start.1 = (bf16[512,128]{1,0:T(8,128)(2,1)S(1)}, bf16[512,128]{1,0:T(8,128)(2,1)S(1)}, u32[]{:S(2)}, u32[]{:S(2)}) collective-permute-start(bf16[512,128]{1,0:T(8,128)(2,1)S(1)} %copy-done.13), channel_id=1, source_target_pairs={{0,12},{1,3},{2,14},{3,1},{4,8},{5,7},{6,10},{7,5},{8,4},{9,11},{1... | collective-permute-start | bytes 393224 | tf_op jit(solution)/shard_map/ppermute | solution.py:416
  30.2 13.6 %collective-permute-start.2 = (bf16[512,128]{1,0:T(8,128)(2,1)S(1)}, bf16[512,128]{1,0:T(8,128)(2,1)S(1)}, u32[]{:S(2)}, u32[]{:S(2)}) collective-permute-start(bf16[512,128]{1,0:T(8,128)(2,1)S(1)} %copy-done.12), channel_id=1, source_target_pairs={{0,4},{1,11},{2,6},{3,9},{4,0},{5,15},{6,2},{7,13},{8,12},{9,3},{1... | collective-permute-start | bytes 393224 | tf_op jit(solution)/shard_map/ppermute | solution.py:416
  31.1 21.5 %collective-permute-start.3 = (bf16[512,128]{1,0:T(8,128)(2,1)S(1)}, bf16[512,128]{1,0:T(8,128)(2,1)S(1)}, u32[]{:S(2)}, u32[]{:S(2)}) collective-permute-start(bf16[512,128]{1,0:T(8,128)(2,1)S(1)} %copy-done.11), channel_id=1, source_target_pairs={{0,10},{1,5},{2,8},{3,7},{4,14},{5,1},{6,12},{7,3},{8,2},{9,13},{1... | collective-permute-start | bytes 393224 | tf_op jit(solution)/shard_map/ppermute | solution.py:416
  35.1 17.5 %collective-permute-start.4 = (bf16[512,128]{1,0:T(8,128)(2,1)S(1)}, bf16[512,128]{1,0:T(8,128)(2,1)S(1)}, u32[]{:S(2)}, u32[]{:S(2)}) collective-permute-start(bf16[512,128]{1,0:T(8,128)(2,1)S(1)} %copy-done.10), channel_id=1, source_target_pairs={{0,8},{1,7},{2,10},{3,5},{4,12},{5,3},{6,14},{7,1},{8,0},{9,15},{1... | collective-permute-start | bytes 393224 | tf_op jit(solution)/shard_map/ppermute | solution.py:416
  43.2 9.4 %collective-permute-start.5 = (bf16[512,128]{1,0:T(8,128)(2,1)S(1)}, bf16[512,128]{1,0:T(8,128)(2,1)S(1)}, u32[]{:S(2)}, u32[]{:S(2)}) collective-permute-start(bf16[512,128]{1,0:T(8,128)(2,1)S(1)} %copy-done.9), channel_id=1, source_target_pairs={{0,6},{1,9},{2,4},{3,11},{4,2},{5,13},{6,0},{7,15},{8,14},{9,1},{1... | collective-permute-start | bytes 393224 | tf_op jit(solution)/shard_map/ppermute | solution.py:416
  43.8 8.8 %copy-start.4 = (bf16[512,128]{1,0:T(8,128)(2,1)S(1)}, bf16[512,128]{1,0:T(8,128)(2,1)}, u32[]{:S(2)}) copy-start(bf16[512,128]{1,0:T(8,128)(2,1)} %get-tuple-element.40.refs_0_) | copy-start | bytes 393220
  43.8 8.8 %collective-permute-start.6 = (bf16[512,128]{1,0:T(8,128)(2,1)S(1)}, bf16[512,128]{1,0:T(8,128)(2,1)S(1)}, u32[]{:S(2)}, u32[]{:S(2)}) collective-permute-start(bf16[512,128]{1,0:T(8,128)(2,1)S(1)} %copy-done.8), channel_id=1, source_target_pairs={{0,14},{1,15},{2,12},{3,13},{4,10},{5,11},{6,8},{7,9},{8,6},{9,7},... | collective-permute-start | bytes 393224 | tf_op jit(solution)/shard_map/ppermute | solution.py:416
  52.6 19.4 %copy-start = (bf16[1,128,4096]{2,1,0:T(8,128)(2,1)S(1)}, bf16[1,128,4096]{2,1,0:T(8,128)(2,1)}, u32[]{:S(2)}) copy-start(bf16[1,128,4096]{2,1,0:T(8,128)(2,1)} %param.14) | copy-start | bytes 3145732
  52.6 19.4 %copy-start.1 = (bf16[1,128,4096]{2,1,0:T(8,128)(2,1)S(1)}, bf16[1,128,4096]{2,1,0:T(8,128)(2,1)}, u32[]{:S(2)}) copy-start(bf16[1,128,4096]{2,1,0:T(8,128)(2,1)} %param.15) | copy-start | bytes 3145732
  72.5 1.5 %collective-permute-start.15 = (bf16[16,48,128]{2,1,0:T(8,128)(2,1)S(1)}, bf16[16,48,128]{2,1,0:T(8,128)(2,1)S(1)}, u32[]{:S(2)}, u32[]{:S(2)}) collective-permute-start(bf16[16,48,128]{2,1,0:T(8,128)(2,1)S(1)} %get-tuple-element.63), channel_id=1, source_target_pairs={{0,1},{1,0},{2,3},{3,2},{4,5},{5,4},{6,7},{7,6},{8,9},{9,8},{10,11... | collective-permute-start | bytes 589832 | tf_op jit(solution)/shard_map/ppermute | solution.py:512
  97.1 1.4 %collective-permute-start.16 = (bf16[16,48,128]{2,1,0:T(8,128)(2,1)S(1)}, bf16[16,48,128]{2,1,0:T(8,128)(2,1)S(1)}, u32[]{:S(2)}, u32[]{:S(2)}) collective-permute-start(bf16[16,48,128]{2,1,0:T(8,128)(2,1)S(1)} %all_to_all.17.refs_0_), channel_id=1, source_target_pairs={{0,1},{1,0},{2,3},{3,2},{4,5},{5,4},{6,7},{7,6},{8,9},{9,8},{10,11... | collective-permute-start | bytes 589832 | tf_op jit(solution)/shard_map/ppermute | solution.py:530

commit v6 on v5

--- a/solution.py
+++ b/solution.py
@@ -22,6 +22,7 @@
 BF16 = jnp.bfloat16
 NT = (((1,), (1,)), ((), ()))
 ORDERS = ((0, 1, 6, 2, 5, 4, 3, 7), (0, 6, 1, 5, 2, 3, 4, 7))
+LATER = ((0, 1, 2, 3, 7, 4, 5, 6), (0, 2, 1, 3, 7, 4, 6, 5))
 BLOCK = 256
 VMEM_LIMIT = 24 * 1024 * 1024
 VMEM_PACK = 56 * 1024 * 1024
@@ -55,10 +56,10 @@
     return lax.rem(lax.div(index, HALF_HEADS), 2), lax.rem(index, HALF_HEADS)
 
 
-def partners():
+def partners(orders=ORDERS):
     _, slot = place()
     core = lax.rem(lax.axis_index("dp"), 2)
-    return [jnp.bitwise_xor(slot, jnp.where(core == 0, a, b)) for a, b in zip(*ORDERS)]
+    return [jnp.bitwise_xor(slot, jnp.where(core == 0, a, b)) for a, b in zip(*orders)]
 
 
 def rows_at(index):
@@ -134,8 +135,9 @@
 
 def spread(array, odd, peers, firsts, at, seconds, late):
     tok = array.shape[0]
-    for peer, first, second in zip(peers, firsts, seconds):
+    for peer, first in zip(peers, firsts):
         first[at:at + tok, :] = head_columns(array, peer + HALF_HEADS * odd)
+    for peer, second in zip(partners(LATER), seconds):
         second[late:late + tok, :] = head_columns(array, second_head(peer) + HALF_HEADS * (1 - odd))
 
 
@@ -256,7 +258,7 @@
     odd, slot = place()
     tok = HEAD_WIDTH
     length = token_low.shape[0]
-    for peer, part in zip(partners(), parts):
+    for peer, part in zip(partners(LATER), parts):
         at = rows_at(peer)
         late = rows_at(peer + HALF_HEADS)
         queries[at, :] = part[:tok, :]
@@ -409,10 +411,10 @@
 
     cores = lax.axis_size("dp")
 
-    def exchange(parts):
+    def exchange(parts, orders):
         moved = [parts[0]]
         for k in range(1, peers):
-            pairs = [(c * cores + d, (c ^ ORDERS[d % 2][k]) * cores + d) for c in range(count) for d in range(cores)]
+            pairs = [(c * cores + d, (c ^ orders[d % 2][k]) * cores + d) for c in range(count) for d in range(cores)]
             moved.append(lax.ppermute(parts[k], ("ctx", "dp"), pairs))
         return tuple(moved)
 
@@ -431,7 +433,7 @@
     )
     firsts, seconds = packed[:peers], packed[peers:]
     firsts = (call(keep_kernel, jax.ShapeDtypeStruct(firsts[0].shape, BF16), firsts[:1]),) + tuple(firsts[1:])
-    firsts = exchange(firsts)
+    firsts = exchange(firsts, ORDERS)
     cross = call(
         assemble_kernel,
         jax.ShapeDtypeStruct((peers, 2 * tok + 16, HEAD_WIDTH), BF16),
@@ -439,7 +441,7 @@
         moved=2 << 20,
     )
     cross = lax.ppermute(cross, "ctx", ahead)
-    seconds = exchange(seconds)
+    seconds = exchange(seconds, LATER)
     length = peers * tok
     ups = (query_up_weight, key_up_weight, value_up_weight, down_t)
 

time: 99.7 us -> 98.9 us (level)
  starting transfers between devices: 29.8 us -> 27 us
  waiting for transfers between devices: 14.8 us -> 16.5 us
    ppermute x14, starting transfers between devices: 24.5 us -> 21.9 us  [exchange(): moved.append(lax.ppermute(parts[k], ('ctx', 'dp'), pairs))]
    ppermute x14, waiting for transfers between devices: 11.9 us -> 13.7 us  [exchange(): moved.append(lax.ppermute(parts[k], ('ctx', 'dp'), pairs))]
  transfers between devices with their start and end apart: 17 -> 17, of which waited for: 5 -> 10; matrix products, arithmetic and copies ran while one was open for 0% -> 0% of each run, Pallas kernels for 4% -> 4%
where the time goes in v6:
time: 98.9 us; the launch traced here: 98.6 us
  blocking collectives  35.4 us (36%)
  starting transfers between devices  27 us (27%)
  Pallas kernels  17.9 us (18%)
  waiting for transfers between devices  16.5 us (17%)
    ppermute x14, starting transfers between devices, exchange(): moved.append(lax.ppermute(parts[k], ('ctx', 'dp'), pairs))  21.9 us
    pallas_call x9, Pallas kernels, call(): pl.pallas_call(kernel, out_shape=out_shape, in_specs=[pl.BlockSpec(memory...  17.9 us
    ppermute x14, waiting for transfers between devices, exchange(): moved.append(lax.ppermute(parts[k], ('ctx', 'dp'), pairs))  13.7 us
    all_to_all x1, blocking collectives, per_device(): terms = lax.all_to_all(terms, 'ctx', 0, 0)  12.3 us
    all_to_all x1, blocking collectives, per_device(): parts = lax.all_to_all(parts, 'ctx', 0, 0)  11.8 us
    all_to_all x1, blocking collectives, per_device(): mine = lax.all_to_all(shared, 'ctx', 0, 0)  11.3 us
    ppermute x1, starting transfers between devices, per_device(): cross = lax.ppermute(cross, 'ctx', ahead)  5.02 us
  transfers between devices with their start and end apart: 17, of which 10 were waited for; matrix products, arithmetic and copies ran while one was open for 0% of the time, Pallas kernels for 4%

profile of v6, /device:TPU:0, one launch (start us, length us, event | category | flops | bytes accessed | tf_op | source)
XLA Modules:
  0.0 98.6 jit_solution(579819315812879885)
XLA Ops:
  0.6 5.0 %shard_map.197 = (bf16[544,128]{1,0:T(8,128)(2,1)}, bf16[544,128]{1,0:T(8,128)(2,1)}, bf16[544,128]{1,0:T(8,128)(2,1)}, bf16[544,128]{1,0:T(8,128)(2,1)}, bf16[5...) custom-call(bf16[128,2048]{1,0:T(8,128)(2,1)} %bitcast.21, ...), custom_call_target="tpu_custom_call" | custom-call | flops 268435456 | bytes 4194304 | tf_op jit(solution)/shard_map/pallas_call | solution.py:40
  5.7 3.0 %collective-permute-start.7 = (bf16[544,128]{1,0:T(8,128)(2,1)}, bf16[544,128]{1,0:T(8,128)(2,1)S(1)}, u32[]{:S(2)}, u32[]{:S(2)}) collective-permute-start(bf16[544,128]{1,0:T(8,128)(2,1)} %get-tuple-element.49), channel_id=1, source_target_pairs={{0,2},{1,13},{2,0},{3,15},{4,6},{5,9},{6,4},{7,11},{8,10},{9,5},{1... | collective-permute-start | bytes 417800 | tf_op jit(solution)/shard_map/ppermute | solution.py:418
  8.7 2.5 %collective-permute-start.8 = (bf16[544,128]{1,0:T(8,128)(2,1)}, bf16[544,128]{1,0:T(8,128)(2,1)S(1)}, u32[]{:S(2)}, u32[]{:S(2)}) collective-permute-start(bf16[544,128]{1,0:T(8,128)(2,1)} %get-tuple-element.50), channel_id=1, source_target_pairs={{0,12},{1,3},{2,14},{3,1},{4,8},{5,7},{6,10},{7,5},{8,4},{9,11},{1... | collective-permute-start | bytes 417800 | tf_op jit(solution)/shard_map/ppermute | solution.py:418
  11.2 0.5 collective-permute-start.9
  11.7 0.0 collective-permute-start.10
  11.8 2.0 %collective-permute-start.11 = (bf16[544,128]{1,0:T(8,128)(2,1)}, bf16[544,128]{1,0:T(8,128)(2,1)S(1)}, u32[]{:S(2)}, u32[]{:S(2)}) collective-permute-start(bf16[544,128]{1,0:T(8,128)(2,1)} %get-tuple-element.53), channel_id=1, source_target_pairs={{0,8},{1,7},{2,10},{3,5},{4,12},{5,3},{6,14},{7,1},{8,0},{9,15},{1... | collective-permute-start | bytes 417800 | tf_op jit(solution)/shard_map/ppermute | solution.py:418
  13.7 0.0 collective-permute-done.7.refs_1_
  13.7 4.0 %collective-permute-start.12 = (bf16[544,128]{1,0:T(8,128)(2,1)}, bf16[544,128]{1,0:T(8,128)(2,1)S(1)}, u32[]{:S(2)}, u32[]{:S(2)}) collective-permute-start(bf16[544,128]{1,0:T(8,128)(2,1)} %get-tuple-element.54), channel_id=1, source_target_pairs={{0,6},{1,9},{2,4},{3,11},{4,2},{5,13},{6,0},{7,15},{8,14},{9,1},{1... | collective-permute-start | bytes 417800 | tf_op jit(solution)/shard_map/ppermute | solution.py:418
  17.8 0.0 collective-permute-done.8.refs_2_
  17.8 2.3 %collective-permute-start.13 = (bf16[544,128]{1,0:T(8,128)(2,1)}, bf16[544,128]{1,0:T(8,128)(2,1)S(1)}, u32[]{:S(2)}, u32[]{:S(2)}) collective-permute-start(bf16[544,128]{1,0:T(8,128)(2,1)} %get-tuple-element.55), channel_id=1, source_target_pairs={{0,14},{1,15},{2,12},{3,13},{4,10},{5,11},{6,8},{7,9},{8,6},{9,7},... | collective-permute-start | bytes 417800 | tf_op jit(solution)/shard_map/ppermute | solution.py:418
  20.1 0.9 copy-done.2
  21.0 0.0 copy-start.14
  21.0 0.0 copy-start.13
  21.0 0.0 copy-start.12
  21.0 0.0 copy-start.11
  21.0 0.0 copy-start.10
  21.0 0.0 copy-start.9
  21.0 0.0 copy-start.8
  21.1 0.0 copy-start.3
  21.1 0.0 copy-start.5
  21.1 0.0 copy-start.6
  21.1 0.0 copy-start.7
  21.1 0.0 collective-permute-done.9.refs_3_
  21.1 0.0 collective-permute-done.10.refs_4_
  21.1 0.0 collective-permute-done.11.refs_5_
  21.1 2.5 %collective-permute-done.12.refs_6_ = bf16[544,128]{1,0:T(8,128)(2,1)S(1)} collective-permute-done((bf16[544,128]{1,0:T(8,128)(2,1)}, bf16[544,128]{1,0:T(8,128)(2,1)S(1)}, u32[]{:S(2)}, u32[]{:S(2)}) %collective-permute-start.12) | collective-permute-done | bytes 139296 | tf_op jit(solution)/shard_map/ppermute | solution.py:418
  23.7 1.2 %collective-permute-done.13.refs_7_ = bf16[544,128]{1,0:T(8,128)(2,1)S(1)} collective-permute-done((bf16[544,128]{1,0:T(8,128)(2,1)}, bf16[544,128]{1,0:T(8,128)(2,1)S(1)}, u32[]{:S(2)}, u32[]{:S(2)}) %collective-permute-start.13) | collective-permute-done | bytes 139296 | tf_op jit(solution)/shard_map/ppermute | solution.py:418
  24.9 0.1 shard_map.199
  24.9 5.0 %collective-permute-start.14 = (bf16[8,272,128]{2,1,0:T(8,128)(2,1)S(1)}, bf16[8,272,128]{2,1,0:T(8,128)(2,1)S(1)}, u32[]{:S(2)}, u32[]{:S(2)}) collective-permute-start(bf16[8,272,128]{2,1,0:T(8,128)(2,1)S(1)} %shard_map.199), channel_id=1, source_target_pairs={{0,24},{2,26},{4,28},{6,30},{8,16},{10,18},{12,20},{14,22},{16,8},... | collective-permute-start | bytes 1671176 | tf_op jit(solution)/shard_map/ppermute | solution.py:443
  29.9 0.0 copy-done.14
  29.9 0.0 collective-permute-start
  29.9 0.0 copy-done.13
  29.9 1.1 %collective-permute-start.1 = (bf16[512,128]{1,0:T(8,128)(2,1)S(1)}, bf16[512,128]{1,0:T(8,128)(2,1)S(1)}, u32[]{:S(2)}, u32[]{:S(2)}) collective-permute-start(bf16[512,128]{1,0:T(8,128)(2,1)S(1)} %copy-done.13), channel_id=1, source_target_pairs={{0,4},{1,3},{2,6},{3,1},{4,0},{5,7},{6,2},{7,5},{8,12},{9,11},{10,... | collective-permute-start | bytes 393224 | tf_op jit(solution)/shard_map/ppermute | solution.py:418
  31.0 0.0 copy-done.12
  31.0 2.4 %collective-permute-start.2 = (bf16[512,128]{1,0:T(8,128)(2,1)S(1)}, bf16[512,128]{1,0:T(8,128)(2,1)S(1)}, u32[]{:S(2)}, u32[]{:S(2)}) collective-permute-start(bf16[512,128]{1,0:T(8,128)(2,1)S(1)} %copy-done.12), channel_id=1, source_target_pairs={{0,6},{1,7},{2,4},{3,5},{4,2},{5,3},{6,0},{7,1},{8,14},{9,15},{10,... | collective-permute-start | bytes 393224 | tf_op jit(solution)/shard_map/ppermute | solution.py:418
  33.4 0.0 collective-permute-start.3
  33.4 1.5 %collective-permute-done.refs_1_ = bf16[512,128]{1,0:T(8,128)(2,1)S(1)} collective-permute-done((bf16[512,128]{1,0:T(8,128)(2,1)S(1)}, bf16[512,128]{1,0:T(8,128)(2,1)S(1)}, u32[]{:S(2)}, u32[]{:S(2)}) %collective-permute-start) | collective-permute-done | bytes 131104 | tf_op jit(solution)/shard_map/ppermute | solution.py:418
  34.9 0.5 collective-permute-start.4
  35.4 0.0 collective-permute-done.1.refs_2_
  35.4 0.0 copy-done.9
  35.4 1.0 %collective-permute-start.5 = (bf16[512,128]{1,0:T(8,128)(2,1)S(1)}, bf16[512,128]{1,0:T(8,128)(2,1)S(1)}, u32[]{:S(2)}, u32[]{:S(2)}) collective-permute-start(bf16[512,128]{1,0:T(8,128)(2,1)S(1)} %copy-done.9), channel_id=1, source_target_pairs={{0,10},{1,13},{2,8},{3,15},{4,14},{5,9},{6,12},{7,11},{8,2},{9,5},... | collective-permute-start | bytes 393224 | tf_op jit(solution)/shard_map/ppermute | solution.py:418
  36.4 0.4 collective-permute-done.2.refs_3_
  36.9 0.0 copy-done.8
  36.9 2.5 %collective-permute-start.6 = (bf16[512,128]{1,0:T(8,128)(2,1)S(1)}, bf16[512,128]{1,0:T(8,128)(2,1)S(1)}, u32[]{:S(2)}, u32[]{:S(2)}) collective-permute-start(bf16[512,128]{1,0:T(8,128)(2,1)S(1)} %copy-done.8), channel_id=1, source_target_pairs={{0,12},{1,11},{2,14},{3,9},{4,8},{5,15},{6,10},{7,13},{8,4},{9,3},... | collective-permute-start | bytes 393224 | tf_op jit(solution)/shard_map/ppermute | solution.py:418
  39.4 0.0 copy-done.7
  39.4 4.1 %shard_map.200 = (f32[8,32,128]{2,1,0:T(8,128)S(1)}, f32[32,128]{1,0:T(8,128)S(1)}, bf16[8,32,128]{2,1,0:T(8,128)(2,1)S(1)}, bf16[1024,128]{1,0:T(8,128)(2,1)S(1)}) custom-call(bf16[544,128]{1,0:T(8,128)(2,1)S(1)} %shard_map.198.refs_0_, bf16[544,128]{1,0:T(8,128)(2,1)S(1)} %collective-permute-done.7.refs_1_, ...), custom_call_target="tpu_custom_call" | custom-call | flops 1610612736 | bytes 3145728 | tf_op jit(solution)/shard_map/pallas_call | solution.py:40
  43.5 1.5 %collective-permute-done.3.refs_4_ = bf16[512,128]{1,0:T(8,128)(2,1)S(1)} collective-permute-done((bf16[512,128]{1,0:T(8,128)(2,1)S(1)}, bf16[512,128]{1,0:T(8,128)(2,1)S(1)}, u32[]{:S(2)}, u32[]{:S(2)}) %collective-permute-start.3) | collective-permute-done | bytes 131104 | tf_op jit(solution)/shard_map/ppermute | solution.py:418
  45.0 1.4 %collective-permute-done.4.refs_5_ = bf16[512,128]{1,0:T(8,128)(2,1)S(1)} collective-permute-done((bf16[512,128]{1,0:T(8,128)(2,1)S(1)}, bf16[512,128]{1,0:T(8,128)(2,1)S(1)}, u32[]{:S(2)}, u32[]{:S(2)}) %collective-permute-start.4) | collective-permute-done | bytes 131104 | tf_op jit(solution)/shard_map/ppermute | solution.py:418
  46.4 2.2 %collective-permute-done.5.refs_6_ = bf16[512,128]{1,0:T(8,128)(2,1)S(1)} collective-permute-done((bf16[512,128]{1,0:T(8,128)(2,1)S(1)}, bf16[512,128]{1,0:T(8,128)(2,1)S(1)}, u32[]{:S(2)}, u32[]{:S(2)}) %collective-permute-start.5) | collective-permute-done | bytes 131104 | tf_op jit(solution)/shard_map/ppermute | solution.py:418
  48.6 2.9 %collective-permute-done.6.refs_7_ = bf16[512,128]{1,0:T(8,128)(2,1)S(1)} collective-permute-done((bf16[512,128]{1,0:T(8,128)(2,1)S(1)}, bf16[512,128]{1,0:T(8,128)(2,1)S(1)}, u32[]{:S(2)}, u32[]{:S(2)}) %collective-permute-start.6) | collective-permute-done | bytes 131104 | tf_op jit(solution)/shard_map/ppermute | solution.py:418
  51.5 0.0 collective-permute-done.14.refs_8_
  51.5 0.0 copy-done.4
  51.5 0.0 copy-start.1
  51.5 7.4 %shard_map.201 = (bf16[16,32,128]{2,1,0:T(8,128)(2,1)S(1)}, f32[64,128]{1,0:T(8,128)S(1)}) custom-call(bf16[512,128]{1,0:T(8,128)(2,1)S(1)} %copy-done.4, bf16[512,128]{1,0:T(8,128)(2,1)S(1)} %collective-permute-done.refs_1_, bf16[512,128]{1,0:T(8,128)(2,1)S(1)} %collective-permute-done.1.refs_2_, bf16[512,128]{1,0:T(8,128)(2,1)S(1)} %collective-permute-done.2.refs_3_, ...), custom_call_target="tpu_custom_call" | custom-call | flops 4831838208 | bytes 3145728 | tf_op jit(solution)/shard_map/pallas_call | solution.py:40
  58.9 12.3 %all_to_all.15.terms = bf16[16,32,128]{2,1,0:T(8,128)(2,1)S(1)} all-to-all(bf16[16,32,128]{2,1,0:T(8,128)(2,1)S(1)} %get-tuple-element.60), channel_id=1, replica_groups=mesh['ctx'=16,'dp'=2] {'ctx'}, dimensions={0} | all-to-all | bytes 262144 | tf_op jit(solution)/shard_map/all_to_all | solution.py:486
  71.2 0.0 copy-done.1
  71.2 0.4 shard_map.202
  71.6 0.1 collective-permute-start.15
  71.7 1.4 %collective-permute-done.15.b = bf16[16,48,128]{2,1,0:T(8,128)(2,1)S(1)} collective-permute-done((bf16[16,48,128]{2,1,0:T(8,128)(2,1)S(1)}, bf16[16,48,128]{2,1,0:T(8,128)(2,1)S(1)}, u32[]{:S(2)}, u32[]{:S(2)}) %collective-permute-start.15) | collective-permute-done | bytes 196640 | tf_op jit(solution)/shard_map/ppermute | solution.py:514
  73.1 11.8 %all_to_all.16.parts = bf16[16,48,128]{2,1,0:T(8,128)(2,1)S(1)} all-to-all(bf16[16,48,128]{2,1,0:T(8,128)(2,1)S(1)} %shard_map.203), channel_id=1, replica_groups=mesh['ctx'=16,'dp'=2] {'ctx'}, dimensions={0} | all-to-all | bytes 393216 | tf_op jit(solution)/shard_map/all_to_all | solution.py:516
  85.0 11.3 %all_to_all.17.refs_0_ = bf16[16,48,128]{2,1,0:T(8,128)(2,1)S(1)} all-to-all(bf16[16,48,128]{2,1,0:T(8,128)(2,1)S(1)} %shard_map.204), channel_id=1, replica_groups=mesh['ctx'=16,'dp'=2] {'ctx'}, dimensions={0} | all-to-all | bytes 393216 | tf_op jit(solution)/shard_map/all_to_all | solution.py:531
  96.3 0.0 collective-permute-start.16
  96.3 1.4 %collective-permute-done.16.refs_1_ = bf16[16,48,128]{2,1,0:T(8,128)(2,1)S(1)} collective-permute-done((bf16[16,48,128]{2,1,0:T(8,128)(2,1)S(1)}, bf16[16,48,128]{2,1,0:T(8,128)(2,1)S(1)}, u32[]{:S(2)}, u32[]{:S(2)}) %collective-permute-start.16) | collective-permute-done | bytes 196640 | tf_op jit(solution)/shard_map/ppermute | solution.py:532
  97.7 0.9 shard_map.205
  (12 shorter events, 0.1 us)
Async XLA Ops:
  5.7 8.1 %collective-permute-start.7 = (bf16[544,128]{1,0:T(8,128)(2,1)}, bf16[544,128]{1,0:T(8,128)(2,1)S(1)}, u32[]{:S(2)}, u32[]{:S(2)}) collective-permute-start(bf16[544,128]{1,0:T(8,128)(2,1)} %get-tuple-element.49), channel_id=1, source_target_pairs={{0,2},{1,13},{2,0},{3,15},{4,6},{5,9},{6,4},{7,11},{8,10},{9,5},{1... | collective-permute-start | bytes 417800 | tf_op jit(solution)/shard_map/ppermute | solution.py:418
  8.7 9.1 %collective-permute-start.8 = (bf16[544,128]{1,0:T(8,128)(2,1)}, bf16[544,128]{1,0:T(8,128)(2,1)S(1)}, u32[]{:S(2)}, u32[]{:S(2)}) collective-permute-start(bf16[544,128]{1,0:T(8,128)(2,1)} %get-tuple-element.50), channel_id=1, source_target_pairs={{0,12},{1,3},{2,14},{3,1},{4,8},{5,7},{6,10},{7,5},{8,4},{9,11},{1... | collective-permute-start | bytes 417800 | tf_op jit(solution)/shard_map/ppermute | solution.py:418
  11.2 9.9 %collective-permute-start.9 = (bf16[544,128]{1,0:T(8,128)(2,1)}, bf16[544,128]{1,0:T(8,128)(2,1)S(1)}, u32[]{:S(2)}, u32[]{:S(2)}) collective-permute-start(bf16[544,128]{1,0:T(8,128)(2,1)} %get-tuple-element.51), channel_id=1, source_target_pairs={{0,4},{1,11},{2,6},{3,9},{4,0},{5,15},{6,2},{7,13},{8,12},{9,3},{1... | collective-permute-start | bytes 417800 | tf_op jit(solution)/shard_map/ppermute | solution.py:418
  11.7 9.4 %collective-permute-start.10 = (bf16[544,128]{1,0:T(8,128)(2,1)}, bf16[544,128]{1,0:T(8,128)(2,1)S(1)}, u32[]{:S(2)}, u32[]{:S(2)}) collective-permute-start(bf16[544,128]{1,0:T(8,128)(2,1)} %get-tuple-element.52), channel_id=1, source_target_pairs={{0,10},{1,5},{2,8},{3,7},{4,14},{5,1},{6,12},{7,3},{8,2},{9,13},{1... | collective-permute-start | bytes 417800 | tf_op jit(solution)/shard_map/ppermute | solution.py:418
  11.8 9.4 %collective-permute-start.11 = (bf16[544,128]{1,0:T(8,128)(2,1)}, bf16[544,128]{1,0:T(8,128)(2,1)S(1)}, u32[]{:S(2)}, u32[]{:S(2)}) collective-permute-start(bf16[544,128]{1,0:T(8,128)(2,1)} %get-tuple-element.53), channel_id=1, source_target_pairs={{0,8},{1,7},{2,10},{3,5},{4,12},{5,3},{6,14},{7,1},{8,0},{9,15},{1... | collective-permute-start | bytes 417800 | tf_op jit(solution)/shard_map/ppermute | solution.py:418
  13.7 9.9 %collective-permute-start.12 = (bf16[544,128]{1,0:T(8,128)(2,1)}, bf16[544,128]{1,0:T(8,128)(2,1)S(1)}, u32[]{:S(2)}, u32[]{:S(2)}) collective-permute-start(bf16[544,128]{1,0:T(8,128)(2,1)} %get-tuple-element.54), channel_id=1, source_target_pairs={{0,6},{1,9},{2,4},{3,11},{4,2},{5,13},{6,0},{7,15},{8,14},{9,1},{1... | collective-permute-start | bytes 417800 | tf_op jit(solution)/shard_map/ppermute | solution.py:418
  17.8 7.1 %collective-permute-start.13 = (bf16[544,128]{1,0:T(8,128)(2,1)}, bf16[544,128]{1,0:T(8,128)(2,1)S(1)}, u32[]{:S(2)}, u32[]{:S(2)}) collective-permute-start(bf16[544,128]{1,0:T(8,128)(2,1)} %get-tuple-element.55), channel_id=1, source_target_pairs={{0,14},{1,15},{2,12},{3,13},{4,10},{5,11},{6,8},{7,9},{8,6},{9,7},... | collective-permute-start | bytes 417800 | tf_op jit(solution)/shard_map/ppermute | solution.py:418
  20.1 0.9 copy-start.2
  21.0 9.0 %copy-start.14 = (bf16[512,128]{1,0:T(8,128)(2,1)S(1)}, bf16[512,128]{1,0:T(8,128)(2,1)}, u32[]{:S(2)}) copy-start(bf16[512,128]{1,0:T(8,128)(2,1)} %get-tuple-element.41) | copy-start | bytes 393220
  21.0 8.9 %copy-start.13 = (bf16[512,128]{1,0:T(8,128)(2,1)S(1)}, bf16[512,128]{1,0:T(8,128)(2,1)}, u32[]{:S(2)}) copy-start(bf16[512,128]{1,0:T(8,128)(2,1)} %get-tuple-element.42) | copy-start | bytes 393220
  21.0 10.0 %copy-start.12 = (bf16[512,128]{1,0:T(8,128)(2,1)S(1)}, bf16[512,128]{1,0:T(8,128)(2,1)}, u32[]{:S(2)}) copy-start(bf16[512,128]{1,0:T(8,128)(2,1)} %get-tuple-element.43) | copy-start | bytes 393220
  21.0 12.4 %copy-start.11 = (bf16[512,128]{1,0:T(8,128)(2,1)S(1)}, bf16[512,128]{1,0:T(8,128)(2,1)}, u32[]{:S(2)}) copy-start(bf16[512,128]{1,0:T(8,128)(2,1)} %get-tuple-element.44) | copy-start | bytes 393220
  21.0 13.9 %copy-start.10 = (bf16[512,128]{1,0:T(8,128)(2,1)S(1)}, bf16[512,128]{1,0:T(8,128)(2,1)}, u32[]{:S(2)}) copy-start(bf16[512,128]{1,0:T(8,128)(2,1)} %get-tuple-element.45) | copy-start | bytes 393220
  21.0 14.4 %copy-start.9 = (bf16[512,128]{1,0:T(8,128)(2,1)S(1)}, bf16[512,128]{1,0:T(8,128)(2,1)}, u32[]{:S(2)}) copy-start(bf16[512,128]{1,0:T(8,128)(2,1)} %get-tuple-element.46) | copy-start | bytes 393220
  21.0 15.8 %copy-start.8 = (bf16[512,128]{1,0:T(8,128)(2,1)S(1)}, bf16[512,128]{1,0:T(8,128)(2,1)}, u32[]{:S(2)}) copy-start(bf16[512,128]{1,0:T(8,128)(2,1)} %get-tuple-element.47) | copy-start | bytes 393220
  21.1 18.3 %copy-start.3 = (bf16[2048,8]{0,1:T(8,128)(2,1)S(1)}, bf16[2048,8]{0,1:T(8,128)(2,1)}, u32[]{:S(2)}) copy-start(bf16[2048,8]{0,1:T(8,128)(2,1)} %param.26) | copy-start | bytes 98308
  21.1 18.3 %copy-start.5 = (bf16[8,2048]{1,0:T(8,128)(2,1)S(1)}, bf16[8,2048]{1,0:T(8,128)(2,1)}, u32[]{:S(2)}) copy-start(bf16[8,2048]{1,0:T(8,128)(2,1)} %refs_13_.1) | copy-start | bytes 98308
  21.1 18.3 %copy-start.6 = (bf16[8,2048]{1,0:T(8,128)(2,1)S(1)}, bf16[8,2048]{1,0:T(8,128)(2,1)}, u32[]{:S(2)}) copy-start(bf16[8,2048]{1,0:T(8,128)(2,1)} %refs_14_.1) | copy-start | bytes 98308
  21.1 18.3 %copy-start.7 = (bf16[8,2048]{1,0:T(8,128)(2,1)S(1)}, bf16[8,2048]{1,0:T(8,128)(2,1)}, u32[]{:S(2)}) copy-start(bf16[8,2048]{1,0:T(8,128)(2,1)} %refs_15_.1) | copy-start | bytes 98308
  24.9 26.6 %collective-permute-start.14 = (bf16[8,272,128]{2,1,0:T(8,128)(2,1)S(1)}, bf16[8,272,128]{2,1,0:T(8,128)(2,1)S(1)}, u32[]{:S(2)}, u32[]{:S(2)}) collective-permute-start(bf16[8,272,128]{2,1,0:T(8,128)(2,1)S(1)} %shard_map.199), channel_id=1, source_target_pairs={{0,24},{2,26},{4,28},{6,30},{8,16},{10,18},{12,20},{14,22},{16,8},... | collective-permute-start | bytes 1671176 | tf_op jit(solution)/shard_map/ppermute | solution.py:443
  29.9 5.0 %collective-permute-start = (bf16[512,128]{1,0:T(8,128)(2,1)S(1)}, bf16[512,128]{1,0:T(8,128)(2,1)S(1)}, u32[]{:S(2)}, u32[]{:S(2)}) collective-permute-start(bf16[512,128]{1,0:T(8,128)(2,1)S(1)} %copy-done.14), channel_id=1, source_target_pairs={{0,2},{1,5},{2,0},{3,7},{4,6},{5,1},{6,4},{7,3},{8,10},{9,13},{10,... | collective-permute-start | bytes 393224 | tf_op jit(solution)/shard_map/ppermute | solution.py:418
  29.9 5.5 %collective-permute-start.1 = (bf16[512,128]{1,0:T(8,128)(2,1)S(1)}, bf16[512,128]{1,0:T(8,128)(2,1)S(1)}, u32[]{:S(2)}, u32[]{:S(2)}) collective-permute-start(bf16[512,128]{1,0:T(8,128)(2,1)S(1)} %copy-done.13), channel_id=1, source_target_pairs={{0,4},{1,3},{2,6},{3,1},{4,0},{5,7},{6,2},{7,5},{8,12},{9,11},{10,... | collective-permute-start | bytes 393224 | tf_op jit(solution)/shard_map/ppermute | solution.py:418
  31.0 5.9 %collective-permute-start.2 = (bf16[512,128]{1,0:T(8,128)(2,1)S(1)}, bf16[512,128]{1,0:T(8,128)(2,1)S(1)}, u32[]{:S(2)}, u32[]{:S(2)}) collective-permute-start(bf16[512,128]{1,0:T(8,128)(2,1)S(1)} %copy-done.12), channel_id=1, source_target_pairs={{0,6},{1,7},{2,4},{3,5},{4,2},{5,3},{6,0},{7,1},{8,14},{9,15},{10,... | collective-permute-start | bytes 393224 | tf_op jit(solution)/shard_map/ppermute | solution.py:418
  33.4 11.6 %collective-permute-start.3 = (bf16[512,128]{1,0:T(8,128)(2,1)S(1)}, bf16[512,128]{1,0:T(8,128)(2,1)S(1)}, u32[]{:S(2)}, u32[]{:S(2)}) collective-permute-start(bf16[512,128]{1,0:T(8,128)(2,1)S(1)} %copy-done.11), channel_id=1, source_target_pairs={{0,14},{1,15},{2,12},{3,13},{4,10},{5,11},{6,8},{7,9},{8,6},{9,7},... | collective-permute-start | bytes 393224 | tf_op jit(solution)/shard_map/ppermute | solution.py:418
  34.9 11.5 %collective-permute-start.4 = (bf16[512,128]{1,0:T(8,128)(2,1)S(1)}, bf16[512,128]{1,0:T(8,128)(2,1)S(1)}, u32[]{:S(2)}, u32[]{:S(2)}) collective-permute-start(bf16[512,128]{1,0:T(8,128)(2,1)S(1)} %copy-done.10), channel_id=1, source_target_pairs={{0,8},{1,9},{2,10},{3,11},{4,12},{5,13},{6,14},{7,15},{8,0},{9,1},... | collective-permute-start | bytes 393224 | tf_op jit(solution)/shard_map/ppermute | solution.py:418
  35.4 13.2 %collective-permute-start.5 = (bf16[512,128]{1,0:T(8,128)(2,1)S(1)}, bf16[512,128]{1,0:T(8,128)(2,1)S(1)}, u32[]{:S(2)}, u32[]{:S(2)}) collective-permute-start(bf16[512,128]{1,0:T(8,128)(2,1)S(1)} %copy-done.9), channel_id=1, source_target_pairs={{0,10},{1,13},{2,8},{3,15},{4,14},{5,9},{6,12},{7,11},{8,2},{9,5},... | collective-permute-start | bytes 393224 | tf_op jit(solution)/shard_map/ppermute | solution.py:418
  36.9 14.6 %copy-start.4 = (bf16[512,128]{1,0:T(8,128)(2,1)S(1)}, bf16[512,128]{1,0:T(8,128)(2,1)}, u32[]{:S(2)}) copy-start(bf16[512,128]{1,0:T(8,128)(2,1)} %get-tuple-element.40.refs_0_) | copy-start | bytes 393220
  36.9 14.6 %collective-permute-start.6 = (bf16[512,128]{1,0:T(8,128)(2,1)S(1)}, bf16[512,128]{1,0:T(8,128)(2,1)S(1)}, u32[]{:S(2)}, u32[]{:S(2)}) collective-permute-start(bf16[512,128]{1,0:T(8,128)(2,1)S(1)} %copy-done.8), channel_id=1, source_target_pairs={{0,12},{1,11},{2,14},{3,9},{4,8},{5,15},{6,10},{7,13},{8,4},{9,3},... | collective-permute-start | bytes 393224 | tf_op jit(solution)/shard_map/ppermute | solution.py:418
  51.5 19.7 %copy-start = (bf16[1,128,4096]{2,1,0:T(8,128)(2,1)S(1)}, bf16[1,128,4096]{2,1,0:T(8,128)(2,1)}, u32[]{:S(2)}) copy-start(bf16[1,128,4096]{2,1,0:T(8,128)(2,1)} %param.14) | copy-start | bytes 3145732
  51.5 19.7 %copy-start.1 = (bf16[1,128,4096]{2,1,0:T(8,128)(2,1)S(1)}, bf16[1,128,4096]{2,1,0:T(8,128)(2,1)}, u32[]{:S(2)}) copy-start(bf16[1,128,4096]{2,1,0:T(8,128)(2,1)} %param.15) | copy-start | bytes 3145732
  71.6 1.5 %collective-permute-start.15 = (bf16[16,48,128]{2,1,0:T(8,128)(2,1)S(1)}, bf16[16,48,128]{2,1,0:T(8,128)(2,1)S(1)}, u32[]{:S(2)}, u32[]{:S(2)}) collective-permute-start(bf16[16,48,128]{2,1,0:T(8,128)(2,1)S(1)} %get-tuple-element.63), channel_id=1, source_target_pairs={{0,1},{1,0},{2,3},{3,2},{4,5},{5,4},{6,7},{7,6},{8,9},{9,8},{10,11... | collective-permute-start | bytes 589832 | tf_op jit(solution)/shard_map/ppermute | solution.py:514
  96.3 1.4 %collective-permute-start.16 = (bf16[16,48,128]{2,1,0:T(8,128)(2,1)S(1)}, bf16[16,48,128]{2,1,0:T(8,128)(2,1)S(1)}, u32[]{:S(2)}, u32[]{:S(2)}) collective-permute-start(bf16[16,48,128]{2,1,0:T(8,128)(2,1)S(1)} %all_to_all.17.refs_0_), channel_id=1, source_target_pairs={{0,1},{1,0},{2,3},{3,2},{4,5},{5,4},{6,7},{7,6},{8,9},{9,8},{10,11... | collective-permute-start | bytes 589832 | tf_op jit(solution)/shard_map/ppermute | solution.py:532
